TPU v7x, 32 devices: a whole 2x2x4 slice. The times are simulated.
32 devices in a mesh: ctx: 16 (over z, y, core), ch: 2 (over x).
Axes of the slice: x: 2, y: 2, z: 4, core: 2. Of those that a mesh axis runs over, the one named last changes fastest.
Arguments:
- query_proj: bfloat16 [2048, 4096], P('ctx', 'ch'), may hold values from -6 to 6
- key_proj: bfloat16 [2048, 4096], P('ctx', 'ch'), may hold values from -6 to 6
- value_proj: bfloat16 [2048, 4096], P('ctx', 'ch'), may hold values from -6 to 6
- output_grad: bfloat16 [2048, 4096], P('ctx', 'ch'), may hold values from -6 to 6
- residue: float32 [4096, 16], P(('ch', 'ctx')), may hold values from -5 to 5
- decay_rate: float32 [4096, 16], P(('ch', 'ctx')), may hold values from 4.8828126e-05 to 0.0625
Outputs:
- query_grad: bfloat16 [2048, 4096], P('ctx', 'ch')
- key_grad: bfloat16 [2048, 4096], P('ctx', 'ch')
- value_grad: bfloat16 [2048, 4096], P('ctx', 'ch')
- residue_grad: float32 [4096, 16], P(('ch', 'ctx'))
- log_rate_grad: float32 [4096, 16], P(('ch', 'ctx'))
All inputs are finite; a program needn't handle non-finite values.
Results may differ from a plain program's by a relative error of at most 0.0085.
Values may be sent and summed in bfloat16 or wider, within the bound.
No kernel may reach another device: no remote copies, remote signals or barrier semaphores. Data moves between devices by JAX's collectives and lax.ppermute only.
A program may use at most 64 MiB of HBM per device.

v0:
```python
import math

import jax
import jax.numpy as jnp
from jax import lax
from jax.sharding import PartitionSpec as P

HIGHEST = lax.Precision.HIGHEST


def filter_bank(residue, decay_rate, tokens):
    positions = jnp.arange(tokens, dtype=jnp.float32)[None, :]
    filters = jnp.zeros((residue.shape[0], tokens), jnp.float32)
    for mode_index in range(residue.shape[1]):
        rate = decay_rate[:, mode_index : mode_index + 1]
        filters = filters + residue[:, mode_index : mode_index + 1] * (
            jnp.sqrt(rate) * jnp.exp(-rate * positions)
        )
    return filters


def parameter_grads(lag_grad, residue, decay_rate, tokens):
    positions = jnp.arange(tokens, dtype=jnp.float32)[None, :]
    residue_cols = []
    log_cols = []
    for mode_index in range(residue.shape[1]):
        rate = decay_rate[:, mode_index : mode_index + 1]
        basis = jnp.sqrt(rate) * jnp.exp(-rate * positions)
        residue_cols.append(jnp.sum(lag_grad * basis, axis=1))
        log_cols.append(
            jnp.sum(lag_grad * basis * (0.5 - rate * positions), axis=1) * residue[:, mode_index]
        )
    return (jnp.stack(residue_cols, axis=1), jnp.stack(log_cols, axis=1))


def dft_tables(size_outer, size_inner):
    total = size_outer * size_inner
    index_outer = jnp.arange(size_outer, dtype=jnp.int32)
    index_inner = jnp.arange(size_inner, dtype=jnp.int32)
    angle_outer = (
        2.0
        * math.pi
        / size_outer
        * (index_outer[:, None] * index_outer[None, :] % size_outer).astype(jnp.float32)
    )
    angle_inner = (
        2.0
        * math.pi
        / size_inner
        * (index_inner[:, None] * index_inner[None, :] % size_inner).astype(jnp.float32)
    )
    angle_twist = (
        2.0
        * math.pi
        / total
        * (index_outer[:, None] * index_inner[None, :] % total).astype(jnp.float32)
    )
    return (
        jnp.cos(angle_outer),
        jnp.sin(angle_outer),
        jnp.cos(angle_inner),
        jnp.sin(angle_inner),
        jnp.cos(angle_twist),
        jnp.sin(angle_twist),
    )


def inner_product(spectrum, table):
    return jnp.einsum("ckb,bj->ckj", spectrum, table, precision=HIGHEST)


def forward_real(signal, tables):
    outer_cos, outer_sin, inner_cos, inner_sin, twist_cos, twist_sin = tables
    half = signal.shape[1]
    first_re = jnp.einsum("kn,cnb->ckb", outer_cos[:, :half], signal, precision=HIGHEST)
    first_im = -jnp.einsum("kn,cnb->ckb", outer_sin[:, :half], signal, precision=HIGHEST)
    mixed_re = first_re * twist_cos + first_im * twist_sin
    mixed_im = first_im * twist_cos - first_re * twist_sin
    spec_re = inner_product(mixed_re, inner_cos) + inner_product(mixed_im, inner_sin)
    spec_im = inner_product(mixed_im, inner_cos) - inner_product(mixed_re, inner_sin)
    return (spec_re, spec_im)


def inverse_real(spec_re, spec_im, tables):
    outer_cos, outer_sin, inner_cos, inner_sin, twist_cos, twist_sin = tables
    half = outer_cos.shape[0] // 2
    total = outer_cos.shape[0] * inner_cos.shape[0]
    back_re = inner_product(spec_re, inner_cos) - inner_product(spec_im, inner_sin)
    back_im = inner_product(spec_im, inner_cos) + inner_product(spec_re, inner_sin)
    turn_re = back_re * twist_cos - back_im * twist_sin
    turn_im = back_im * twist_cos + back_re * twist_sin
    signal = jnp.einsum("nk,ckb->cnb", outer_cos[:half], turn_re, precision=HIGHEST)
    signal = signal - jnp.einsum("nk,ckb->cnb", outer_sin[:half], turn_im, precision=HIGHEST)
    return signal * (1.0 / total)


def convolve(gated, gate_grad, filters):
    width, tokens = gated.shape
    total = 2 * tokens
    log_total = total.bit_length() - 1
    size_outer = 2 ** ((log_total + 1) // 2)
    size_inner = total // size_outer
    half = size_outer // 2
    tables = dft_tables(size_outer, size_inner)

    def to_rows(block):
        return block.astype(jnp.float32).reshape(width, half, size_inner)

    gate_re, gate_im = forward_real(to_rows(gated), tables)
    grad_re, grad_im = forward_real(to_rows(gate_grad), tables)
    filt_re, filt_im = forward_real(to_rows(filters), tables)
    conv_out = inverse_real(
        filt_re * gate_re - filt_im * gate_im, filt_re * gate_im + filt_im * gate_re, tables
    )
    conv_grad = inverse_real(
        filt_re * grad_re + filt_im * grad_im, filt_re * grad_im - filt_im * grad_re, tables
    )
    lag_grad = inverse_real(
        gate_re * grad_re + gate_im * grad_im, gate_re * grad_im - gate_im * grad_re, tables
    )
    conv_out = conv_out.reshape(width, tokens).astype(jnp.bfloat16)
    conv_grad = conv_grad.reshape(width, tokens).astype(jnp.bfloat16)
    lag_grad = lag_grad.reshape(width, tokens)
    return (conv_out, conv_grad, lag_grad)


def times_bf16(left, right):
    return (left.astype(jnp.float32) * right.astype(jnp.float32)).astype(jnp.bfloat16)


def local(query_proj, key_proj, value_proj, output_grad, residue, decay_rate):
    tok_dev, local_channels = query_proj.shape
    tokens = tok_dev * lax.axis_size("ctx")
    filters = filter_bank(residue, decay_rate, tokens)

    def to_channels(block):
        return block.T

    def to_tokens(block):
        return block.T

    query_own, key_own, value_own, upstream_own = (
        lax.all_to_all(to_channels(query_proj), "ctx", split_axis=0, concat_axis=1, tiled=True),
        lax.all_to_all(to_channels(key_proj), "ctx", split_axis=0, concat_axis=1, tiled=True),
        lax.all_to_all(to_channels(value_proj), "ctx", split_axis=0, concat_axis=1, tiled=True),
        lax.all_to_all(to_channels(output_grad), "ctx", split_axis=0, concat_axis=1, tiled=True),
    )
    gated = times_bf16(key_own, value_own)
    gate_grad = times_bf16(upstream_own, query_own)
    conv_out, conv_grad, lag_grad = convolve(gated, gate_grad, filters)
    query_own_grad = times_bf16(upstream_own, conv_out)
    key_own_grad = times_bf16(conv_grad, value_own)
    value_own_grad = times_bf16(conv_grad, key_own)
    query_back, key_back, value_back = (
        lax.all_to_all(query_own_grad, "ctx", split_axis=1, concat_axis=0, tiled=True),
        lax.all_to_all(key_own_grad, "ctx", split_axis=1, concat_axis=0, tiled=True),
        lax.all_to_all(value_own_grad, "ctx", split_axis=1, concat_axis=0, tiled=True),
    )
    query_grad = to_tokens(query_back)
    key_grad = to_tokens(key_back)
    value_grad = to_tokens(value_back)
    residue_part, log_part = parameter_grads(lag_grad, residue, decay_rate, tokens)
    scale = float(tokens) ** (-0.5)
    return (query_grad, key_grad, value_grad, residue_part * scale, log_part * scale)


def solution(mesh):
    in_specs = (
        P("ctx", "ch"),
        P("ctx", "ch"),
        P("ctx", "ch"),
        P("ctx", "ch"),
        P(("ch", "ctx"), None),
        P(("ch", "ctx"), None),
    )
    out_specs = (
        P("ctx", "ch"),
        P("ctx", "ch"),
        P("ctx", "ch"),
        P(("ch", "ctx"), None),
        P(("ch", "ctx"), None),
    )
    return jax.shard_map(local, mesh=mesh, in_specs=in_specs, out_specs=out_specs, check_vma=False)
```

profile of v0, /device:TPU:0, one launch (start us, length us, event | category | flops | bytes accessed | tf_op | source)
XLA Modules:
  0.0 272.9 jit_solution(3431453552114593290)
XLA Ops:
  0.7 2.1 copy.99
  2.8 7.5 %all-to-all-start.4 = ((bf16[16,128,128]{2,1,0:T(8,128)(2,1)}), bf16[16,128,128]{2,1,0:T(8,128)(2,1)S(1)}, u32[]{:S(2)}, u32[]{:S(2)}) async-start(bf16[16,128,128]{2,1,0:T(8,128)(2,1)} %bitcast.73), calls=%async_computation.4 | async-start | bytes 1048576 | tf_op jit(solution)/shard_map/all_to_all | solution.py:143
  10.3 1.0 copy.80
  11.3 13.4 %all-to-all-done.4 = bf16[16,128,128]{2,1,0:T(8,128)(2,1)S(1)} async-done(((bf16[16,128,128]{2,1,0:T(8,128)(2,1)}), bf16[16,128,128]{2,1,0:T(8,128)(2,1)S(1)}, u32[]{:S(2)}, u32[]{:S(2)}) %all-to-all-start.4) | async-done | bytes 524320 | tf_op jit(solution)/shard_map/all_to_all | solution.py:143
  25.6 4.1 %all-to-all-start.1 = ((bf16[16,128,128]{2,1,0:T(8,128)(2,1)}), bf16[16,128,128]{2,1,0:T(8,128)(2,1)S(1)}, u32[]{:S(2)}, u32[]{:S(2)}) async-start(bf16[16,128,128]{2,1,0:T(8,128)(2,1)} %bitcast.58), calls=%async_computation.1 | async-start | bytes 1048576 | tf_op jit(solution)/shard_map/all_to_all | solution.py:144
  31.9 12.3 %all-to-all-done.1 = bf16[16,128,128]{2,1,0:T(8,128)(2,1)S(1)} async-done(((bf16[16,128,128]{2,1,0:T(8,128)(2,1)}), bf16[16,128,128]{2,1,0:T(8,128)(2,1)S(1)}, u32[]{:S(2)}, u32[]{:S(2)}) %all-to-all-start.1) | async-done | bytes 524320 | tf_op jit(solution)/shard_map/all_to_all | solution.py:144
  44.1 4.1 %all-to-all-start.2 = ((bf16[16,128,128]{2,1,0:T(8,128)(2,1)}), bf16[16,128,128]{2,1,0:T(8,128)(2,1)S(1)}, u32[]{:S(2)}, u32[]{:S(2)}) async-start(bf16[16,128,128]{2,1,0:T(8,128)(2,1)} %bitcast.60), calls=%async_computation.2 | async-start | bytes 1048576 | tf_op jit(solution)/shard_map/all_to_all | solution.py:145
  50.0 6.4 %fusion.249 = f32[128,64,64]{0,2,1:T(8,128)} fusion(f32[64,64]{0,1:T(8,128)S(1)} %fusion.222, f32[128]{0:T(128)S(1)} %get-tuple-element.134, f32[128]{0:T(128)S(1)} %get-tuple-element.166, f32[128]{0:T(128)S(1)} %get-tuple-element.156, f32[128]{0:T(128)S(1)} %get-tuple-element.132, f32[128]{0:T(128)S(1)} %get-tuple-element.167, ...), kind=kOutput, calls=%fused_computation.260 | convolution fusion | flops 217841664 | bytes 2170880 | tf_op jit(solution)/shard_map/kn,cnb->ckb/dot_general | solution.py:76
  56.4 6.3 %all-to-all-done.2 = bf16[16,128,128]{2,1,0:T(8,128)(2,1)S(1)} async-done(((bf16[16,128,128]{2,1,0:T(8,128)(2,1)}), bf16[16,128,128]{2,1,0:T(8,128)(2,1)S(1)}, u32[]{:S(2)}, u32[]{:S(2)}) %all-to-all-start.2) | async-done | bytes 524320 | tf_op jit(solution)/shard_map/all_to_all | solution.py:145
  62.7 4.3 %all-to-all-start = ((bf16[16,128,128]{2,1,0:T(8,128)(2,1)}), bf16[16,128,128]{2,1,0:T(8,128)(2,1)S(1)}, u32[]{:S(2)}, u32[]{:S(2)}) async-start(bf16[16,128,128]{2,1,0:T(8,128)(2,1)} %bitcast.1), calls=%async_computation | async-start | bytes 1048576 | tf_op jit(solution)/shard_map/all_to_all | solution.py:146
  67.3 6.4 %fusion.248 = f32[128,64,64]{0,2,1:T(8,128)} fusion(f32[64,64]{0,1:T(8,128)S(1)} %fusion.223, f32[128]{0:T(128)S(1)} %get-tuple-element.134, f32[128]{0:T(128)S(1)} %get-tuple-element.166, f32[128]{0:T(128)S(1)} %get-tuple-element.156, f32[128]{0:T(128)S(1)} %get-tuple-element.132, f32[128]{0:T(128)S(1)} %get-tuple-element.167, ...), kind=kOutput, calls=%fused_computation.259 | convolution fusion | flops 217841664 | bytes 2170880 | tf_op jit(solution)/shard_map/kn,cnb->ckb/dot_general | solution.py:75
  74.4 1.0 fusion.169
  75.4 2.4 fusion.171
  77.8 3.6 %all-to-all-done = bf16[16,128,128]{2,1,0:T(8,128)(2,1)S(1)} async-done(((bf16[16,128,128]{2,1,0:T(8,128)(2,1)}), bf16[16,128,128]{2,1,0:T(8,128)(2,1)S(1)}, u32[]{:S(2)}, u32[]{:S(2)}) %all-to-all-start) | async-done | bytes 524320 | tf_op jit(solution)/shard_map/all_to_all | solution.py:146
  81.4 2.2 fusion.163
  83.6 1.3 copy.100
  84.9 1.0 fusion.165
  86.5 5.1 %fusion = (f32[128,64,64]{0,1,2:T(8,128)S(1)}, f32[128,64,64]{0,1,2:T(8,128)S(1)}, f32[128,64,64]{0,1,2:T(8,128)S(1)}, f32[128,64,64]{0,1,2:T(8,128)S(1)}, f32[1...) fusion(f32[128,64,64]{0,2,1:T(8,128)S(1)} %fusion.165, f32[64,64]{0,1:T(8,128)S(1)} %get-tuple-element.169, ...), kind=kOutput, calls=%fused_computation.2 | convolution fusion | flops 212336640 | bytes 23674880 | tf_op jit(solution)/shard_map/kn,cnb->ckb/dot_general | solution.py:75
  91.7 3.3 %fusion.30 = f32[128,64,64]{0,2,1:T(8,128)S(1)} fusion(f32[128,64,64]{0,1,2:T(8,128)S(1)} %get-tuple-element.73), kind=kOutput, calls=%fused_computation.54 | convolution fusion | flops 402710528 | bytes 4194304 | tf_op jit(solution)/shard_map/ckb,bj->ckj/dot_general | solution.py:69
  95.0 3.3 %fusion.32 = f32[128,64,64]{0,2,1:T(8,128)S(1)} fusion(f32[128,64,64]{0,1,2:T(8,128)S(1)} %get-tuple-element.73), kind=kOutput, calls=%fused_computation.56 | convolution fusion | flops 402710528 | bytes 4194304 | tf_op jit(solution)/shard_map/ckb,bj->ckj/dot_general | solution.py:69
  98.4 3.3 %fusion.38 = f32[128,64,64]{0,2,1:T(8,128)S(1)} fusion(f32[128,64,64]{0,1,2:T(8,128)S(1)} %get-tuple-element.84), kind=kOutput, calls=%fused_computation.62 | convolution fusion | flops 402710528 | bytes 4194304 | tf_op jit(solution)/shard_map/ckb,bj->ckj/dot_general | solution.py:69
  101.7 3.8 %fusion.40 = f32[128,64,64]{0,2,1:T(8,128)S(1)} fusion(f32[128,64,64]{0,1,2:T(8,128)S(1)} %get-tuple-element.84), kind=kOutput, calls=%fused_computation.64 | convolution fusion | flops 402710528 | bytes 4194304 | tf_op jit(solution)/shard_map/ckb,bj->ckj/dot_general | solution.py:69
  105.4 3.3 %fusion.46 = f32[128,64,64]{0,2,1:T(8,128)S(1)} fusion(f32[128,64,64]{0,1,2:T(8,128)S(1)} %get-tuple-element.86), kind=kOutput, calls=%fused_computation.70 | convolution fusion | flops 402710528 | bytes 4194304 | tf_op jit(solution)/shard_map/ckb,bj->ckj/dot_general | solution.py:69
  108.8 3.3 %fusion.48 = f32[128,64,64]{0,2,1:T(8,128)S(1)} fusion(f32[128,64,64]{0,1,2:T(8,128)S(1)} %get-tuple-element.86), kind=kOutput, calls=%fused_computation.72 | convolution fusion | flops 402710528 | bytes 4194304 | tf_op jit(solution)/shard_map/ckb,bj->ckj/dot_general | solution.py:69
  112.1 3.4 %fusion.66 = f32[128,64,64]{0,2,1:T(8,128)S(1)} fusion(f32[128,64,64]{0,2,1:T(8,128)S(1)} %fusion.32, f32[128,64,64]{0,1,2:T(8,128)S(1)} %get-tuple-element.72), kind=kOutput, calls=%fused_computation.82 | convolution fusion | flops 403234816 | bytes 6291456 | tf_op jit(solution)/shard_map/ckb,bj->ckj/dot_general | solution.py:69
  115.5 3.6 %fusion.69 = f32[128,64,64]{0,2,1:T(8,128)S(1)} fusion(f32[128,64,64]{0,2,1:T(8,128)S(1)} %fusion.30, f32[128,64,64]{0,1,2:T(8,128)S(1)} %get-tuple-element.72), kind=kOutput, calls=%fused_computation.83 | convolution fusion | flops 403234816 | bytes 6291456 | tf_op jit(solution)/shard_map/ckb,bj->ckj/dot_general | solution.py:69
  119.1 3.4 %fusion.54 = f32[128,64,64]{0,2,1:T(8,128)S(1)} fusion(f32[128,64,64]{0,2,1:T(8,128)S(1)} %fusion.48, f32[128,64,64]{0,1,2:T(8,128)S(1)} %get-tuple-element.87), kind=kOutput, calls=%fused_computation.78 | convolution fusion | flops 403234816 | bytes 6291456 | tf_op jit(solution)/shard_map/ckb,bj->ckj/dot_general | solution.py:69
  122.4 3.4 %fusion.57 = f32[128,64,64]{0,2,1:T(8,128)S(1)} fusion(f32[128,64,64]{0,2,1:T(8,128)S(1)} %fusion.46, f32[128,64,64]{0,1,2:T(8,128)S(1)} %get-tuple-element.87), kind=kOutput, calls=%fused_computation.79 | convolution fusion | flops 403234816 | bytes 6291456 | tf_op jit(solution)/shard_map/ckb,bj->ckj/dot_general | solution.py:69
  125.8 3.6 %fusion.60 = f32[128,64,64]{0,2,1:T(8,128)S(1)} fusion(f32[128,64,64]{0,2,1:T(8,128)S(1)} %fusion.40, f32[128,64,64]{0,1,2:T(8,128)S(1)} %get-tuple-element.85), kind=kOutput, calls=%fused_computation.80 | convolution fusion | flops 403234816 | bytes 6291456 | tf_op jit(solution)/shard_map/ckb,bj->ckj/dot_general | solution.py:69
  129.4 5.0 %multiply_add_fusion = (f32[128,64,64]{0,2,1:T(8,128)S(1)}, f32[128,64,64]{0,2,1:T(8,128)S(1)}, f32[128,64,64]{0,2,1:T(8,128)S(1)}, f32[128,64,64]{0,2,1:T(8,128...) fusion(f32[128,64,64]{0,2,1:T(8,128)S(1)} %fusion.69, f32[128,64,64]{0,2,1:T(8,128)S(1)} %fusion.60, ...), kind=kOutput, calls=%fused_computation.33 | convolution fusion | flops 412672000 | bytes 27262976 | tf_op jit(solution)/shard_map/ckb,bj->ckj/dot_general | solution.py:69
  134.4 3.5 %fusion.177 = f32[128,64,64]{0,2,1:T(8,128)} fusion(f32[128,64,64]{0,2,1:T(8,128)S(1)} %get-tuple-element.66), kind=kOutput, calls=%fused_computation.208 | convolution fusion | flops 402710528 | bytes 4194304 | tf_op jit(solution)/shard_map/ckb,bj->ckj/dot_general | solution.py:69
  138.0 3.4 %fusion.197 = f32[128,64,64]{0,2,1:T(8,128)} fusion(f32[128,64,64]{0,2,1:T(8,128)S(1)} %get-tuple-element.66), kind=kOutput, calls=%fused_computation.228 | convolution fusion | flops 402710528 | bytes 4194304 | tf_op jit(solution)/shard_map/ckb,bj->ckj/dot_general | solution.py:69
  141.3 3.4 %fusion.195 = f32[128,64,64]{0,2,1:T(8,128)} fusion(f32[128,64,64]{0,2,1:T(8,128)S(1)} %get-tuple-element.67), kind=kOutput, calls=%fused_computation.226 | convolution fusion | flops 402710528 | bytes 4194304 | tf_op jit(solution)/shard_map/ckb,bj->ckj/dot_general | solution.py:69
  144.8 3.9 %fusion.179 = f32[128,64,64]{0,2,1:T(8,128)} fusion(f32[128,64,64]{0,2,1:T(8,128)S(1)} %get-tuple-element.67), kind=kOutput, calls=%fused_computation.210 | convolution fusion | flops 402710528 | bytes 4194304 | tf_op jit(solution)/shard_map/ckb,bj->ckj/dot_general | solution.py:69
  148.7 2.2 fusion.199
  150.8 2.1 fusion.183
  153.0 2.1 fusion.181
  155.1 2.1 fusion.201
  157.3 2.1 fusion.205
  159.4 3.7 %fusion.189 = f32[128,64,64]{0,2,1:T(8,128)} fusion(f32[128,64,64]{0,2,1:T(8,128)S(1)} %get-tuple-element.80), kind=kOutput, calls=%fused_computation.220 | convolution fusion | flops 402710528 | bytes 4194304 | tf_op jit(solution)/shard_map/ckb,bj->ckj/dot_general | solution.py:69
  163.1 3.4 %fusion.187 = f32[128,64,64]{0,2,1:T(8,128)} fusion(f32[128,64,64]{0,2,1:T(8,128)S(1)} %get-tuple-element.81), kind=kOutput, calls=%fused_computation.218 | convolution fusion | flops 402710528 | bytes 4194304 | tf_op jit(solution)/shard_map/ckb,bj->ckj/dot_general | solution.py:69
  166.6 3.4 %fusion.207 = f32[128,64,64]{0,2,1:T(8,128)} fusion(f32[128,64,64]{0,2,1:T(8,128)S(1)} %get-tuple-element.81), kind=kOutput, calls=%fused_computation.238 | convolution fusion | flops 402710528 | bytes 4194304 | tf_op jit(solution)/shard_map/ckb,bj->ckj/dot_general | solution.py:69
  170.0 7.2 %fusion.14 = f32[128,64,32]{0,2,1:T(8,128)S(1)} fusion(f32[64,64]{0,1:T(8,128)S(1)} %get-tuple-element.169, f32[64,64]{0,1:T(8,128)S(1)} %get-tuple-element.170, f32[128,64,64]{0,2,1:T(8,128)S(1)} %fusion.183, f32[128,64,64]{0,2,1:T(8,128)S(1)} %fusion.201, f32[128,64,64]{0,2,1:T(8,128)S(1)} %fusion.181, f32[128,64,64]{0,2,1:T(8,128)S(1)} %fusion.199, ...), kind=kOutput, calls=%fused_computation.34 | convolution fusion | flops 203948032 | bytes 9486336 | tf_op jit(solution)/shard_map/nk,ckb->cnb/dot_general | solution.py:93
  177.1 7.0 %fusion.108 = f32[128,32,64]{0,1,2:T(8,128)S(1)} fusion(f32[128,64,32]{0,2,1:T(8,128)S(1)} %fusion.14, f32[64,64]{0,1:T(8,128)S(1)} %get-tuple-element.169, f32[64,64]{0,1:T(8,128)S(1)} %get-tuple-element.170, f32[128,64,64]{0,2,1:T(8,128)S(1)} %fusion.183, f32[128,64,64]{0,2,1:T(8,128)S(1)} %fusion.201, f32[128,64,64]{0,2,1:T(8,128)S(1)} %fusion.181, ...), kind=kOutput, calls=%fused_computation.101 | convolution fusion | flops 204996608 | bytes 10534912 | tf_op jit(solution)/shard_map/nk,ckb->cnb/dot_general | solution.py:92
  184.1 1.6 copy.113
  185.7 2.5 copy.114
  188.3 2.5 fusion.112
  190.8 4.7 %all-to-all-start.6 = ((bf16[128,16,128]{2,0,1:T(8,128)(2,1)}), bf16[128,16,128]{2,0,1:T(8,128)(2,1)}, u32[]{:S(2)}, u32[]{:S(2)}) async-start(bf16[128,16,128]{2,0,1:T(8,128)(2,1)} %get-tuple-element.82), calls=%async_computation.6 | async-start | bytes 1048576 | tf_op jit(solution)/shard_map/all_to_all | solution.py:157
  195.5 8.3 %fusion.22 = f32[128,64,32]{0,2,1:T(8,128)S(1)} fusion(f32[64,64]{0,1:T(8,128)S(1)} %get-tuple-element.169, f32[64,64]{0,1:T(8,128)S(1)} %get-tuple-element.170, f32[128,64,64]{0,2,1:T(8,128)} %fusion.189, f32[128,64,64]{0,2,1:T(8,128)} %fusion.207, f32[128,64,64]{0,2,1:T(8,128)} %fusion.187, f32[128,64,64]{0,2,1:T(8,128)S(1)} %fusion.205, ...), kind=kOutput, calls=%fused_computation.44 | convolution fusion | flops 203948032 | bytes 9486336 | tf_op jit(solution)/shard_map/nk,ckb->cnb/dot_general | solution.py:93
  203.8 7.0 %fusion.99 = f32[128,32,64]{0,1,2:T(8,128)S(1)} fusion(f32[128,64,32]{0,2,1:T(8,128)S(1)} %fusion.22, f32[64,64]{0,1:T(8,128)S(1)} %get-tuple-element.169, f32[64,64]{0,1:T(8,128)S(1)} %get-tuple-element.170, f32[128,64,64]{0,2,1:T(8,128)S(1)} %copy-done, f32[128,64,64]{0,2,1:T(8,128)S(1)} %copy-done.2, f32[128,64,64]{0,2,1:T(8,128)S(1)} %copy-done.1, ...), kind=kOutput, calls=%fused_computation.98 | convolution fusion | flops 204996608 | bytes 10534912 | tf_op jit(solution)/shard_map/nk,ckb->cnb/dot_general | solution.py:92
  211.4 1.3 copy.98
  212.8 8.3 %fusion.6 = f32[128,64,32]{0,2,1:T(8,128)S(1)} fusion(f32[64,64]{0,1:T(8,128)S(1)} %get-tuple-element.169, f32[64,64]{0,1:T(8,128)S(1)} %get-tuple-element.170, f32[128,64,64]{0,2,1:T(8,128)} %fusion.179, f32[128,64,64]{0,2,1:T(8,128)} %fusion.197, f32[128,64,64]{0,2,1:T(8,128)S(1)} %copy-done.3, f32[128,64,64]{0,2,1:T(8,128)} %fusion.195, ...), kind=kOutput, calls=%fused_computation.24 | convolution fusion | flops 203948032 | bytes 9486336 | tf_op jit(solution)/shard_map/nk,ckb->cnb/dot_general | solution.py:93
  221.2 11.1 %multiply_reduce_fusion.15 = (f32[128]{0:T(128)S(1)}, f32[128]{0:T(128)S(1)}, f32[128,32,64]{0,1,2:T(8,128)}) fusion(f32[128]{0:T(128)S(1)} %copy-done.30, f32[32,64]{0,1:T(8,128)S(1)} %copy-done.22, f32[128]{0:T(128)S(1)} %copy-done.29, f32[128]{0:T(128)S(1)} %copy-done.27, f32[128,64,32]{0,2,1:T(8,128)S(1)} %fusion.6, f32[64,64]{0,1:T(8,128)S(1)} %fusion.223, ...), kind=kOutput, calls=%fused_computation.125 | convolution fusion | flops 206569216 | bytes 10545664 | tf_op jit(solution)/shard_map/nk,ckb->cnb/dot_general | solution.py:92
  232.5 6.2 %all-to-all-start.5 = ((bf16[128,16,128]{2,0,1:T(8,128)(2,1)}), bf16[128,16,128]{2,0,1:T(8,128)(2,1)S(1)}, u32[]{:S(2)}, u32[]{:S(2)}) async-start(bf16[128,16,128]{2,0,1:T(8,128)(2,1)} %get-tuple-element.83), calls=%async_computation.5 | async-start | bytes 1048576 | tf_op jit(solution)/shard_map/all_to_all | solution.py:156
  238.8 2.2 fusion.117
  241.1 1.9 multiply_reduce_fusion.10
  243.3 1.9 multiply_reduce_fusion
  245.2 7.9 %all-to-all-done.5 = bf16[128,16,128]{2,0,1:T(8,128)(2,1)S(1)} async-done(((bf16[128,16,128]{2,0,1:T(8,128)(2,1)}), bf16[128,16,128]{2,0,1:T(8,128)(2,1)S(1)}, u32[]{:S(2)}, u32[]{:S(2)}) %all-to-all-start.5) | async-done | bytes 524320 | tf_op jit(solution)/shard_map/all_to_all | solution.py:156
  253.1 4.1 %all-to-all-start.3 = ((bf16[128,16,128]{2,0,1:T(8,128)(2,1)}), bf16[128,16,128]{2,0,1:T(8,128)(2,1)S(1)}, u32[]{:S(2)}, u32[]{:S(2)}) async-start(bf16[128,16,128]{2,0,1:T(8,128)(2,1)} %fusion.117), calls=%async_computation.3 | async-start | bytes 1048576 | tf_op jit(solution)/shard_map/all_to_all | solution.py:155
  257.4 1.9 multiply_reduce_fusion.5
  260.6 2.0 copy.124
  262.7 1.0 copy.123
  263.7 8.0 %all-to-all-done.3 = bf16[128,16,128]{2,0,1:T(8,128)(2,1)S(1)} async-done(((bf16[128,16,128]{2,0,1:T(8,128)(2,1)}), bf16[128,16,128]{2,0,1:T(8,128)(2,1)S(1)}, u32[]{:S(2)}, u32[]{:S(2)}) %all-to-all-start.3) | async-done | bytes 524320 | tf_op jit(solution)/shard_map/all_to_all | solution.py:155
  271.7 1.0 copy.122
  (232 shorter events, 7.8 us)
Async XLA Ops:
  0.6 29.0 %copy-start.19 = (bf16[128,2048]{1,0:T(8,128)(2,1)S(1)}, bf16[128,2048]{1,0:T(8,128)(2,1)}, u32[]{:S(2)}) copy-start(bf16[128,2048]{1,0:T(8,128)(2,1)} %param.8) | copy-start | bytes 1572868
  2.8 28.2 %copy-start.25 = (f32[128,16]{0,1:T(8,128)S(1)}, f32[128,16]{0,1:T(8,128)}, u32[]{:S(2)}) copy-start(f32[128,16]{0,1:T(8,128)} %param.11) | copy-start | bytes 24580
  2.8 28.2 %copy-start.23 = (f32[128,16]{0,1:T(8,128)S(1)}, f32[128,16]{0,1:T(8,128)}, u32[]{:S(2)}) copy-start(f32[128,16]{0,1:T(8,128)} %param.10) | copy-start | bytes 24580
  2.8 22.0 %all-to-all-start.4 = ((bf16[16,128,128]{2,1,0:T(8,128)(2,1)}), bf16[16,128,128]{2,1,0:T(8,128)(2,1)S(1)}, u32[]{:S(2)}, u32[]{:S(2)}) async-start(bf16[16,128,128]{2,1,0:T(8,128)(2,1)} %bitcast.73), calls=%async_computation.4 | async-start | bytes 1048576 | tf_op jit(solution)/shard_map/all_to_all | solution.py:143
  10.3 38.0 %copy-start.20 = (bf16[128,2048]{1,0:T(8,128)(2,1)S(1)}, bf16[128,2048]{1,0:T(8,128)(2,1)}, u32[]{:S(2)}) copy-start(bf16[128,2048]{1,0:T(8,128)(2,1)} %param.9) | copy-start | bytes 1572868
  25.6 18.6 %all-to-all-start.1 = ((bf16[16,128,128]{2,1,0:T(8,128)(2,1)}), bf16[16,128,128]{2,1,0:T(8,128)(2,1)S(1)}, u32[]{:S(2)}, u32[]{:S(2)}) async-start(bf16[16,128,128]{2,1,0:T(8,128)(2,1)} %bitcast.58), calls=%async_computation.1 | async-start | bytes 1048576 | tf_op jit(solution)/shard_map/all_to_all | solution.py:144
  31.0 54.0 %copy-start.16 = (f32[64,64]{0,1:T(8,128)}, f32[64,64]{0,1:T(8,128)S(1)}, u32[]{:S(2)}) copy-start(f32[64,64]{0,1:T(8,128)S(1)} %fusion.222) | copy-start | bytes 49156
  31.0 36.0 %copy-start.26 = (f32[128]{0:T(128)}, f32[128]{0:T(128)S(1)}, u32[]{:S(2)}) copy-start(f32[128]{0:T(128)S(1)} %get-tuple-element.158) | copy-start | bytes 1540
  31.0 36.0 %copy-start.63 = (f32[128]{0:T(128)}, f32[128]{0:T(128)S(1)}, u32[]{:S(2)}) copy-start(f32[128]{0:T(128)S(1)} %get-tuple-element.159) | copy-start | bytes 1540
  31.0 36.0 %copy-start.65 = (f32[128]{0:T(128)}, f32[128]{0:T(128)S(1)}, u32[]{:S(2)}) copy-start(f32[128]{0:T(128)S(1)} %get-tuple-element.160) | copy-start | bytes 1540
  31.1 36.0 %copy-start.67 = (f32[128]{0:T(128)}, f32[128]{0:T(128)S(1)}, u32[]{:S(2)}) copy-start(f32[128]{0:T(128)S(1)} %get-tuple-element.166) | copy-start | bytes 1540
  31.1 36.0 %copy-start.69 = (f32[128]{0:T(128)}, f32[128]{0:T(128)S(1)}, u32[]{:S(2)}) copy-start(f32[128]{0:T(128)S(1)} %get-tuple-element.167) | copy-start | bytes 1540
  31.1 36.0 %copy-start.71 = (f32[128]{0:T(128)}, f32[128]{0:T(128)S(1)}, u32[]{:S(2)}) copy-start(f32[128]{0:T(128)S(1)} %get-tuple-element.161) | copy-start | bytes 1540
  31.1 36.0 %copy-start.73 = (f32[128]{0:T(128)}, f32[128]{0:T(128)S(1)}, u32[]{:S(2)}) copy-start(f32[128]{0:T(128)S(1)} %get-tuple-element.162) | copy-start | bytes 1540
  31.1 36.0 %copy-start.75 = (f32[128]{0:T(128)}, f32[128]{0:T(128)S(1)}, u32[]{:S(2)}) copy-start(f32[128]{0:T(128)S(1)} %get-tuple-element.163) | copy-start | bytes 1540
  31.1 36.0 %copy-start.77 = (f32[128]{0:T(128)}, f32[128]{0:T(128)S(1)}, u32[]{:S(2)}) copy-start(f32[128]{0:T(128)S(1)} %get-tuple-element.164) | copy-start | bytes 1540
  31.1 36.0 %copy-start.79 = (f32[128]{0:T(128)}, f32[128]{0:T(128)S(1)}, u32[]{:S(2)}) copy-start(f32[128]{0:T(128)S(1)} %get-tuple-element.165) | copy-start | bytes 1540
  31.8 35.3 %copy-start.31 = (f32[128]{0:T(128)}, f32[128]{0:T(128)S(1)}, u32[]{:S(2)}) copy-start(f32[128]{0:T(128)S(1)} %get-tuple-element.124) | copy-start | bytes 1540
  31.8 35.4 %copy-start.34 = (f32[128]{0:T(128)}, f32[128]{0:T(128)S(1)}, u32[]{:S(2)}) copy-start(f32[128]{0:T(128)S(1)} %get-tuple-element.126) | copy-start | bytes 1540
  31.8 35.4 %copy-start.37 = (f32[128]{0:T(128)}, f32[128]{0:T(128)S(1)}, u32[]{:S(2)}) copy-start(f32[128]{0:T(128)S(1)} %get-tuple-element.139) | copy-start | bytes 1540
  31.8 35.4 %copy-start.39 = (f32[128]{0:T(128)}, f32[128]{0:T(128)S(1)}, u32[]{:S(2)}) copy-start(f32[128]{0:T(128)S(1)} %get-tuple-element.140) | copy-start | bytes 1540
  31.8 35.4 %copy-start.41 = (f32[128]{0:T(128)}, f32[128]{0:T(128)S(1)}, u32[]{:S(2)}) copy-start(f32[128]{0:T(128)S(1)} %get-tuple-element.141) | copy-start | bytes 1540
  31.8 35.4 %copy-start.44 = (f32[128]{0:T(128)}, f32[128]{0:T(128)S(1)}, u32[]{:S(2)}) copy-start(f32[128]{0:T(128)S(1)} %get-tuple-element.128) | copy-start | bytes 1540
  31.8 35.4 %copy-start.46 = (f32[128]{0:T(128)}, f32[128]{0:T(128)S(1)}, u32[]{:S(2)}) copy-start(f32[128]{0:T(128)S(1)} %get-tuple-element.129) | copy-start | bytes 1540
  31.8 35.4 %copy-start.48 = (f32[128]{0:T(128)}, f32[128]{0:T(128)S(1)}, u32[]{:S(2)}) copy-start(f32[128]{0:T(128)S(1)} %get-tuple-element.130) | copy-start | bytes 1540
  31.8 35.4 %copy-start.51 = (f32[128]{0:T(128)}, f32[128]{0:T(128)S(1)}, u32[]{:S(2)}) copy-start(f32[128]{0:T(128)S(1)} %get-tuple-element.132) | copy-start | bytes 1540
  31.8 35.4 %copy-start.54 = (f32[128]{0:T(128)}, f32[128]{0:T(128)S(1)}, u32[]{:S(2)}) copy-start(f32[128]{0:T(128)S(1)} %get-tuple-element.134) | copy-start | bytes 1540
  31.8 35.4 %copy-start.57 = (f32[128]{0:T(128)}, f32[128]{0:T(128)S(1)}, u32[]{:S(2)}) copy-start(f32[128]{0:T(128)S(1)} %get-tuple-element.136) | copy-start | bytes 1540
  31.8 35.4 %copy-start.59 = (f32[128]{0:T(128)}, f32[128]{0:T(128)S(1)}, u32[]{:S(2)}) copy-start(f32[128]{0:T(128)S(1)} %get-tuple-element.137) | copy-start | bytes 1540
  31.9 35.4 %copy-start.61 = (f32[128]{0:T(128)}, f32[128]{0:T(128)S(1)}, u32[]{:S(2)}) copy-start(f32[128]{0:T(128)S(1)} %get-tuple-element.138) | copy-start | bytes 1540
  44.1 29.8 %copy-start.8 = (bf16[16,128,128]{2,1,0:T(8,128)(2,1)}, bf16[16,128,128]{2,1,0:T(8,128)(2,1)S(1)}, u32[]{:S(2)}) copy-start(bf16[16,128,128]{2,1,0:T(8,128)(2,1)S(1)} %all-to-all-done.1) | copy-start | bytes 1572868
  44.1 18.6 %all-to-all-start.2 = ((bf16[16,128,128]{2,1,0:T(8,128)(2,1)}), bf16[16,128,128]{2,1,0:T(8,128)(2,1)S(1)}, u32[]{:S(2)}, u32[]{:S(2)}) async-start(bf16[16,128,128]{2,1,0:T(8,128)(2,1)} %bitcast.60), calls=%async_computation.2 | async-start | bytes 1048576 | tf_op jit(solution)/shard_map/all_to_all | solution.py:145
  48.3 18.9 %copy-start.21 = (f32[32,64]{0,1:T(8,128)}, f32[32,64]{0,1:T(8,128)S(1)}, u32[]{:S(2)}) copy-start(f32[32,64]{0,1:T(8,128)S(1)} %multiply_add_fusion.4) | copy-start | bytes 24580
  49.9 17.3 %copy-start.28 = (f32[128]{0:T(128)}, f32[128]{0:T(128)S(1)}, u32[]{:S(2)}) copy-start(f32[128]{0:T(128)S(1)} %get-tuple-element.105) | copy-start | bytes 1540
  49.9 17.3 %copy-start.81 = (f32[128]{0:T(128)}, f32[128]{0:T(128)S(1)}, u32[]{:S(2)}) copy-start(f32[128]{0:T(128)S(1)} %get-tuple-element.117) | copy-start | bytes 1540
  49.9 17.3 %copy-start.84 = (f32[128]{0:T(128)}, f32[128]{0:T(128)S(1)}, u32[]{:S(2)}) copy-start(f32[128]{0:T(128)S(1)} %get-tuple-element.119) | copy-start | bytes 1540
  49.9 17.3 %copy-start.87 = (f32[128]{0:T(128)}, f32[128]{0:T(128)S(1)}, u32[]{:S(2)}) copy-start(f32[128]{0:T(128)S(1)} %get-tuple-element.121) | copy-start | bytes 1540
  49.9 17.3 %copy-start.91 = (f32[128]{0:T(128)}, f32[128]{0:T(128)S(1)}, u32[]{:S(2)}) copy-start(f32[128]{0:T(128)S(1)} %get-tuple-element.107) | copy-start | bytes 1540
  50.0 17.3 %copy-start.94 = (f32[128]{0:T(128)}, f32[128]{0:T(128)S(1)}, u32[]{:S(2)}) copy-start(f32[128]{0:T(128)S(1)} %get-tuple-element.109) | copy-start | bytes 1540
  50.0 17.3 %copy-start.97 = (f32[128]{0:T(128)}, f32[128]{0:T(128)S(1)}, u32[]{:S(2)}) copy-start(f32[128]{0:T(128)S(1)} %get-tuple-element.111) | copy-start | bytes 1540
  50.0 17.3 %copy-start.100 = (f32[128]{0:T(128)}, f32[128]{0:T(128)S(1)}, u32[]{:S(2)}) copy-start(f32[128]{0:T(128)S(1)} %get-tuple-element.113) | copy-start | bytes 1540
  50.0 17.3 %copy-start.103 = (f32[128]{0:T(128)}, f32[128]{0:T(128)S(1)}, u32[]{:S(2)}) copy-start(f32[128]{0:T(128)S(1)} %get-tuple-element.115) | copy-start | bytes 1540
  62.7 11.2 %copy-start.12 = (bf16[16,128,128]{2,1,0:T(8,128)(2,1)}, bf16[16,128,128]{2,1,0:T(8,128)(2,1)S(1)}, u32[]{:S(2)}) copy-start(bf16[16,128,128]{2,1,0:T(8,128)(2,1)S(1)} %all-to-all-done.2) | copy-start | bytes 1572868
  62.7 18.7 %all-to-all-start = ((bf16[16,128,128]{2,1,0:T(8,128)(2,1)}), bf16[16,128,128]{2,1,0:T(8,128)(2,1)S(1)}, u32[]{:S(2)}, u32[]{:S(2)}) async-start(bf16[16,128,128]{2,1,0:T(8,128)(2,1)} %bitcast.1), calls=%async_computation | async-start | bytes 1048576 | tf_op jit(solution)/shard_map/all_to_all | solution.py:146
  190.8 41.7 %all-to-all-start.6 = ((bf16[128,16,128]{2,0,1:T(8,128)(2,1)}), bf16[128,16,128]{2,0,1:T(8,128)(2,1)}, u32[]{:S(2)}, u32[]{:S(2)}) async-start(bf16[128,16,128]{2,0,1:T(8,128)(2,1)} %get-tuple-element.82), calls=%async_computation.6 | async-start | bytes 1048576 | tf_op jit(solution)/shard_map/all_to_all | solution.py:157
  221.2 17.5 %copy-start.11 = (bf16[16,128,128]{2,1,0:T(8,128)(2,1)S(1)}, bf16[16,128,128]{2,1,0:T(8,128)(2,1)}, u32[]{:S(2)}) copy-start(bf16[16,128,128]{2,1,0:T(8,128)(2,1)} %copy-done.10) | copy-start | bytes 1572868
  232.5 20.7 %all-to-all-start.5 = ((bf16[128,16,128]{2,0,1:T(8,128)(2,1)}), bf16[128,16,128]{2,0,1:T(8,128)(2,1)S(1)}, u32[]{:S(2)}, u32[]{:S(2)}) async-start(bf16[128,16,128]{2,0,1:T(8,128)(2,1)} %get-tuple-element.83), calls=%async_computation.5 | async-start | bytes 1048576 | tf_op jit(solution)/shard_map/all_to_all | solution.py:156
  243.0 14.2 %copy-start.32 = (f32[128]{0:T(128)S(1)}, f32[128]{0:T(128)}, u32[]{:S(2)}) copy-start(f32[128]{0:T(128)} %copy-done.31) | copy-start | bytes 1540
  243.0 14.2 %copy-start.33 = (f32[128]{0:T(128)S(1)}, f32[128]{0:T(128)}, u32[]{:S(2)}) copy-start(f32[128]{0:T(128)} %get-tuple-element.125) | copy-start | bytes 1540
  243.0 14.2 %copy-start.35 = (f32[128]{0:T(128)S(1)}, f32[128]{0:T(128)}, u32[]{:S(2)}) copy-start(f32[128]{0:T(128)} %copy-done.34) | copy-start | bytes 1540
  243.1 14.2 %copy-start.36 = (f32[128]{0:T(128)S(1)}, f32[128]{0:T(128)}, u32[]{:S(2)}) copy-start(f32[128]{0:T(128)} %get-tuple-element.127) | copy-start | bytes 1540
  243.1 14.2 %copy-start.38 = (f32[128]{0:T(128)S(1)}, f32[128]{0:T(128)}, u32[]{:S(2)}) copy-start(f32[128]{0:T(128)} %copy-done.37) | copy-start | bytes 1540
  243.1 14.2 %copy-start.40 = (f32[128]{0:T(128)S(1)}, f32[128]{0:T(128)}, u32[]{:S(2)}) copy-start(f32[128]{0:T(128)} %copy-done.39) | copy-start | bytes 1540
  243.1 14.2 %copy-start.42 = (f32[128]{0:T(128)S(1)}, f32[128]{0:T(128)}, u32[]{:S(2)}) copy-start(f32[128]{0:T(128)} %copy-done.41) | copy-start | bytes 1540
  243.1 14.2 %copy-start.64 = (f32[128]{0:T(128)S(1)}, f32[128]{0:T(128)}, u32[]{:S(2)}) copy-start(f32[128]{0:T(128)} %copy-done.63) | copy-start | bytes 1540
  243.1 14.2 %copy-start.66 = (f32[128]{0:T(128)S(1)}, f32[128]{0:T(128)}, u32[]{:S(2)}) copy-start(f32[128]{0:T(128)} %copy-done.65) | copy-start | bytes 1540
  243.1 14.2 %copy-start.82 = (f32[128]{0:T(128)S(1)}, f32[128]{0:T(128)}, u32[]{:S(2)}) copy-start(f32[128]{0:T(128)} %copy-done.81) | copy-start | bytes 1540
  243.1 14.2 %copy-start.83 = (f32[128]{0:T(128)S(1)}, f32[128]{0:T(128)}, u32[]{:S(2)}) copy-start(f32[128]{0:T(128)} %get-tuple-element.118) | copy-start | bytes 1540
  243.1 14.2 %copy-start.85 = (f32[128]{0:T(128)S(1)}, f32[128]{0:T(128)}, u32[]{:S(2)}) copy-start(f32[128]{0:T(128)} %copy-done.84) | copy-start | bytes 1540
  243.1 14.2 %copy-start.86 = (f32[128]{0:T(128)S(1)}, f32[128]{0:T(128)}, u32[]{:S(2)}) copy-start(f32[128]{0:T(128)} %get-tuple-element.120) | copy-start | bytes 1540
  243.2 14.2 %copy-start.88 = (f32[128]{0:T(128)S(1)}, f32[128]{0:T(128)}, u32[]{:S(2)}) copy-start(f32[128]{0:T(128)} %copy-done.87) | copy-start | bytes 1540
  243.2 14.2 %copy-start.89 = (f32[128]{0:T(128)S(1)}, f32[128]{0:T(128)}, u32[]{:S(2)}) copy-start(f32[128]{0:T(128)} %get-tuple-element.122) | copy-start | bytes 1540
  245.2 14.1 %copy-start.24 = (f32[128,16]{0,1:T(8,128)S(1)}, f32[128,16]{0,1:T(8,128)}, u32[]{:S(2)}) copy-start(f32[128,16]{0,1:T(8,128)} %param.10) | copy-start | bytes 24580
  253.1 18.6 %all-to-all-start.3 = ((bf16[128,16,128]{2,0,1:T(8,128)(2,1)}), bf16[128,16,128]{2,0,1:T(8,128)(2,1)S(1)}, u32[]{:S(2)}, u32[]{:S(2)}) async-start(bf16[128,16,128]{2,0,1:T(8,128)(2,1)} %fusion.117), calls=%async_computation.3 | async-start | bytes 1048576 | tf_op jit(solution)/shard_map/all_to_all | solution.py:155
  (49 other events, 320.4 us)
where the time goes:
time: 278 us; the launch traced here: 273 us
  matrix products  149 us (54%)
  waiting for transfers between devices  51.6 us (19%)
  starting transfers between devices  34.9 us (13%)
  local copies, waits for them, and re-layouts  18.8 us (7%)
  other arithmetic  15.5 us (6%)
    dot_general x24, matrix products, inner_product(): return jnp.einsum('ckb,bj->ckj', spectrum, table, precision=HIGHEST)  78.1 us
    dot_general x3, matrix products, inverse_real(): jnp.einsum('nk,ckb->cnb', outer_cos[:half], turn_re, precision=HIGHEST)  25 us
    dot_general x3, matrix products, inverse_real(): jnp.einsum('nk,ckb->cnb', outer_sin[:half], turn_im, precision=HIGHEST)  23.8 us
    dot_general x3, matrix products, forward_real(): jnp.einsum('kn,cnb->ckb', outer_cos[:, :half], signal, precision=HIGHEST)  14 us
    all_to_all x1, waiting for transfers between devices, local(): lax.all_to_all(to_channels(query_proj), 'ctx', split_axis=0, concat_axis=...  13.4 us
    all_to_all x1, waiting for transfers between devices, local(): lax.all_to_all(to_channels(key_proj), 'ctx', split_axis=0, concat_axis=1,...  12.3 us
    unnamed x219, local copies, waits for them, and re-layouts  10.9 us
    dot_general x3, matrix products, forward_real(): jnp.einsum('kn,cnb->ckb', outer_sin[:, :half], signal, precision=HIGHEST)  8.5 us
  transfers between devices with their start and end apart: 7, of which 6 were waited for; matrix products, arithmetic and copies ran while one was open for 26% of the time, Pallas kernels for 0%

commit v1 on v0

v1 whole, which is shorter than its diff:
```python
import functools

import jax
import jax.numpy as jnp
from jax import lax
from jax.experimental import pallas as pl
from jax.experimental.pallas import tpu as pltpu
from jax.sharding import PartitionSpec as P

LANES = 128
SETS = 2
F32 = jnp.float32
BF16 = jnp.bfloat16


def load_rows(ref, start, size, stride):
    return ref[pl.ds(start, size, stride=stride), :]


def gate_kernel(q_ref, k_ref, v_ref, u_ref, x_ref, g_ref, *, groups):
    tokens = q_ref.shape[0]
    members = groups // SETS

    def body(tile, _):
        rows = pl.ds(pl.multiple_of(tile * 16, 16), 16)
        for group in range(groups):
            member, which = group // SETS, group % SETS
            cols = slice(group * LANES, (group + 1) * LANES)
            x = (k_ref[rows, cols].astype(F32) * v_ref[rows, cols].astype(F32)).astype(BF16).astype(F32)
            g = (u_ref[rows, cols].astype(F32) * q_ref[rows, cols].astype(F32)).astype(BF16).astype(F32)
            for half in range(2):
                where = pl.ds((tile * 16 + half * 8) * members + member, 8, stride=members)
                x_ref[which, where, :] = x[half * 8 : half * 8 + 8]
                g_ref[which, where, :] = g[half * 8 : half * 8 + 8]
        return 0

    lax.fori_loop(0, tokens // 16, body, 0)


def param_rows(par_ref, which, param, mode, modes, members):
    return load_rows(par_ref, (which * 2 + param) * modes + mode, members, SETS * 2 * modes)


def state_kernel(x_ref, g_ref, par_ref, s_ref, k_ref, *, tokens, modes, members, unroll):
    for which in range(SETS):
        w = [jnp.exp(-param_rows(par_ref, which, 0, m, modes, members)) for m in range(modes)]

        def step(t, carry):
            s, k = carry
            x = x_ref[which, pl.ds(t * members, members), :]
            g = g_ref[which, pl.ds((tokens - 1 - t) * members, members), :]
            return (
                tuple(w[m] * s[m] + x for m in range(modes)),
                tuple(w[m] * k[m] + g for m in range(modes)),
            )

        zero = tuple(jnp.zeros((members, LANES), F32) for _ in range(modes))
        s, k = lax.fori_loop(0, tokens, step, (zero, zero), unroll=unroll)
        for m in range(modes):
            s_ref[which, pl.ds(m, members, stride=modes), :] = s[m]
            k_ref[which, pl.ds(m, members, stride=modes), :] = k[m]


def local_kernel(x_ref, g_ref, par_ref, y_ref, z_ref, r_ref, d_ref, sd_ref, kd_ref, *, tokens, modes, members, unroll, part):
    for which in range(SETS):
        for first in range(0, modes, part):
            rate = [param_rows(par_ref, which, 0, first + m, modes, members) for m in range(part)]
            w = [jnp.exp(-rate[m]) for m in range(part)]
            amp = [param_rows(par_ref, which, 1, first + m, modes, members) * jnp.sqrt(rate[m]) for m in range(part)]
            zero = tuple(jnp.zeros((members, LANES), F32) for _ in range(part))

            def forward(t, carry):
                h, hd, r, d = carry
                at = pl.ds(t * members, members)
                x = x_ref[which, at, :]
                g = g_ref[which, at, :]
                hd = tuple(w[m] * (hd[m] + h[m]) for m in range(part))
                h = tuple(w[m] * h[m] + x for m in range(part))
                r = tuple(r[m] + g * h[m] for m in range(part))
                d = tuple(d[m] + g * hd[m] for m in range(part))
                y = functools.reduce(jnp.add, [amp[m] * h[m] for m in range(part)])
                if first:
                    y = y + y_ref[which, at, :]
                y_ref[which, at, :] = y
                return h, hd, r, d

            h, hd, r, d = lax.fori_loop(0, tokens, forward, (zero, zero, zero, zero), unroll=unroll)

            def backward(step, carry):
                k, kd = carry
                at = pl.ds((tokens - 1 - step) * members, members)
                g = g_ref[which, at, :]
                kd = tuple(w[m] * (kd[m] + k[m]) for m in range(part))
                k = tuple(w[m] * k[m] + g for m in range(part))
                z = functools.reduce(jnp.add, [amp[m] * k[m] for m in range(part)])
                if first:
                    z = z + z_ref[which, at, :]
                z_ref[which, at, :] = z
                return k, kd

            k, kd = lax.fori_loop(0, tokens, backward, (zero, zero), unroll=unroll)
            for m in range(part):
                at = pl.ds(first + m, members, stride=modes)
                r_ref[which, at, :] = r[m]
                d_ref[which, at, :] = d[m]
                sd_ref[which, at, :] = hd[m]
                kd_ref[which, at, :] = kd[m]


def finish_kernel(
    y_ref, z_ref, par_ref, hin_ref, kin_ref, k_ref, v_ref, u_ref, dq_ref, dk_ref, dv_ref, yo_ref, zo_ref,
    *, tokens, modes, members, unroll,
):
    groups = members * SETS
    for which in range(SETS):
        rate = [param_rows(par_ref, which, 0, m, modes, members) for m in range(modes)]
        w = [jnp.exp(-rate[m]) for m in range(modes)]
        amp = [param_rows(par_ref, which, 1, m, modes, members) * jnp.sqrt(rate[m]) * w[m] for m in range(modes)]
        p = tuple(amp[m] * hin_ref[which, pl.ds(m, members, stride=modes), :] for m in range(modes))
        q = tuple(amp[m] * kin_ref[which, pl.ds(m, members, stride=modes), :] for m in range(modes))

        def step(t, carry):
            p, q = carry
            at = pl.ds(t * members, members)
            back = pl.ds((tokens - 1 - t) * members, members)
            yo_ref[which, at, :] = y_ref[which, at, :] + functools.reduce(jnp.add, p)
            zo_ref[which, back, :] = z_ref[which, back, :] + functools.reduce(jnp.add, q)
            return tuple(w[m] * p[m] for m in range(modes)), tuple(w[m] * q[m] for m in range(modes))

        lax.fori_loop(0, tokens, step, (p, q), unroll=unroll)

    def body(tile, _):
        rows = pl.ds(pl.multiple_of(tile * 16, 16), 16)
        for group in range(groups):
            member, which = group // SETS, group % SETS
            cols = slice(group * LANES, (group + 1) * LANES)
            halves = [pl.ds((tile * 16 + half * 8) * members + member, 8, stride=members) for half in range(2)]
            y = jnp.concatenate([yo_ref[which, at, :] for at in halves], axis=0).astype(BF16).astype(F32)
            z = jnp.concatenate([zo_ref[which, at, :] for at in halves], axis=0).astype(BF16).astype(F32)
            dq_ref[rows, cols] = (u_ref[rows, cols].astype(F32) * y).astype(BF16)
            dk_ref[rows, cols] = (z * v_ref[rows, cols].astype(F32)).astype(BF16)
            dv_ref[rows, cols] = (z * k_ref[rows, cols].astype(F32)).astype(BF16)
        return 0

    lax.fori_loop(0, tokens // 16, body, 0)


def call(body, out_shape, n_in, flops, scratch=()):
    whole = pl.BlockSpec(memory_space=pltpu.VMEM)
    return pl.pallas_call(
        body,
        out_shape=out_shape,
        in_specs=[whole] * n_in,
        out_specs=jax.tree.map(lambda _: whole, out_shape),
        scratch_shapes=scratch,
        compiler_params=pltpu.CompilerParams(vmem_limit_bytes=32 * 1024 * 1024),
        cost_estimate=pl.CostEstimate(flops=flops, bytes_accessed=4 * 1024 * 1024, transcendentals=0),
    )


def exchange(value, distance, count):
    return lax.ppermute(value, "ctx", [(i, i ^ distance) for i in range(count)])


def gather_params(own, count):
    me = lax.axis_index("ctx")
    value, distance, axis = own, count // 2, 0
    while distance:
        other = exchange(value, distance, count)
        upper = (me // distance) % 2 == 1
        value = jnp.stack([jnp.where(upper, other, value), jnp.where(upper, value, other)], axis=axis)
        distance //= 2
        axis += 1
    return value.reshape((count,) + own.shape)


def scan_states(s, k, rate, count, tokens):
    me = lax.axis_index("ctx")
    core = me % 2
    other = 1 - core

    def fade(rate, chunks):
        return jnp.exp(rate * (-float(tokens) * jnp.asarray(chunks).astype(F32)))

    both = jnp.stack([s, k])
    mine = lax.dynamic_index_in_dim(both, core, 1, keepdims=False)
    theirs = exchange(lax.dynamic_index_in_dim(both, other, 1, keepdims=False).astype(BF16), 1, count).astype(F32)
    rate = lax.dynamic_index_in_dim(rate, core, 0, keepdims=False)
    fade_one = fade(rate, 1)
    first = jnp.where(core == 0, mine, theirs)
    last = jnp.where(core == 0, theirs, mine)
    s_sum = fade_one * first[0] + last[0]
    k_sum = first[1] + fade_one * last[1]
    before = jnp.zeros_like(s_sum)
    after = jnp.zeros_like(s_sum)
    span = 2
    pair = me // 2
    while span < count:
        ways = 4 if span * 4 == count else 2
        place = (me // span) % ways
        inside = 2 * (pair % (span // 2))
        total_s, total_k = s_sum, k_sum
        for hop in range(1, ways):
            partner = place ^ hop
            earlier = partner < place
            if span * ways == count:
                got = exchange(jnp.where(earlier, k_sum, s_sum).astype(BF16), hop * span, count).astype(F32)
                got_s = got_k = got
            else:
                got_s, got_k = exchange(jnp.stack([s_sum, k_sum]).astype(BF16), hop * span, count).astype(F32)
                far = fade(rate, span)
                total_s = jnp.where(earlier, far * got_s + s_sum, far * s_sum + got_s)
                total_k = jnp.where(earlier, got_k + far * k_sum, k_sum + far * got_k)
            gap_before = span * (place - partner - 1) + inside
            gap_after = span * (partner - place - 1) + (span - 2 - inside)
            weight = fade(rate, jnp.where(earlier, gap_before, gap_after))
            before = before + jnp.where(earlier, weight * got_s, 0.0)
            after = after + jnp.where(earlier, 0.0, weight * got_k)
        s_sum, k_sum = total_s, total_k
        span *= ways
    enter_first = jnp.stack([before, last[1] + fade_one * after])
    enter_last = jnp.stack([first[0] + fade_one * before, after])
    keep = jnp.where(core == 0, enter_first, enter_last)
    send = jnp.where(core == 0, enter_last, enter_first)
    got = exchange(send.astype(BF16), 1, count).astype(F32)
    whole = jnp.where(core == 0, jnp.stack([keep, got], 1), jnp.stack([got, keep], 1))
    return whole[0], whole[1]


def local(query_proj, key_proj, value_proj, output_grad, residue, decay_rate):
    tokens, channels = query_proj.shape
    own_channels, modes = residue.shape
    count = lax.axis_size("ctx")
    total_tokens = tokens * count
    groups = channels // LANES
    members = groups // SETS
    sizes = dict(tokens=tokens, modes=modes, members=members)
    work = tokens * channels * modes

    own = jnp.stack([decay_rate.T, residue.T])
    params = gather_params(own, count)
    if own_channels != LANES:
        params = params.transpose(1, 2, 0, 3).reshape(2, modes, groups, LANES).transpose(2, 0, 1, 3)
    rows = params.reshape(groups * 2 * modes, LANES)

    big = jax.ShapeDtypeStruct((SETS, tokens * members, LANES), F32)
    small = jax.ShapeDtypeStruct((SETS, members * modes, LANES), F32)
    gated, gate_grad = call(functools.partial(gate_kernel, groups=groups), (big, big), 4, work)(
        query_proj, key_proj, value_proj, output_grad
    )
    s, k = call(functools.partial(state_kernel, unroll=4, **sizes), (small, small), 3, work * 4)(gated, gate_grad, rows)
    y, z, r, d, s_d, k_d = call(
        functools.partial(local_kernel, unroll=2, part=min(8, modes), **sizes), (big, big) + (small,) * 4, 3, work * 16
    )(gated, gate_grad, rows)

    shape = (SETS, members, modes, LANES)
    s, k, r, d, s_d, k_d = (a.reshape(shape) for a in (s, k, r, d, s_d, k_d))
    rate = params[:, 0].reshape(members, SETS, modes, LANES).transpose(1, 0, 2, 3)
    h_in, k_in = scan_states(s, k, rate, count, tokens)
    w = jnp.exp(-rate)
    r_part = r + w * h_in * k
    d_part = d + w * (h_in * k_d + k_in * (s_d + s)) + float(tokens) * jnp.exp(-rate * float(tokens + 1)) * h_in * k_in

    dq, dk, dv = call(
        functools.partial(finish_kernel, unroll=2, **sizes),
        (jax.ShapeDtypeStruct((tokens, channels), BF16),) * 3,
        8,
        work * 4,
        (pltpu.VMEM(big.shape, F32), pltpu.VMEM(big.shape, F32)),
    )(y, z, rows, h_in.reshape(small.shape), k_in.reshape(small.shape), key_proj, value_proj, output_grad)

    parts = jnp.stack([r_part, d_part], axis=2).transpose(1, 0, 2, 3, 4).reshape(groups, 2, modes, LANES)
    if own_channels != LANES:
        parts = parts.transpose(1, 2, 0, 3).reshape(2, modes, count, own_channels).transpose(2, 0, 1, 3)
    sums = lax.all_to_all(parts, "ctx", split_axis=0, concat_axis=0, tiled=True).sum(axis=0)
    scale = float(total_tokens) ** (-0.5)
    root = jnp.sqrt(decay_rate)
    r_own, d_own = sums[0].T, sums[1].T
    residue_grad = scale * root * r_own
    log_grad = scale * residue * root * (0.5 * r_own - decay_rate * d_own)
    return dq, dk, dv, residue_grad, log_grad


def solution(mesh):
    in_specs = (P("ctx", "ch"),) * 4 + (P(("ch", "ctx"), None),) * 2
    out_specs = (P("ctx", "ch"),) * 3 + (P(("ch", "ctx"), None),) * 2
    return jax.shard_map(local, mesh=mesh, in_specs=in_specs, out_specs=out_specs, check_vma=False)
```

time: 278 us -> 74.6 us (0.27); the launches traced: 273 us -> 73.9 us
  matrix products: 149 us -> 0 us
  waiting for transfers between devices: 51.6 us -> 14.2 us
  Pallas kernels: 0 us -> 22.9 us
  starting transfers between devices: 34.9 us -> 20.2 us
  local copies, waits for them, and re-layouts: 18.8 us -> 6.63 us
  other arithmetic: 15.5 us -> 8.8 us
    dot_general x36 -> x0, matrix products: 149 us -> none  [the longest x24 78.1 us: inner_product(): return jnp.einsum('ckb,bj->ckj', spectrum, table, precision=HIGHEST)]
    all_to_all x7 -> x1, waiting for transfers between devices: 51.6 us -> 2.8 us  [local(): lax.all_to_all(parts, 'ctx', split_axis=0, concat_axis=0, tiled=True)]
    all_to_all x7 -> x1, starting transfers between devices: 34.9 us -> 5.31 us  [local(): lax.all_to_all(parts, 'ctx', split_axis=0, concat_axis=0, tiled=True)]
    pallas_call x0 -> x4, Pallas kernels: none -> 22.9 us  [the longest x1 13.3 us: local(): call(functools.partial(local_kernel, unroll=2, part=min(8, modes), **size...]
    ppermute x0 -> x10, starting transfers between devices: none -> 14.9 us  [exchange(): return lax.ppermute(value, 'ctx', [(i, i ^ distance) for i in range(count)])]
    ppermute x0 -> x10, waiting for transfers between devices: none -> 11.4 us  [exchange(): return lax.ppermute(value, 'ctx', [(i, i ^ distance) for i in range(count)])]
    convert_element_type x6 -> x0, local copies, waits for them, and re-layouts: 7.67 us -> none  [the longest x2 4.12 us: times_bf16(): left.astype(jnp.float32) * right.astype(jnp.float32)]
    unnamed x219 -> x48, local copies, waits for them, and re-layouts: 10.9 us -> 4.83 us
  transfers between devices with their start and end apart: 7 -> 11, of which waited for: 6 -> 7; matrix products, arithmetic and copies ran while one was open for 26% -> 2% of each run, Pallas kernels for 0% -> 27%
where the time goes in v1:
time: 74.6 us; the launch traced here: 73.9 us
  Pallas kernels  22.9 us (31%)
  starting transfers between devices  20.2 us (27%)
  waiting for transfers between devices  14.2 us (19%)
  other arithmetic  8.8 us (12%)
  local copies, waits for them, and re-layouts  6.63 us (9%)
  between operations  1.09 us (1%)
    ppermute x10, starting transfers between devices, exchange(): return lax.ppermute(value, 'ctx', [(i, i ^ distance) for i in range(count)])  14.9 us
    pallas_call x1, Pallas kernels, local(): call(functools.partial(local_kernel, unroll=2, part=min(8, modes), **size...  13.3 us
    ppermute x10, waiting for transfers between devices, exchange(): return lax.ppermute(value, 'ctx', [(i, i ^ distance) for i in range(count)])  11.4 us
    pallas_call x1, Pallas kernels, local(): call(functools.partial(finish_kernel, unroll=2, **sizes), (jax.ShapeDtype...  6.13 us
    all_to_all x1, starting transfers between devices, local(): lax.all_to_all(parts, 'ctx', split_axis=0, concat_axis=0, tiled=True)  5.31 us
    unnamed x48, local copies, waits for them, and re-layouts  4.83 us
    pallas_call x1, Pallas kernels, local(): call(functools.partial(state_kernel, unroll=4, **sizes), (small, small),...  2.96 us
    all_to_all x1, waiting for transfers between devices, local(): lax.all_to_all(parts, 'ctx', split_axis=0, concat_axis=0, tiled=True)  2.8 us
  transfers between devices with their start and end apart: 11, of which 7 were waited for; matrix products, arithmetic and copies ran while one was open for 2% of the time, Pallas kernels for 27%

profile of v1, /device:TPU:0, one launch (start us, length us, event | category | flops | bytes accessed | tf_op | source)
XLA Modules:
  0.0 73.9 jit_solution(14665431726111922798)
XLA Ops:
  0.6 0.7 pad_maximum_fusion.5
  1.3 4.0 %collective-permute-start = (f32[2,16,128]{2,1,0:T(8,128)S(1)}, f32[2,16,128]{2,1,0:T(8,128)S(1)}, u32[]{:S(2)}, u32[]{:S(2)}) collective-permute-start(f32[2,16,128]{2,1,0:T(8,128)S(1)} %pad_maximum_fusion.5), channel_id=1, source_target_pairs={{0,16},{2,18},{4,20},{6,22},{8,24},{10,26},{12,28},{14,30},{16,0},... | collective-permute-start | bytes 49160 | tf_op jit(solution)/shard_map/ppermute | solution.py:162
  5.4 1.7 %collective-permute-done = f32[2,16,128]{2,1,0:T(8,128)S(1)} collective-permute-done((f32[2,16,128]{2,1,0:T(8,128)S(1)}, f32[2,16,128]{2,1,0:T(8,128)S(1)}, u32[]{:S(2)}, u32[]{:S(2)}) %collective-permute-start) | collective-permute-done | bytes 16416 | tf_op jit(solution)/shard_map/ppermute | solution.py:162
  7.1 0.0 copy-done.23
  7.1 0.0 copy-done.22
  7.1 2.0 %collective-permute-start.1 = (f32[2,2,16,128]{3,2,1,0:T(8,128)S(1)}, f32[2,2,16,128]{3,2,1,0:T(8,128)S(1)}, u32[]{:S(2)}, u32[]{:S(2)}) collective-permute-start(f32[2,2,16,128]{3,2,1,0:T(8,128)S(1)} %pad_maximum_fusion.4), channel_id=1, source_target_pairs={{0,8},{2,10},{4,12},{6,14},{8,0},{10,2},{12,4},{14,6},{16,24},{18,... | collective-permute-start | bytes 98312 | tf_op jit(solution)/shard_map/ppermute | solution.py:162
  9.1 2.0 %collective-permute-done.1 = f32[2,2,16,128]{3,2,1,0:T(8,128)S(1)} collective-permute-done((f32[2,2,16,128]{3,2,1,0:T(8,128)S(1)}, f32[2,2,16,128]{3,2,1,0:T(8,128)S(1)}, u32[]{:S(2)}, u32[]{:S(2)}) %collective-permute-start.1) | collective-permute-done | bytes 32800 | tf_op jit(solution)/shard_map/ppermute | solution.py:162
  11.1 2.0 %collective-permute-start.2 = (f32[2,2,2,16,128]{4,3,2,1,0:T(8,128)S(1)}, f32[2,2,2,16,128]{4,3,2,1,0:T(8,128)S(1)}, u32[]{:S(2)}, u32[]{:S(2)}) collective-permute-start(f32[2,2,2,16,128]{4,3,2,1,0:T(8,128)S(1)} %pad_maximum_fusion.2), channel_id=1, source_target_pairs={{0,4},{2,6},{4,0},{6,2},{8,12},{10,14},{12,8},{14,10},{16,20},{18,... | collective-permute-start | bytes 196616 | tf_op jit(solution)/shard_map/ppermute | solution.py:162
  13.1 2.4 %collective-permute-done.2 = f32[2,2,2,16,128]{4,3,2,1,0:T(8,128)S(1)} collective-permute-done((f32[2,2,2,16,128]{4,3,2,1,0:T(8,128)S(1)}, f32[2,2,2,16,128]{4,3,2,1,0:T(8,128)S(1)}, u32[]{:S(2)}, u32[]{:S(2)}) %collective-permute-start.2) | collective-permute-done | bytes 65568 | tf_op jit(solution)/shard_map/ppermute | solution.py:162
  15.5 0.1 collective-permute-start.3
  15.6 0.0 copy-start.2
  15.6 1.0 %copy-done.2 = bf16[128,2048]{1,0:T(8,128)(2,1)S(1)} copy-done((bf16[128,2048]{1,0:T(8,128)(2,1)S(1)}, bf16[128,2048]{1,0:T(8,128)(2,1)}, u32[]{:S(2)}) %copy-start.2) | copy-done | bytes 524312
  16.7 1.0 %copy-done.11 = bf16[128,2048]{1,0:T(8,128)(2,1)S(1)} copy-done((bf16[128,2048]{1,0:T(8,128)(2,1)S(1)}, bf16[128,2048]{1,0:T(8,128)(2,1)}, u32[]{:S(2)}) %copy-start.11) | copy-done | bytes 524312
  17.7 0.5 shard_map.101
  18.2 0.0 collective-permute-done.3
  18.3 3.0 %shard_map.103 = (f32[2,128,128]{2,1,0:T(8,128)S(1)}, f32[2,128,128]{2,1,0:T(8,128)S(1)}) custom-call(f32[2,1024,128]{2,1,0:T(8,128)S(1)} %get-tuple-element.18.x_ref, f32[2,1024,128]{2,1,0:T(8,128)S(1)} %get-tuple-element.19.g_ref, f32[512,128]{1,0:T(8,128)S(1)} %bitcast.318), custom_call_target="tpu_custom_call" | custom-call | flops 16777216 | bytes 4194304 | tf_op jit(solution)/shard_map/pallas_call | solution.py:251
  21.3 0.0 copy-start.4
  21.3 0.7 fusion.15
  22.0 0.5 collective-permute-start.4
  22.4 0.0 copy-start.13
  22.5 1.2 %collective-permute-done.4 = bf16[2,8,16,128]{3,2,1,0:T(8,128)(2,1)} collective-permute-done((bf16[2,8,16,128]{3,2,1,0:T(8,128)(2,1)}, bf16[2,8,16,128]{3,2,1,0:T(8,128)(2,1)}, u32[]{:S(2)}, u32[]{:S(2)}) %collective-permute-start.4) | collective-permute-done | bytes 65568 | tf_op jit(solution)/shard_map/ppermute | solution.py:162
  23.7 0.0 copy-done.5
  23.7 0.9 %convert_select_fusion.1 = (f32[2,8,16,128]{3,2,1,0:T(8,128)S(1)}, f32[2,8,16,128]{3,2,1,0:T(8,128)S(1)}) fusion(bf16[2,8,16,128]{3,2,1,0:T(8,128)(2,1)} %collective-permute-done.4, pred[]{:T(512)S(6)} %eq.33, s32[]{:T(128)S(6)} %select_n.239, f32[1,2,8,16,128]{4,3,2,0,1:T(8,128)S(1)} %bitcast.323, f32[1,2,8,16,128]{4,3,2,0,1:T(8,128)S(1)} %bitcast.326), kind=kLoop, calls=%fused_computation.8 | loop fusion | flops 163840 | bytes 589829 | tf_op jit(solution)/shard_map/jit(_where)/select_n | solution.py:190
  24.5 0.0 copy-start.16
  24.6 0.6 copy-done.16
  25.2 0.0 copy-done.18
  25.2 0.6 pad_maximum_fusion.3
  25.9 1.9 %collective-permute-start.5 = (bf16[2,8,16,128]{3,2,1,0:T(8,128)(2,1)}, bf16[2,8,16,128]{3,2,1,0:T(8,128)(2,1)}, u32[]{:S(2)}, u32[]{:S(2)}) collective-permute-start(bf16[2,8,16,128]{3,2,1,0:T(8,128)(2,1)} %pad_maximum_fusion.3), channel_id=1, source_target_pairs={{0,4},{2,6},{4,0},{6,2},{8,12},{10,14},{12,8},{14,10},{16,20},{18,... | collective-permute-start | bytes 196616 | tf_op jit(solution)/shard_map/ppermute | solution.py:162
  27.8 2.9 %collective-permute-done.5 = bf16[2,8,16,128]{3,2,1,0:T(8,128)(2,1)} collective-permute-done((bf16[2,8,16,128]{3,2,1,0:T(8,128)(2,1)}, bf16[2,8,16,128]{3,2,1,0:T(8,128)(2,1)}, u32[]{:S(2)}, u32[]{:S(2)}) %collective-permute-start.5) | collective-permute-done | bytes 65568 | tf_op jit(solution)/shard_map/ppermute | solution.py:162
  30.7 0.8 %convert_element_type.51 = f32[2,8,16,128]{3,2,1,0:T(8,128)S(1)} convert(bf16[2,8,16,128]{3,2,1,0:T(8,128)(2,1)} %collective-permute-done.5) | non-fusion elementwise | flops 32768 | bytes 196608 | tf_op jit(solution)/shard_map/convert_element_type | solution.py:210
  31.6 1.7 %select_convert_fusion.2 = (bf16[8,16,128]{2,1,0:T(8,128)(2,1)}, bf16[8,16,128]{2,1,0:T(8,128)(2,1)S(1)}, bf16[8,16,128]{2,1,0:T(8,128)(2,1)S(1)}) fusion(pred[]{:T(512)S(6)} %lt.59, f32[2,8,16,128]{3,2,1,0:T(8,128)} %copy-done.18, f32[2,8,16,128]{3,2,1,0:T(8,128)} %copy-done.16, f32[2,8,16,128]{3,2,1,0:T(8,128)S(1)} %convert_element_type.51, ...), kind=kLoop, calls=%fused_computation.78 | loop fusion | flops 278528 | bytes 557062 | tf_op jit(solution)/shard_map/convert_element_type | solution.py:207
  33.2 0.0 copy-done.20
  33.2 0.6 select_convert_fusion.1
  33.8 2.8 %collective-permute-start.7 = (bf16[8,16,128]{2,1,0:T(8,128)(2,1)}, bf16[8,16,128]{2,1,0:T(8,128)(2,1)}, u32[]{:S(2)}, u32[]{:S(2)}) collective-permute-start(bf16[8,16,128]{2,1,0:T(8,128)(2,1)} %get-tuple-element.52), channel_id=1, source_target_pairs={{0,16},{2,18},{4,20},{6,22},{8,24},{10,26},{12,28},{14,30},{16,0},... | collective-permute-start | bytes 98312 | tf_op jit(solution)/shard_map/ppermute | solution.py:162
  36.6 1.3 %collective-permute-start.8 = (bf16[8,16,128]{2,1,0:T(8,128)(2,1)}, bf16[8,16,128]{2,1,0:T(8,128)(2,1)}, u32[]{:S(2)}, u32[]{:S(2)}) collective-permute-start(bf16[8,16,128]{2,1,0:T(8,128)(2,1)} %get-tuple-element.53), channel_id=1, source_target_pairs={{0,24},{2,26},{4,28},{6,30},{8,16},{10,18},{12,20},{14,22},{16,8},... | collective-permute-start | bytes 98312 | tf_op jit(solution)/shard_map/ppermute | solution.py:162
  38.0 0.3 collective-permute-start.6
  38.3 13.3 %shard_map.102 = (f32[2,1024,128]{2,1,0:T(8,128)S(1)}, f32[2,1024,128]{2,1,0:T(8,128)S(1)}, f32[2,128,128]{2,1,0:T(8,128)S(1)}, f32[2,128,128]{2,1,0:T(8,128)S(1...) custom-call(f32[2,1024,128]{2,1,0:T(8,128)S(1)} %get-tuple-element.18.x_ref, ...), custom_call_target="tpu_custom_call" | custom-call | flops 67108864 | bytes 4194304 | tf_op jit(solution)/shard_map/pallas_call | solution.py:252
  51.6 0.0 copy-start.15
  51.6 0.0 copy-start.17
  51.6 0.0 copy-start.19
  51.7 0.0 collective-permute-done.7
  51.7 0.0 collective-permute-done.8
  51.7 0.0 collective-permute-done.6
  51.7 1.0 %copy-done.15 = f32[16,1,16,128]{3,2,1,0:T(8,128)S(1)} copy-done((f32[16,1,16,128]{3,2,1,0:T(8,128)S(1)}, f32[16,1,16,128]{3,2,1,0:T(8,128)}, u32[]{:S(2)}) %copy-start.15) | copy-done | bytes 131096
  52.7 0.2 copy-done.17
  52.9 0.2 copy-done.19
  53.1 0.9 %bitcast_add_fusion.1 = (f32[8,16,128]{2,1,0:T(8,128)S(1)}, f32[8,16,128]{2,1,0:T(8,128)S(1)}, f32[8,16,128]{2,1,0:T(8,128)S(1)}, f32[8,16,128]{2,1,0:T(8,128)S(1)}) fusion(f32[2,8,16,128]{3,2,1,0:T(8,128)S(1)} %copy-done.17, f32[8,2,16,128]{3,2,1,0:T(8,128)S(1)} %bitcast.334, s32[]{:T(128)S(6)} %select_n.239, ...), kind=kLoop, calls=%fused_computation.61 | loop fusion | flops 507904 | bytes 688152 | tf_op jit(solution)/shard_map/add | solution.py:222
  54.0 0.1 collective-permute-start.9
  54.1 1.2 %collective-permute-done.9 = bf16[2,8,16,128]{3,2,1,0:T(8,128)(2,1)S(1)} collective-permute-done((bf16[2,8,16,128]{3,2,1,0:T(8,128)(2,1)S(1)}, bf16[2,8,16,128]{3,2,1,0:T(8,128)(2,1)S(1)}, u32[]{:S(2)}, u32[]{:S(2)}) %collective-permute-start.9) | collective-permute-done | bytes 65568 | tf_op jit(solution)/shard_map/ppermute | solution.py:162
  55.4 0.0 copy-start.12
  55.4 0.1 fusion.14
  55.5 0.6 copy-done.12
  56.1 0.0 copy-start.8
  56.2 0.7 copy.31
  56.9 5.3 %all-to-all-start = ((f32[16,2,16,128]{3,2,1,0:T(8,128)}), f32[16,2,16,128]{3,2,1,0:T(8,128)}, u32[]{:S(2)}, u32[]{:S(2)}) async-start(f32[16,2,16,128]{3,2,1,0:T(8,128)} %bitcast.336), calls=%async_computation | async-start | bytes 524288 | tf_op jit(solution)/shard_map/all_to_all | solution.py:275
  62.2 0.0 copy-start.3
  62.2 1.0 %fusion.38 = (f32[1,2,8,16,128]{4,3,1,2,0:T(8,128)S(1)}, f32[1,2,8,16,128]{4,3,1,2,0:T(8,128)S(1)}) fusion(f32[2,2,8,16,128]{4,3,1,2,0:T(8,128)} %copy-done.12), kind=kLoop, calls=%fused_computation.95 | loop fusion | bytes 524288 | tf_op jit(solution)/shard_map/slice | solution.py:227
  63.3 0.0 copy-done.10
  63.3 0.0 copy-done.8
  63.3 0.1 copy-done.3
  63.4 6.1 %shard_map.104 = (bf16[128,2048]{1,0:T(8,128)(2,1)}, bf16[128,2048]{1,0:T(8,128)(2,1)}, bf16[128,2048]{1,0:T(8,128)(2,1)}) custom-call(f32[2,1024,128]{2,1,0:T(8,128)S(1)} %copy-done.8, f32[2,1024,128]{2,1,0:T(8,128)S(1)} %copy-done.10, f32[512,128]{1,0:T(8,128)S(1)} %bitcast.321, f32[2,128,128]{2,1,0:T(8,128)S(1)} %bitcast.327, ...), custom_call_target="tpu_custom_call" | custom-call | flops 16777216 | bytes 4194304 | tf_op jit(solution)/shard_map/pallas_call | solution.py:264
  69.5 2.8 %all-to-all-done = f32[16,2,16,128]{3,2,1,0:T(8,128)} async-done(((f32[16,2,16,128]{3,2,1,0:T(8,128)}), f32[16,2,16,128]{3,2,1,0:T(8,128)}, u32[]{:S(2)}, u32[]{:S(2)}) %all-to-all-start) | async-done | bytes 262176 | tf_op jit(solution)/shard_map/all_to_all | solution.py:275
  72.3 1.0 %reduce_sum.9 = f32[2,16,128]{2,1,0:T(8,128)S(1)} reduce(f32[16,2,16,128]{3,2,1,0:T(8,128)} %all-to-all-done, f32[]{:T(128)} %constant.131.clone.1), dimensions={0}, to_apply=%region_0.1 | reduce | flops 61440 | bytes 278532 | tf_op jit(solution)/shard_map/reduce_sum | solution.py:275
  73.3 0.6 fusion.37
  (41 shorter events, 0.3 us)
Async XLA Ops:
  1.3 5.8 %collective-permute-start = (f32[2,16,128]{2,1,0:T(8,128)S(1)}, f32[2,16,128]{2,1,0:T(8,128)S(1)}, u32[]{:S(2)}, u32[]{:S(2)}) collective-permute-start(f32[2,16,128]{2,1,0:T(8,128)S(1)} %pad_maximum_fusion.5), channel_id=1, source_target_pairs={{0,16},{2,18},{4,20},{6,22},{8,24},{10,26},{12,28},{14,30},{16,0},... | collective-permute-start | bytes 49160 | tf_op jit(solution)/shard_map/ppermute | solution.py:162
  5.4 1.7 %copy-start.23 = (f32[128,16]{0,1:T(8,128)S(1)}, f32[128,16]{0,1:T(8,128)}, u32[]{:S(2)}) copy-start(f32[128,16]{0,1:T(8,128)} %param.11) | copy-start | bytes 24580
  5.4 1.7 %copy-start.22 = (f32[128,16]{0,1:T(8,128)S(1)}, f32[128,16]{0,1:T(8,128)}, u32[]{:S(2)}) copy-start(f32[128,16]{0,1:T(8,128)} %param.10) | copy-start | bytes 24580
  5.4 10.2 %copy-start = (bf16[128,2048]{1,0:T(8,128)(2,1)S(1)}, bf16[128,2048]{1,0:T(8,128)(2,1)}, u32[]{:S(2)}) copy-start(bf16[128,2048]{1,0:T(8,128)(2,1)} %k_ref.3) | copy-start | bytes 1572868
  5.4 10.2 %copy-start.1 = (bf16[128,2048]{1,0:T(8,128)(2,1)S(1)}, bf16[128,2048]{1,0:T(8,128)(2,1)}, u32[]{:S(2)}) copy-start(bf16[128,2048]{1,0:T(8,128)(2,1)} %v_ref.3) | copy-start | bytes 1572868
  7.1 4.0 %collective-permute-start.1 = (f32[2,2,16,128]{3,2,1,0:T(8,128)S(1)}, f32[2,2,16,128]{3,2,1,0:T(8,128)S(1)}, u32[]{:S(2)}, u32[]{:S(2)}) collective-permute-start(f32[2,2,16,128]{3,2,1,0:T(8,128)S(1)} %pad_maximum_fusion.4), channel_id=1, source_target_pairs={{0,8},{2,10},{4,12},{6,14},{8,0},{10,2},{12,4},{14,6},{16,24},{18,... | collective-permute-start | bytes 98312 | tf_op jit(solution)/shard_map/ppermute | solution.py:162
  11.1 4.3 %collective-permute-start.2 = (f32[2,2,2,16,128]{4,3,2,1,0:T(8,128)S(1)}, f32[2,2,2,16,128]{4,3,2,1,0:T(8,128)S(1)}, u32[]{:S(2)}, u32[]{:S(2)}) collective-permute-start(f32[2,2,2,16,128]{4,3,2,1,0:T(8,128)S(1)} %pad_maximum_fusion.2), channel_id=1, source_target_pairs={{0,4},{2,6},{4,0},{6,2},{8,12},{10,14},{12,8},{14,10},{16,20},{18,... | collective-permute-start | bytes 196616 | tf_op jit(solution)/shard_map/ppermute | solution.py:162
  15.5 2.8 %collective-permute-start.3 = (f32[2,2,2,2,16,128]{5,4,3,2,1,0:T(8,128)S(1)}, f32[2,2,2,2,16,128]{5,4,3,2,1,0:T(8,128)S(1)}, u32[]{:S(2)}, u32[]{:S(2)}) collective-permute-start(f32[2,2,2,2,16,128]{5,4,3,2,1,0:T(8,128)S(1)} %pad_maximum_fusion.1), channel_id=1, source_target_pairs={{0,2},{2,0},{4,6},{6,4},{8,10},{10,8},{12,14},{14,12},{16,18},{18,... | collective-permute-start | bytes 393224 | tf_op jit(solution)/shard_map/ppermute | solution.py:162
  15.6 1.0 %copy-start.2 = (bf16[128,2048]{1,0:T(8,128)(2,1)S(1)}, bf16[128,2048]{1,0:T(8,128)(2,1)}, u32[]{:S(2)}) copy-start(bf16[128,2048]{1,0:T(8,128)(2,1)} %u_ref.3) | copy-start | bytes 1572868
  16.7 1.0 %copy-start.11 = (bf16[128,2048]{1,0:T(8,128)(2,1)S(1)}, bf16[128,2048]{1,0:T(8,128)(2,1)}, u32[]{:S(2)}) copy-start(bf16[128,2048]{1,0:T(8,128)(2,1)} %q_ref.1) | copy-start | bytes 1572868
  21.3 0.7 copy-start.4
  22.0 1.7 %collective-permute-start.4 = (bf16[2,8,16,128]{3,2,1,0:T(8,128)(2,1)}, bf16[2,8,16,128]{3,2,1,0:T(8,128)(2,1)}, u32[]{:S(2)}, u32[]{:S(2)}) collective-permute-start(bf16[2,8,16,128]{3,2,1,0:T(8,128)(2,1)} %fusion.15), channel_id=1, source_target_pairs={{0,2},{2,0},{4,6},{6,4},{8,10},{10,8},{12,14},{14,12},{16,18},{18,... | collective-permute-start | bytes 196616 | tf_op jit(solution)/shard_map/ppermute | solution.py:162
  22.4 1.2 %copy-start.5 = (f32[2,128,128]{2,1,0:T(8,128)S(1)}, f32[2,128,128]{2,1,0:T(8,128)}, u32[]{:S(2)}) copy-start(f32[2,128,128]{2,1,0:T(8,128)} %copy-done.4) | copy-start | bytes 393220
  22.4 2.1 %copy-start.13 = (f32[16,1,16,128]{3,2,1,0:T(8,128)}, f32[16,1,16,128]{3,2,1,0:T(8,128)S(1)}, u32[]{:S(2)}) copy-start(f32[16,1,16,128]{3,2,1,0:T(8,128)S(1)} %slice.38) | copy-start | bytes 393220
  24.5 0.7 copy-start.16
  24.6 0.7 copy-start.18
  25.9 4.8 %collective-permute-start.5 = (bf16[2,8,16,128]{3,2,1,0:T(8,128)(2,1)}, bf16[2,8,16,128]{3,2,1,0:T(8,128)(2,1)}, u32[]{:S(2)}, u32[]{:S(2)}) collective-permute-start(bf16[2,8,16,128]{3,2,1,0:T(8,128)(2,1)} %pad_maximum_fusion.3), channel_id=1, source_target_pairs={{0,4},{2,6},{4,0},{6,2},{8,12},{10,14},{12,8},{14,10},{16,20},{18,... | collective-permute-start | bytes 196616 | tf_op jit(solution)/shard_map/ppermute | solution.py:162
  27.8 3.8 %copy-start.14 = (f32[16,1,16,128]{3,2,1,0:T(8,128)S(1)}, f32[16,1,16,128]{3,2,1,0:T(8,128)}, u32[]{:S(2)}) copy-start(f32[16,1,16,128]{3,2,1,0:T(8,128)} %copy-done.13) | copy-start | bytes 393220
  31.6 1.7 %copy-start.20 = (f32[2,8,16,128]{3,2,1,0:T(8,128)}, f32[2,8,16,128]{3,2,1,0:T(8,128)S(1)}, u32[]{:S(2)}) copy-start(f32[2,8,16,128]{3,2,1,0:T(8,128)S(1)} %convert_element_type.51) | copy-start | bytes 393220
  33.8 17.8 %collective-permute-start.7 = (bf16[8,16,128]{2,1,0:T(8,128)(2,1)}, bf16[8,16,128]{2,1,0:T(8,128)(2,1)}, u32[]{:S(2)}, u32[]{:S(2)}) collective-permute-start(bf16[8,16,128]{2,1,0:T(8,128)(2,1)} %get-tuple-element.52), channel_id=1, source_target_pairs={{0,16},{2,18},{4,20},{6,22},{8,24},{10,26},{12,28},{14,30},{16,0},... | collective-permute-start | bytes 98312 | tf_op jit(solution)/shard_map/ppermute | solution.py:162
  36.6 15.1 %collective-permute-start.8 = (bf16[8,16,128]{2,1,0:T(8,128)(2,1)}, bf16[8,16,128]{2,1,0:T(8,128)(2,1)}, u32[]{:S(2)}, u32[]{:S(2)}) collective-permute-start(bf16[8,16,128]{2,1,0:T(8,128)(2,1)} %get-tuple-element.53), channel_id=1, source_target_pairs={{0,24},{2,26},{4,28},{6,30},{8,16},{10,18},{12,20},{14,22},{16,8},... | collective-permute-start | bytes 98312 | tf_op jit(solution)/shard_map/ppermute | solution.py:162
  38.0 13.7 %collective-permute-start.6 = (bf16[8,16,128]{2,1,0:T(8,128)(2,1)}, bf16[8,16,128]{2,1,0:T(8,128)(2,1)}, u32[]{:S(2)}, u32[]{:S(2)}) collective-permute-start(bf16[8,16,128]{2,1,0:T(8,128)(2,1)} %get-tuple-element.35), channel_id=1, source_target_pairs={{0,8},{2,10},{4,12},{6,14},{8,0},{10,2},{12,4},{14,6},{16,24},{18,... | collective-permute-start | bytes 98312 | tf_op jit(solution)/shard_map/ppermute | solution.py:162
  38.2 13.4 %copy-start.6 = (f32[2,128,128]{2,1,0:T(8,128)S(1)}, f32[2,128,128]{2,1,0:T(8,128)}, u32[]{:S(2)}) copy-start(f32[2,128,128]{2,1,0:T(8,128)} %copy-done.4) | copy-start | bytes 393220
  38.3 13.5 %copy-start.21 = (f32[2,8,16,128]{3,2,1,0:T(8,128)S(1)}, f32[2,8,16,128]{3,2,1,0:T(8,128)}, u32[]{:S(2)}) copy-start(f32[2,8,16,128]{3,2,1,0:T(8,128)} %copy-done.20) | copy-start | bytes 393220
  51.6 3.8 %copy-start.7 = (f32[2,1024,128]{2,1,0:T(8,128)}, f32[2,1024,128]{2,1,0:T(8,128)S(1)}, u32[]{:S(2)}) copy-start(f32[2,1024,128]{2,1,0:T(8,128)S(1)} %get-tuple-element.20.y_ref) | copy-start | bytes 3145732
  51.6 3.8 %copy-start.9 = (f32[2,1024,128]{2,1,0:T(8,128)}, f32[2,1024,128]{2,1,0:T(8,128)S(1)}, u32[]{:S(2)}) copy-start(f32[2,1024,128]{2,1,0:T(8,128)S(1)} %get-tuple-element.21.z_ref) | copy-start | bytes 3145732
  51.6 1.1 %copy-start.15 = (f32[16,1,16,128]{3,2,1,0:T(8,128)S(1)}, f32[16,1,16,128]{3,2,1,0:T(8,128)}, u32[]{:S(2)}) copy-start(f32[16,1,16,128]{3,2,1,0:T(8,128)} %copy-done.13) | copy-start | bytes 393220
  51.6 1.3 %copy-start.17 = (f32[2,8,16,128]{3,2,1,0:T(8,128)S(1)}, f32[2,8,16,128]{3,2,1,0:T(8,128)}, u32[]{:S(2)}) copy-start(f32[2,8,16,128]{3,2,1,0:T(8,128)} %copy-done.16) | copy-start | bytes 393220
  51.6 1.5 %copy-start.19 = (f32[2,8,16,128]{3,2,1,0:T(8,128)S(1)}, f32[2,8,16,128]{3,2,1,0:T(8,128)}, u32[]{:S(2)}) copy-start(f32[2,8,16,128]{3,2,1,0:T(8,128)} %copy-done.18) | copy-start | bytes 393220
  54.0 1.3 %collective-permute-start.9 = (bf16[2,8,16,128]{3,2,1,0:T(8,128)(2,1)S(1)}, bf16[2,8,16,128]{3,2,1,0:T(8,128)(2,1)S(1)}, u32[]{:S(2)}, u32[]{:S(2)}) collective-permute-start(bf16[2,8,16,128]{3,2,1,0:T(8,128)(2,1)S(1)} %fusion.5), channel_id=1, source_target_pairs={{0,2},{2,0},{4,6},{6,4},{8,10},{10,8},{12,14},{14,12},{16,18},{18,... | collective-permute-start | bytes 196616 | tf_op jit(solution)/shard_map/ppermute | solution.py:162
  55.4 0.7 copy-start.12
  56.1 7.2 %copy-start.10 = (f32[2,1024,128]{2,1,0:T(8,128)S(1)}, f32[2,1024,128]{2,1,0:T(8,128)}, u32[]{:S(2)}) copy-start(f32[2,1024,128]{2,1,0:T(8,128)} %copy-done.9) | copy-start | bytes 3145732
  56.1 7.2 %copy-start.8 = (f32[2,1024,128]{2,1,0:T(8,128)S(1)}, f32[2,1024,128]{2,1,0:T(8,128)}, u32[]{:S(2)}) copy-start(f32[2,1024,128]{2,1,0:T(8,128)} %copy-done.7) | copy-start | bytes 3145732
  56.9 15.4 %all-to-all-start = ((f32[16,2,16,128]{3,2,1,0:T(8,128)}), f32[16,2,16,128]{3,2,1,0:T(8,128)}, u32[]{:S(2)}, u32[]{:S(2)}) async-start(f32[16,2,16,128]{3,2,1,0:T(8,128)} %bitcast.336), calls=%async_computation | async-start | bytes 524288 | tf_op jit(solution)/shard_map/all_to_all | solution.py:275
  62.2 1.2 %copy-start.3 = (bf16[128,2048]{1,0:T(8,128)(2,1)S(1)}, bf16[128,2048]{1,0:T(8,128)(2,1)}, u32[]{:S(2)}) copy-start(bf16[128,2048]{1,0:T(8,128)(2,1)} %u_ref.3) | copy-start | bytes 1572868

commit v2 on v0

v2 whole, which is shorter than its diff:
```python
import functools

import jax
import jax.numpy as jnp
from jax import lax
from jax.experimental import pallas as pl
from jax.experimental.pallas import tpu as pltpu
from jax.sharding import PartitionSpec as P

LANES = 128
SETS = 2
STRETCH = 8
F32 = jnp.float32
BF16 = jnp.bfloat16
VMEM = pl.BlockSpec(memory_space=pltpu.VMEM)
SMEM = pl.BlockSpec(memory_space=pltpu.SMEM)
ANY = pl.BlockSpec(memory_space=pl.ANY)
HBM = pl.BlockSpec(memory_space=pltpu.HBM)


def total(terms):
    terms = list(terms)
    while len(terms) > 1:
        terms = [a + b for a, b in zip(terms[::2], terms[1::2])] + terms[len(terms) & ~1 :]
    return terms[0]


def gate_kernel(q_hbm, k_hbm, v_hbm, u_hbm, x_ref, g_ref, stage_ref, sems, *, groups, pieces):
    tokens = q_hbm.shape[0]
    members = groups // SETS
    rows = tokens // pieces
    copies = []
    for piece in range(pieces):
        at = pl.ds(piece * rows, rows)
        for i, ref in enumerate((q_hbm, k_hbm, v_hbm, u_hbm)):
            copies.append(pltpu.make_async_copy(ref.at[at], stage_ref.at[i, at], sems.at[piece, i]))
            copies[-1].start()

    def body(tile, _):
        at = pl.ds(pl.multiple_of(tile * 16, 16), 16)
        for group in range(groups):
            member, which = group // SETS, group % SETS
            cols = slice(group * LANES, (group + 1) * LANES)
            q, k, v, u = (stage_ref[i, at, cols].astype(F32) for i in range(4))
            x = (k * v).astype(BF16).astype(F32)
            g = (u * q).astype(BF16).astype(F32)
            for half in range(2):
                where = pl.ds((tile * 16 + half * 8) * members + member, 8, stride=members)
                x_ref[which, where, :] = x[half * 8 : half * 8 + 8]
                g_ref[which, where, :] = g[half * 8 : half * 8 + 8]
        return 0

    for piece in range(pieces):
        for copy in copies[piece * 4 : piece * 4 + 4]:
            copy.wait()
        lax.fori_loop(piece * rows // 16, (piece + 1) * rows // 16, body, 0)


def param_rows(par_ref, which, param, mode, modes, members):
    return par_ref[pl.ds((which * 2 + param) * modes + mode, members, stride=SETS * 2 * modes), :]


def rate_block(par_ref, which, member, modes):
    start = ((member * SETS + which) * 2) * modes
    return par_ref[pl.ds(pl.multiple_of(start, modes), modes), :]


def lag_kernel(x_ref, g_ref, lag_ref, *, tokens, members):
    for which in range(SETS):

        def step(i, lags):
            base = i * STRETCH
            x = [x_ref[which, pl.ds((base + t) * members, members), :] for t in range(STRETCH)]
            g = [g_ref[which, pl.ds((base + t) * members, members), :] for t in range(STRETCH)]
            return tuple(lags[j] + total([g[t] * x[t - j] for t in range(j, STRETCH)]) for j in range(STRETCH))

        zero = tuple(jnp.zeros((members, LANES), F32) for _ in range(STRETCH))
        lags = lax.fori_loop(0, tokens // STRETCH, step, zero)
        for j in range(STRETCH):
            lag_ref[which, j] = lags[j]


def state_kernel(me_ref, x_ref, g_ref, par_ref, sk_ref, hs_ref, ks_ref, *scratch, tokens, modes, members, flip):
    core = me_ref[0] % SETS
    which = 1 - core if flip else core
    w = [jnp.exp(-param_rows(par_ref, which, 0, m, modes, members)) for m in range(modes)]
    stretches = tokens // STRETCH

    def step(i, carry):
        s, k = carry
        back = stretches - 1 - i
        for m in range(modes):
            hs_ref[i, m] = s[m]
        for t in range(STRETCH):
            x = x_ref[which, pl.ds((i * STRETCH + t) * members, members), :]
            g = g_ref[which, pl.ds((back * STRETCH + STRETCH - 1 - t) * members, members), :]
            s = tuple(w[m] * s[m] + x for m in range(modes))
            k = tuple(w[m] * k[m] + g for m in range(modes))
        for m in range(modes):
            ks_ref[back, m] = k[m]
        return s, k

    zero = tuple(jnp.zeros((members, LANES), F32) for _ in range(modes))
    s, k = lax.fori_loop(0, stretches, step, (zero, zero), unroll=2)
    full = scratch[0] if flip else sk_ref
    for m in range(modes):
        at = pl.ds(m, members, stride=modes)
        full[0, at, :] = s[m]
        full[1, at, :] = k[m]
    if flip:
        sk_ref[...] = full[...].astype(BF16)


def local_kernel(
    me_ref, x_ref, g_ref, lag_ref, hs_ref, ks_ref, par_ref, y_ref, z_ref, sums_ref, *, tokens, modes, members, part, flip
):
    core = me_ref[0] % SETS
    which = 1 - core if flip else core
    stretches = tokens // STRETCH
    length = float(STRETCH)
    taps = [jnp.zeros((members, LANES), F32)] * STRETCH
    zero = jnp.zeros((members, LANES), F32)
    for first in range(0, modes, part):
        rate = [param_rows(par_ref, which, 0, first + m, modes, members) for m in range(part)]
        w = [jnp.exp(-rate[m]) for m in range(part)]
        fade = [jnp.exp(rate[m] * -length) for m in range(part)]
        amp = [param_rows(par_ref, which, 1, first + m, modes, members) * jnp.sqrt(rate[m]) for m in range(part)]
        power = amp
        for j in range(STRETCH):
            taps[j] = taps[j] + total(power)
            power = [power[m] * w[m] for m in range(part)]

        def step(i, carry):
            back = stretches - 1 - i
            x = [x_ref[which, pl.ds((i * STRETCH + t) * members, members), :] for t in range(STRETCH)]
            g = [g_ref[which, pl.ds((back * STRETCH + t) * members, members), :] for t in range(STRETCH)]
            x = [x[t] * float(STRETCH - 1 - t) for t in range(STRETCH - 1)]
            g = [g[t] * float(t) for t in range(STRETCH)]
            out = []
            for m in range(part):
                same, next_, b_k, b_s, sd, kd = carry[m]
                h, k = hs_ref[i, first + m], ks_ref[i, first + m]
                h_back = hs_ref[back, first + m]
                after = lax.rem(i + 1, stretches)
                k_after = jnp.where(i + 1 == stretches, 0.0, ks_ref[after, first + m])
                after = lax.rem(back + 1, stretches)
                k_back = jnp.where(i == 0, 0.0, ks_ref[after, first + m])
                s_own = x[0]
                for t in range(1, STRETCH - 1):
                    s_own = s_own * w[m] + x[t]
                s_own = s_own * w[m]
                k_own = g[STRETCH - 1]
                for t in range(STRETCH - 2, 0, -1):
                    k_own = k_own * w[m] + g[t]
                k_own = k_own * w[m]
                out.append(
                    (
                        same + h * k,
                        next_ + h * k_after,
                        b_k + h_back * k_own,
                        b_s + k_after * s_own,
                        fade[m] * (sd + length * h) + s_own,
                        fade[m] * (kd + length * k_back) + k_own,
                    )
                )
            return tuple(out)

        sums = lax.fori_loop(0, stretches, step, ((zero,) * 6,) * part, unroll=2)
        for m in range(part):
            same, next_, b_k, b_s, sd, kd = sums[m]
            r, d = lag_ref[which, STRETCH - 1], (length - 1.0) * lag_ref[which, STRETCH - 1]
            for j in range(STRETCH - 2, -1, -1):
                r = r * w[m] + lag_ref[which, j]
                d = d * w[m] + float(j) * lag_ref[which, j]
            at = pl.ds(first + m, members, stride=modes)
            sums_ref[0, at, :] = r + w[m] * (same - fade[m] * next_)
            sums_ref[1, at, :] = d + w[m] * (b_k + b_s + same + (length - 1.0) * (fade[m] * next_))
            sums_ref[2, at, :] = sd
            sums_ref[3, at, :] = kd

    def within(i, _):
        at = [pl.ds((i * STRETCH + t) * members, members) for t in range(STRETCH)]
        x = [x_ref[which, at[t], :] for t in range(STRETCH)]
        g = [g_ref[which, at[t], :] for t in range(STRETCH)]
        for t in range(STRETCH):
            y_ref[at[t], :] = total([taps[j] * x[t - j] for j in range(t + 1)])
            z_ref[at[t], :] = total([taps[j] * g[t + j] for j in range(STRETCH - t)])
        return 0

    lax.fori_loop(0, stretches, within, 0, unroll=2)


def flags(bit):
    bit = bit.astype(F32)
    return bit, 1.0 - bit


def put_message(ref, me, span, at, s, k, last):
    if last:
        earlier, later = flags((me // span) % 2 == 1)
        ref[at, :] = (earlier * k + later * s).astype(BF16)
    else:
        ref[0, at, :] = s.astype(BF16)
        ref[1, at, :] = k.astype(BF16)


def pair_kernel(me_ref, mine_ref, got_ref, par_ref, tot_ref, message_ref, *, tokens, modes, members, last):
    me = me_ref[0]
    core = me % SETS
    second, first = flags(core == 1)
    for member in range(members):
        at = pl.ds(member * modes, modes)
        fade = jnp.exp(rate_block(par_ref, core, member, modes) * -float(tokens))
        s, k = mine_ref[0, at, :], mine_ref[1, at, :]
        gs, gk = got_ref[0, at, :].astype(F32), got_ref[1, at, :].astype(F32)
        s_sum = second * (fade * gs + s) + first * (fade * s + gs)
        k_sum = second * (gk + fade * k) + first * (k + fade * gk)
        tot_ref[0, at, :] = s_sum
        tot_ref[1, at, :] = k_sum
        put_message(message_ref, me, SETS, at, s_sum, k_sum, last)


def level_kernel(
    me_ref, tot_ref, got_ref, enter_ref, par_ref, out_ref, new_ref, message_ref, *, tokens, modes, members, span, last
):
    me = me_ref[0]
    core = me % SETS
    earlier, later = flags((me // span) % 2 == 1)
    inside = (me // 2) % (span // 2) * 2
    gap = earlier * inside.astype(F32) + later * (span - 2 - inside).astype(F32)
    for member in range(members):
        at = pl.ds(member * modes, modes)
        rate = rate_block(par_ref, core, member, modes)
        far = jnp.exp(rate * -float(tokens * span))
        weight = jnp.exp(rate * (gap * -float(tokens)))
        s, k = tot_ref[0, at, :], tot_ref[1, at, :]
        gs, gk = got_ref[0, at, :].astype(F32), got_ref[1, at, :].astype(F32)
        s_sum = earlier * (far * gs + s) + later * (far * s + gs)
        k_sum = earlier * (gk + far * k) + later * (k + far * gk)
        out_ref[0, at, :] = s_sum
        out_ref[1, at, :] = k_sum
        before = earlier * (weight * gs)
        after = later * (weight * gk)
        if span > 2:
            before += enter_ref[0, at, :]
            after += enter_ref[1, at, :]
        new_ref[0, at, :] = before
        new_ref[1, at, :] = after
        put_message(message_ref, me, span * 2, at, s_sum, k_sum, last)


def enter_kernel(
    me_ref, enter_ref, far_ref, mine_ref, got_ref, par_ref, keep_ref, send_ref, *, tokens, modes, members, span
):
    me = me_ref[0]
    core = me % SETS
    second, first = flags(core == 1)
    earlier, later = flags((me // span) % 2 == 1)
    inside = (me // 2) % (span // 2) * 2
    gap = earlier * inside.astype(F32) + later * (span - 2 - inside).astype(F32)
    for member in range(members):
        at = pl.ds(member * modes, modes)
        rate = rate_block(par_ref, core, member, modes)
        value = jnp.exp(rate * (gap * -float(tokens))) * far_ref[at, :].astype(F32)
        before, after = earlier * value, later * value
        if span > 2:
            before += enter_ref[0, at, :]
            after += enter_ref[1, at, :]
        fade = jnp.exp(rate * -float(tokens))
        s, k = mine_ref[0, at, :], mine_ref[1, at, :]
        gs, gk = got_ref[0, at, :].astype(F32), got_ref[1, at, :].astype(F32)
        near_s = (second * gs + first * s) + fade * before
        near_k = (first * gk + second * k) + fade * after
        keep_ref[0, at, :] = first * before + second * near_s
        keep_ref[1, at, :] = first * near_k + second * after
        send_ref[0, at, :] = (second * before + first * near_s).astype(BF16)
        send_ref[1, at, :] = (second * near_k + first * after).astype(BF16)


def finish_kernel(me_ref, y_ref, z_ref, hs_ref, ks_ref, par_ref, in_ref, k_ref, v_ref, u_ref, *refs, tokens, modes, members, flip):
    if flip:
        dq_ref, dk_ref, dv_ref, dq_hbm, dk_hbm, dv_hbm, token_ref, yo_ref, zo_ref, enter_ref, sems = refs[3:]
    else:
        dq_ref, dk_ref, dv_ref, token_ref, yo_ref, zo_ref, enter_ref = refs
    core = me_ref[0] % SETS
    which = 1 - core if flip else core
    stretches = tokens // STRETCH
    enter_ref[...] = in_ref[...].astype(F32)
    rate = [param_rows(par_ref, which, 0, m, modes, members) for m in range(modes)]
    w = [jnp.exp(-rate[m]) for m in range(modes)]
    fade = [jnp.exp(rate[m] * -float(STRETCH)) for m in range(modes)]
    amp = [param_rows(par_ref, which, 1, m, modes, members) * jnp.sqrt(rate[m]) * w[m] for m in range(modes)]
    h = tuple(enter_ref[0, pl.ds(m, members, stride=modes), :] for m in range(modes))
    k = tuple(enter_ref[1, pl.ds(m, members, stride=modes), :] for m in range(modes))

    def step(i, carry):
        h, k = carry
        back = stretches - 1 - i
        p = [amp[m] * (h[m] + hs_ref[i, m]) for m in range(modes)]
        for t in range(STRETCH):
            at = pl.ds((i * STRETCH + t) * members, members)
            yo_ref[at, :] = y_ref[at, :] + total(p)
            if t < STRETCH - 1:
                p = [w[m] * p[m] for m in range(modes)]
        after = lax.rem(back + 1, stretches)
        q = [amp[m] * (k[m] + jnp.where(i == 0, 0.0, ks_ref[after, m])) for m in range(modes)]
        for t in range(STRETCH):
            at = pl.ds((back * STRETCH + STRETCH - 1 - t) * members, members)
            zo_ref[at, :] = z_ref[at, :] + total(q)
            if t < STRETCH - 1:
                q = [w[m] * q[m] for m in range(modes)]
        return tuple(fade[m] * h[m] for m in range(modes)), tuple(fade[m] * k[m] for m in range(modes))

    lax.fori_loop(0, stretches, step, (h, k), unroll=1)

    copies = []
    token_ref[...] = yo_ref[0:8, :]
    for tile in range(tokens // 16):
        rows = pl.ds(tile * 16, 16)
        for member in range(members):
            cols = pl.ds(pl.multiple_of((member * SETS + which) * LANES, LANES), LANES)
            halves = [pl.ds((tile * 16 + half * 8) * members + member, 8, stride=members) for half in range(2)]
            y = jnp.concatenate([yo_ref[at, :] for at in halves], axis=0).astype(BF16).astype(F32)
            z = jnp.concatenate([zo_ref[at, :] for at in halves], axis=0).astype(BF16).astype(F32)
            dq_ref[rows, cols] = (u_ref[rows, cols].astype(F32) * y).astype(BF16)
            dk_ref[rows, cols] = (z * v_ref[rows, cols].astype(F32)).astype(BF16)
            dv_ref[rows, cols] = (z * k_ref[rows, cols].astype(F32)).astype(BF16)
        if flip:
            for index, (ref, out) in enumerate(((dq_ref, dq_hbm), (dk_ref, dk_hbm), (dv_ref, dv_hbm))):
                copies.append(pltpu.make_async_copy(ref.at[rows], out.at[rows], sems.at[index, tile]))
                copies[-1].start()
    for copy in copies:
        copy.wait()


def join(rate, left, right, length):
    r_a, d_a, sd_a, kd_a, s_a, k_a = left
    r_b, d_b, sd_b, kd_b, s_b, k_b = right
    w = jnp.exp(-rate)
    fade = jnp.exp(rate * -length)
    r = r_a + r_b + w * (s_a * k_b)
    d = d_a + d_b + w * (s_a * kd_b + (sd_a + s_a) * k_b)
    sd = fade * (sd_a + length * s_a) + sd_b
    kd = kd_a + fade * (kd_b + length * k_b)
    return r, d, sd, kd


def sums_kernel(me_ref, mine_ref, theirs_ref, sk_ref, got_ref, par_ref, *refs, tokens, modes, members, span):
    keep_ref, send_ref = refs[-2:]
    me = me_ref[0]
    core = me % SETS
    second, first = flags((me // span) % 2 == 1)
    side = (me // (span * 2)) % 2
    own = (me // 2) % span
    for ref, parity in ((keep_ref, side), (send_ref, 1 - side)):
        for to in range(members // span // 2):
            index = to * 2 + parity
            member = index * span + own
            src = pl.ds(pl.multiple_of(index * modes, modes), modes)
            at = pl.ds(pl.multiple_of(member * modes, modes), modes)
            mine = tuple(mine_ref[i, src, :] for i in range(4)) + (sk_ref[0, at, :], sk_ref[1, at, :])
            theirs = tuple(theirs_ref[i, src, :].astype(F32) for i in range(4)) + tuple(
                got_ref[i, at, :].astype(F32) for i in range(2)
            )
            left = tuple(second * b + first * a for a, b in zip(mine, theirs))
            right = tuple(second * a + first * b for a, b in zip(mine, theirs))
            for i, value in enumerate(join(rate_block(par_ref, core, member, modes), left, right, float(tokens * span))):
                ref[i, pl.ds(to * modes, modes), :] = value.astype(ref.dtype)


def sums_last_kernel(
    me_ref, mine_ref, theirs_ref, sk_ref, far_ref, own_ref, after_ref, r_out, log_out, *, modes, span, scale
):
    me = me_ref[0]
    second, first = flags((me // span) % 2 == 1)
    at = pl.ds(pl.multiple_of(me // 2 * modes, modes), modes)
    r_m, d_m, sd_m, kd_m = (mine_ref[i] for i in range(4))
    r_t, d_t, sd_t, kd_t = (theirs_ref[i].astype(F32) for i in range(4))
    far = far_ref[at, :].astype(F32)
    s_a = second * far + first * sk_ref[0, at, :]
    k_b = second * sk_ref[1, at, :] + first * far
    sd_a = second * sd_t + first * sd_m
    kd_b = second * kd_m + first * kd_t
    rate, residue = own_ref[0], own_ref[1]
    w = jnp.exp(-rate)
    r = r_m + r_t + w * (s_a * k_b)
    d = d_m + d_t + w * (s_a * kd_b + (sd_a + s_a) * k_b)
    root = jnp.sqrt(rate) * scale
    r_out[...] = root * r
    log_out[...] = root * residue * (0.5 * r - rate * d)


def call(body, out_shape, in_specs, flops, out_specs=None, scratch=(), aliases=None):
    return pl.pallas_call(
        body,
        out_shape=out_shape,
        in_specs=in_specs,
        out_specs=jax.tree.map(lambda _: VMEM, out_shape) if out_specs is None else out_specs,
        scratch_shapes=scratch,
        input_output_aliases=aliases or {},
        compiler_params=pltpu.CompilerParams(vmem_limit_bytes=16 * 1024 * 1024),
        cost_estimate=pl.CostEstimate(flops=flops, bytes_accessed=1024 * 1024, transcendentals=0),
    )


def exchange(value, distance, count):
    return lax.ppermute(value, "ctx", [(i, i ^ distance) for i in range(count)])


def tie(*values):
    return lax.optimization_barrier(values)


def local(query_proj, key_proj, value_proj, output_grad, residue, decay_rate):
    tokens, channels = query_proj.shape
    own_channels, modes = residue.shape
    count = lax.axis_size("ctx")
    groups = channels // LANES
    members = groups // SETS
    sizes = dict(tokens=tokens, modes=modes, members=members)
    work = tokens * channels * modes // SETS
    index = lax.axis_index("ctx")
    me = index.astype(jnp.int32).reshape(1)

    def shape(*dims, dtype=F32):
        return jax.ShapeDtypeStruct(dims, dtype)

    rows = members * modes
    gates = shape(SETS, tokens * members, LANES)
    series = shape(tokens * members, LANES)
    pair, pair16 = shape(2, rows, LANES), shape(2, rows, LANES, dtype=BF16)
    one16 = shape(rows, LANES, dtype=BF16)

    (own,) = tie(jnp.stack([decay_rate.T, residue.T]))
    params, distance, axis = own, count // 2, 0
    pieces = 4
    gated, gate_grad = call(
        functools.partial(gate_kernel, groups=groups, pieces=pieces),
        (gates, gates),
        [HBM] * 4,
        work,
        scratch=(pltpu.VMEM((4, tokens, channels), BF16), pltpu.SemaphoreType.DMA((pieces, 4))),
    )(*(pltpu.with_memory_space_constraint(a, pltpu.HBM) for a in (query_proj, key_proj, value_proj, output_grad)))
    while distance:
        other = exchange(params, distance, count)
        if axis == 0:
            other, gated, gate_grad = tie(other, gated, gate_grad)
            (lags,) = call(
                functools.partial(lag_kernel, tokens=tokens, members=members),
                (shape(SETS, STRETCH, members, LANES),),
                [VMEM] * 2,
                work,
            )(gated, gate_grad)
        if axis == 1:
            other, lags = tie(other, lags)
        upper = (index // distance) % 2 == 1
        params = jnp.stack([jnp.where(upper, other, params), jnp.where(upper, params, other)], axis=axis)
        distance //= 2
        axis += 1
    params = params.reshape((count,) + own.shape)
    if own_channels != LANES:
        params = params.transpose(1, 2, 0, 3).reshape(2, modes, groups, LANES).transpose(2, 0, 1, 3)
    par = params.reshape(groups * 2 * modes, LANES)

    entering = shape(tokens // STRETCH, modes, members, LANES)
    states_in = [SMEM, VMEM, VMEM, VMEM]
    sk_other, hs_other, ks_other = call(
        functools.partial(state_kernel, flip=True, **sizes),
        (pair16, entering, entering),
        states_in,
        work * 4,
        scratch=(pltpu.VMEM(pair.shape, F32),),
    )(me, gated, gate_grad, par)
    sk_got = exchange(sk_other, 1, count)
    sk_mine, hs_mine, ks_mine = call(
        functools.partial(state_kernel, flip=False, **sizes), (pair, entering, entering), states_in, work * 4
    )(me, gated, gate_grad, par)

    def within(flip, hs, ks):
        body = functools.partial(local_kernel, part=min(4, modes), flip=flip, **sizes)
        return call(body, (series, series, shape(4, rows, LANES)), [SMEM] + [VMEM] * 6, work * 6)(
            me, gated, gate_grad, lags, hs, ks, par
        )

    top = count // 2
    tot, message = call(
        functools.partial(pair_kernel, last=top == SETS, **sizes), (pair, one16 if top == SETS else pair16), [SMEM] + [VMEM] * 3, rows
    )(me, sk_mine, sk_got, par)
    y_other, z_other, sums_other = within(True, hs_other, ks_other)
    enter, levels, span = sk_mine, {}, SETS
    while span < top:
        got = exchange(message, span, count)
        if span == SETS:
            got, sums_other = tie(got, sums_other)
        levels[span] = tot, got
        last = span * 2 == top
        tot, enter, message = call(
            functools.partial(level_kernel, span=span, last=last, **sizes),
            (pair, pair, one16 if last else pair16),
            [SMEM] + [VMEM] * 4,
            rows,
        )(me, tot, got, enter, par)
        if span == SETS:
            tot, hs_mine, ks_mine = tie(tot, hs_mine, ks_mine)
        span *= 2
    far = exchange(message, top, count)
    y_mine, z_mine, sums_mine = within(False, hs_mine, ks_mine)

    def join_sums(span, kept, theirs, *after):
        half = rows // span // 2
        return call(
            functools.partial(sums_kernel, span=span, **sizes),
            (shape(4, half, LANES), shape(4, half, LANES, dtype=BF16)),
            [SMEM] + [VMEM] * (5 + len(after)),
            rows,
        )(me, kept, theirs, *levels[span], par, *after)

    tree = groups == count and top > 2 * SETS
    if tree:
        levels[1] = (sk_mine, sk_got)
        kept, message = join_sums(1, sums_mine, exchange(sums_other.astype(BF16), 1, count))
        kept, message = join_sums(2, kept, exchange(message, 2, count))
    keep, send = call(functools.partial(enter_kernel, span=top, **sizes), (pair, pair16), [SMEM] + [VMEM] * 5, rows)(
        me, enter, far, sk_mine, sk_got, par
    )
    enter_got = exchange(send, 1, count)
    if tree:
        message, keep = tie(message, keep)

    grads = (shape(tokens, channels, dtype=BF16),) * 3
    token = shape(8, LANES)
    scratch = (pltpu.VMEM(series.shape, F32), pltpu.VMEM(series.shape, F32), pltpu.VMEM(pair.shape, F32))
    finish = functools.partial(finish_kernel, **sizes)
    *done, token_first = call(functools.partial(finish, flip=False), grads + (token,), [SMEM] + [VMEM] * 9, work * 4, None, scratch)(
        me, y_mine, z_mine, hs_mine, ks_mine, par, keep, key_proj, value_proj, output_grad
    )
    *done, token_last = call(
        functools.partial(finish, flip=True),
        grads + grads + (token,),
        [SMEM] + [VMEM] * 12,
        work * 4,
        (VMEM,) * 3 + (ANY,) * 3 + (VMEM,),
        scratch + (pltpu.SemaphoreType.DMA((3, tokens // 16)),),
        {10: 0, 11: 1, 12: 2},
    )(me, y_other, z_other, hs_other, ks_other, par, enter_got, key_proj, value_proj, output_grad, *done)
    done = done[3:]

    scale = float(tokens * count) ** (-0.5)
    if tree:
        span = 4
        while span < top:
            kept, message = join_sums(span, kept, exchange(message, span, count), token_first)
            span *= 2
        out = call(
            functools.partial(sums_last_kernel, modes=modes, span=top, scale=scale),
            (shape(modes, LANES),) * 2,
            [SMEM] + [VMEM] * 6,
            rows,
        )(me, kept, exchange(message, top, count), tot, far, own, token_last)
        residue_grad, log_grad = out[0].T, out[1].T
    else:
        core = index % SETS
        dims = (members, modes, LANES)

        def sets(mine, other):
            mine, other = mine.astype(F32).reshape(dims), other.astype(F32).reshape(dims)
            return jnp.where(core == 0, jnp.stack([mine, other]), jnp.stack([other, mine]))

        h_in, k_in = (sets(keep[i], enter_got[i]) for i in range(2))
        s, k = (sets(sk_mine[i], sk_other[i]) for i in range(2))
        r, d, s_d, k_d = (sets(sums_mine[i], sums_other[i]) for i in range(4))
        rate = params[:, 0].reshape(members, SETS, modes, LANES).transpose(1, 0, 2, 3)
        w = jnp.exp(-rate)
        r_part = r + w * h_in * k
        d_part = d + w * (h_in * k_d + k_in * (s_d + s)) + float(tokens) * jnp.exp(-rate * float(tokens + 1)) * h_in * k_in
        parts = jnp.stack([r_part, d_part], axis=2).transpose(1, 0, 2, 3, 4).reshape(groups, 2, modes, LANES)
        parts = parts.transpose(1, 2, 0, 3).reshape(2, modes, count, own_channels).transpose(2, 0, 1, 3)
        sums = lax.all_to_all(parts, "ctx", split_axis=0, concat_axis=0, tiled=True).sum(axis=0)
        root = scale * jnp.sqrt(decay_rate)
        residue_grad = root * sums[0].T
        log_grad = root * residue * (0.5 * sums[0].T - decay_rate * sums[1].T)
    return (*done, residue_grad, log_grad)


def solution(mesh):
    in_specs = (P("ctx", "ch"),) * 4 + (P(("ch", "ctx"), None),) * 2
    out_specs = (P("ctx", "ch"),) * 3 + (P(("ch", "ctx"), None),) * 2
    return jax.shard_map(local, mesh=mesh, in_specs=in_specs, out_specs=out_specs, check_vma=False)
```

time: 278 us -> 46.7 us (0.17); the launches traced: 273 us -> 46.4 us
  matrix products: 149 us -> 0 us
  waiting for transfers between devices: 51.6 us -> 9.12 us
  local copies, waits for them, and re-layouts: 18.8 us -> 0.63 us
  Pallas kernels: 0 us -> 16.4 us
  starting transfers between devices: 34.9 us -> 18.6 us
  other arithmetic: 15.5 us -> 0.83 us
    dot_general x36 -> x0, matrix products: 149 us -> none  [the longest x24 78.1 us: inner_product(): return jnp.einsum('ckb,bj->ckj', spectrum, table, precision=HIGHEST)]
    all_to_all x7 -> x0, waiting for transfers between devices: 51.6 us -> none  [the longest x1 13.4 us: local(): lax.all_to_all(to_channels(query_proj), 'ctx', split_axis=0, concat_axis=...]
    all_to_all x7 -> x0, starting transfers between devices: 34.9 us -> none  [the longest x1 7.52 us: local(): lax.all_to_all(to_channels(query_proj), 'ctx', split_axis=0, concat_axis=...]
    ppermute x0 -> x13, starting transfers between devices: none -> 18.6 us  [exchange(): return lax.ppermute(value, 'ctx', [(i, i ^ distance) for i in range(count)])]
    pallas_call x0 -> x16, Pallas kernels: none -> 16.4 us  [the longest x2 5.41 us: within(): call(body, (series, series, shape(4, rows, LANES)), [SMEM] + [VMEM] * 6,...]
    unnamed x219 -> x6, local copies, waits for them, and re-layouts: 10.9 us -> 0.61 us
    ppermute x0 -> x13, waiting for transfers between devices: none -> 9.12 us  [exchange(): return lax.ppermute(value, 'ctx', [(i, i ^ distance) for i in range(count)])]
    convert_element_type x6 -> x0, local copies, waits for them, and re-layouts: 7.67 us -> none  [the longest x2 4.12 us: times_bf16(): left.astype(jnp.float32) * right.astype(jnp.float32)]
  transfers between devices with their start and end apart: 7 -> 13, of which waited for: 6 -> 5; matrix products, arithmetic and copies ran while one was open for 26% -> 0% of each run, Pallas kernels for 0% -> 31%
where the time goes in v2:
time: 46.7 us; the launch traced here: 46.4 us
  starting transfers between devices  18.6 us (40%)
  Pallas kernels  16.4 us (35%)
  waiting for transfers between devices  9.12 us (20%)
  between operations  0.87 us (2%)
  other arithmetic  0.83 us (2%)
  local copies, waits for them, and re-layouts  0.63 us (1%)
    ppermute x13, starting transfers between devices, exchange(): return lax.ppermute(value, 'ctx', [(i, i ^ distance) for i in range(count)])  18.6 us
    ppermute x13, waiting for transfers between devices, exchange(): return lax.ppermute(value, 'ctx', [(i, i ^ distance) for i in range(count)])  9.12 us
    pallas_call x2, Pallas kernels, within(): call(body, (series, series, shape(4, rows, LANES)), [SMEM] + [VMEM] * 6,...  5.41 us
    pallas_call x1, Pallas kernels, local(): call(functools.partial(finish, flip=True), grads + grads + (token,), [SME...  2.98 us
    pallas_call x1, Pallas kernels, local(): call(functools.partial(finish, flip=False), grads + (token,), [SMEM] + [V...  1.98 us
    pallas_call x1, Pallas kernels, local(): call(functools.partial(gate_kernel, groups=groups, pieces=pieces), (gates...  1.87 us
    pallas_call x1, Pallas kernels, local(): call(functools.partial(state_kernel, flip=True, **sizes), (pair16, enteri...  1.25 us
    pallas_call x1, Pallas kernels, local(): call(functools.partial(state_kernel, flip=False, **sizes), (pair, enterin...  1.22 us
  transfers between devices with their start and end apart: 13, of which 5 were waited for; matrix products, arithmetic and copies ran while one was open for 0% of the time, Pallas kernels for 31%

profile of v2, /device:TPU:0, one launch (start us, length us, event | category | flops | bytes accessed | tf_op | source)
XLA Modules:
  0.0 46.4 jit_solution(340036076788389672)
XLA Ops:
  0.6 0.7 %pad_maximum_fusion.4.own_ref = f32[2,16,128]{2,1,0:T(8,128)S(1)} fusion(f32[1,16,128]{2,1,0:T(8,128)} %bitcast.39, f32[1,16,128]{2,1,0:T(8,128)} %bitcast.40), kind=kLoop, calls=%fused_computation.10 | loop fusion | flops 4096 | bytes 32768 | tf_op jit(solution)/shard_map/stack | solution.py:434
  1.3 4.0 %collective-permute-start = (f32[2,16,128]{2,1,0:T(8,128)S(1)}, f32[2,16,128]{2,1,0:T(8,128)S(1)}, u32[]{:S(2)}, u32[]{:S(2)}) collective-permute-start(f32[2,16,128]{2,1,0:T(8,128)S(1)} %pad_maximum_fusion.4.own_ref), channel_id=1, source_target_pairs={{0,16},{2,18},{4,20},{6,22},{8,24},{10,26},{12,28},{14,30},{16,0},... | collective-permute-start | bytes 49160 | tf_op jit(solution)/shard_map/ppermute | solution.py:407
  5.4 1.9 %shard_map.101 = (f32[2,1024,128]{2,1,0:T(8,128)S(1)}, f32[2,1024,128]{2,1,0:T(8,128)S(1)}) custom-call(bf16[128,2048]{1,0:T(8,128)(2,1)} %q_hbm.1, bf16[128,2048]{1,0:T(8,128)(2,1)} %k_ref.3, bf16[128,2048]{1,0:T(8,128)(2,1)} %v_ref.3, bf16[128,2048]{1,0:T(8,128)(2,1)} %u_ref.3), custom_call_target="tpu_custom_call" | custom-call | flops 2097152 | bytes 1048576 | tf_op jit(solution)/shard_map/pallas_call | solution.py:437
  7.3 0.0 collective-permute-done
  7.3 1.8 %collective-permute-start.1 = (f32[2,2,16,128]{3,2,1,0:T(8,128)S(1)}, f32[2,2,16,128]{3,2,1,0:T(8,128)S(1)}, u32[]{:S(2)}, u32[]{:S(2)}) collective-permute-start(f32[2,2,16,128]{3,2,1,0:T(8,128)S(1)} %pad_maximum_fusion.3), channel_id=1, source_target_pairs={{0,8},{2,10},{4,12},{6,14},{8,0},{10,2},{12,4},{14,6},{16,24},{18,... | collective-permute-start | bytes 98312 | tf_op jit(solution)/shard_map/ppermute | solution.py:407
  9.1 0.5 %shard_map.102.lag_ref = f32[2,8,8,128]{3,2,1,0:T(8,128)S(1)} custom-call(f32[2,1024,128]{2,1,0:T(8,128)S(1)} %get-tuple-element.59.x_ref, f32[2,1024,128]{2,1,0:T(8,128)S(1)} %get-tuple-element.60.g_ref), custom_call_target="tpu_custom_call" | custom-call | flops 2097152 | bytes 1048576 | tf_op jit(solution)/shard_map/pallas_call | solution.py:448
  9.6 1.7 %collective-permute-done.1 = f32[2,2,16,128]{3,2,1,0:T(8,128)S(1)} collective-permute-done((f32[2,2,16,128]{3,2,1,0:T(8,128)S(1)}, f32[2,2,16,128]{3,2,1,0:T(8,128)S(1)}, u32[]{:S(2)}, u32[]{:S(2)}) %collective-permute-start.1) | collective-permute-done | bytes 32800 | tf_op jit(solution)/shard_map/ppermute | solution.py:407
  11.3 1.8 %collective-permute-start.2 = (f32[2,2,2,16,128]{4,3,2,0,1:T(8,128)S(1)}, f32[2,2,2,16,128]{4,3,2,0,1:T(8,128)S(1)}, u32[]{:S(2)}, u32[]{:S(2)}) collective-permute-start(f32[2,2,2,16,128]{4,3,2,0,1:T(8,128)S(1)} %pad_maximum_fusion.2), channel_id=1, source_target_pairs={{0,4},{2,6},{4,0},{6,2},{8,12},{10,14},{12,8},{14,10},{16,20},{18,... | collective-permute-start | bytes 196616 | tf_op jit(solution)/shard_map/ppermute | solution.py:407
  13.1 2.5 %collective-permute-done.2 = f32[2,2,2,16,128]{4,3,2,0,1:T(8,128)S(1)} collective-permute-done((f32[2,2,2,16,128]{4,3,2,0,1:T(8,128)S(1)}, f32[2,2,2,16,128]{4,3,2,0,1:T(8,128)S(1)}, u32[]{:S(2)}, u32[]{:S(2)}) %collective-permute-start.2) | collective-permute-done | bytes 65568 | tf_op jit(solution)/shard_map/ppermute | solution.py:407
  15.7 0.1 collective-permute-start.3
  15.8 1.3 %collective-permute-done.3 = f32[2,2,2,2,16,128]{5,4,3,0,1,2:T(8,128)S(1)} collective-permute-done((f32[2,2,2,2,16,128]{5,4,3,0,1,2:T(8,128)S(1)}, f32[2,2,2,2,16,128]{5,4,3,0,1,2:T(8,128)S(1)}, u32[]{:S(2)}, u32[]{:S(2)}) %collective-permute-start.3) | collective-permute-done | bytes 131104 | tf_op jit(solution)/shard_map/ppermute | solution.py:407
  17.2 1.2 %shard_map.103 = (bf16[2,128,128]{2,1,0:T(8,128)(2,1)S(1)}, f32[16,16,8,128]{3,2,1,0:T(8,128)S(1)}, f32[16,16,8,128]{3,2,1,0:T(8,128)S(1)}) custom-call(s32[1]{0:T(128)} %bitcast.me_ref, f32[2,1024,128]{2,1,0:T(8,128)S(1)} %get-tuple-element.59.x_ref, f32[2,1024,128]{2,1,0:T(8,128)S(1)} %get-tuple-element.60.g_ref, f32[512,128]{1,0:T(8,128)S(1)} %bitcast.26), custom_call_target="tpu_custom_call" | custom-call | flops 8388608 | bytes 1048576 | tf_op jit(solution)/shard_map/pallas_call | solution.py:467
  18.4 0.2 collective-permute-start.4
  18.6 1.2 %shard_map.105 = (f32[2,128,128]{2,1,0:T(8,128)S(1)}, f32[16,16,8,128]{3,2,1,0:T(8,128)S(1)}, f32[16,16,8,128]{3,2,1,0:T(8,128)S(1)}) custom-call(s32[1]{0:T(128)} %bitcast.me_ref, f32[2,1024,128]{2,1,0:T(8,128)S(1)} %get-tuple-element.59.x_ref, f32[2,1024,128]{2,1,0:T(8,128)S(1)} %get-tuple-element.60.g_ref, f32[512,128]{1,0:T(8,128)S(1)} %bitcast.27), custom_call_target="tpu_custom_call" | custom-call | flops 8388608 | bytes 1048576 | tf_op jit(solution)/shard_map/pallas_call | solution.py:475
  19.9 0.0 collective-permute-done.4.got_ref
  19.9 0.1 shard_map.106
  19.9 1.8 %collective-permute-start.5 = (bf16[2,128,128]{2,1,0:T(8,128)(2,1)S(1)}, bf16[2,128,128]{2,1,0:T(8,128)(2,1)S(1)}, u32[]{:S(2)}, u32[]{:S(2)}) collective-permute-start(bf16[2,128,128]{2,1,0:T(8,128)(2,1)S(1)} %get-tuple-element.71), channel_id=1, source_target_pairs={{0,4},{2,6},{4,0},{6,2},{8,12},{10,14},{12,8},{14,10},{16,20},{18,... | collective-permute-start | bytes 196616 | tf_op jit(solution)/shard_map/ppermute | solution.py:407
  21.7 2.7 %shard_map.104 = (f32[1024,128]{1,0:T(8,128)S(1)}, f32[1024,128]{1,0:T(8,128)S(1)}, f32[4,128,128]{2,1,0:T(8,128)S(1)}) custom-call(s32[1]{0:T(128)} %bitcast.me_ref, f32[2,1024,128]{2,1,0:T(8,128)S(1)} %get-tuple-element.59.x_ref, f32[2,1024,128]{2,1,0:T(8,128)S(1)} %get-tuple-element.60.g_ref, f32[2,8,8,128]{3,2,1,0:T(8,128)S(1)} %shard_map.102.lag_ref, ...), custom_call_target="tpu_custom_call" | custom-call | flops 12582912 | bytes 1048576 | tf_op jit(solution)/shard_map/pallas_call | solution.py:481
  24.4 0.0 collective-permute-done.5.got_ref
  24.5 0.1 collective-permute-start.9
  24.6 0.1 shard_map.107
  24.7 1.6 %collective-permute-start.6 = (bf16[2,128,128]{2,1,0:T(8,128)(2,1)S(1)}, bf16[2,128,128]{2,1,0:T(8,128)(2,1)S(1)}, u32[]{:S(2)}, u32[]{:S(2)}) collective-permute-start(bf16[2,128,128]{2,1,0:T(8,128)(2,1)S(1)} %get-tuple-element.78), channel_id=1, source_target_pairs={{0,8},{2,10},{4,12},{6,14},{8,0},{10,2},{12,4},{14,6},{16,24},{18,... | collective-permute-start | bytes 196616 | tf_op jit(solution)/shard_map/ppermute | solution.py:407
  26.3 2.7 %shard_map.110 = (f32[1024,128]{1,0:T(8,128)S(1)}, f32[1024,128]{1,0:T(8,128)S(1)}, f32[4,128,128]{2,1,0:T(8,128)S(1)}) custom-call(s32[1]{0:T(128)} %bitcast.me_ref, f32[2,1024,128]{2,1,0:T(8,128)S(1)} %get-tuple-element.59.x_ref, f32[2,1024,128]{2,1,0:T(8,128)S(1)} %get-tuple-element.60.g_ref, f32[2,8,8,128]{3,2,1,0:T(8,128)S(1)} %shard_map.102.lag_ref, ...), custom_call_target="tpu_custom_call" | custom-call | flops 12582912 | bytes 1048576 | tf_op jit(solution)/shard_map/pallas_call | solution.py:481
  29.0 0.0 collective-permute-done.9.theirs_ref
  29.1 0.2 shard_map.111
  29.2 1.6 %collective-permute-start.10 = (bf16[4,64,128]{2,1,0:T(8,128)(2,1)S(1)}, bf16[4,64,128]{2,1,0:T(8,128)(2,1)S(1)}, u32[]{:S(2)}, u32[]{:S(2)}) collective-permute-start(bf16[4,64,128]{2,1,0:T(8,128)(2,1)S(1)} %get-tuple-element.90), channel_id=1, source_target_pairs={{0,4},{2,6},{4,0},{6,2},{8,12},{10,14},{12,8},{14,10},{16,20},{18,... | collective-permute-start | bytes 196616 | tf_op jit(solution)/shard_map/ppermute | solution.py:407
  30.8 0.0 collective-permute-done.6.got_ref
  30.8 0.0 copy-start.2
  30.8 0.1 shard_map.108
  30.9 2.7 %collective-permute-start.7 = (bf16[128,128]{1,0:T(8,128)(2,1)S(1)}, bf16[128,128]{1,0:T(8,128)(2,1)S(1)}, u32[]{:S(2)}, u32[]{:S(2)}) collective-permute-start(bf16[128,128]{1,0:T(8,128)(2,1)S(1)} %get-tuple-element.81), channel_id=1, source_target_pairs={{0,16},{2,18},{4,20},{6,22},{8,24},{10,26},{12,28},{14,30},{16,0},... | collective-permute-start | bytes 98312 | tf_op jit(solution)/shard_map/ppermute | solution.py:407
  33.6 2.5 %collective-permute-done.7.far_ref = bf16[128,128]{1,0:T(8,128)(2,1)S(1)} collective-permute-done((bf16[128,128]{1,0:T(8,128)(2,1)S(1)}, bf16[128,128]{1,0:T(8,128)(2,1)S(1)}, u32[]{:S(2)}, u32[]{:S(2)}) %collective-permute-start.7) | collective-permute-done | bytes 32800 | tf_op jit(solution)/shard_map/ppermute | solution.py:407
  36.1 0.0 copy-start
  36.1 0.0 copy-start.1
  36.1 0.1 shard_map.109
  36.2 0.1 collective-permute-start.8
  36.2 0.0 collective-permute-done.10.theirs_ref
  36.3 0.1 shard_map.112
  36.4 0.3 collective-permute-start.11
  36.7 0.0 copy-done.2
  36.7 0.4 copy-done
  37.1 0.2 copy-done.1
  37.3 2.0 %shard_map.113 = (bf16[128,2048]{1,0:T(8,128)(2,1)S(1)}, bf16[128,2048]{1,0:T(8,128)(2,1)S(1)}, bf16[128,2048]{1,0:T(8,128)(2,1)S(1)}, f32[8,128]{1,0:T(8,128)S(1)}) custom-call(s32[1]{0:T(128)} %bitcast.me_ref, f32[1024,128]{1,0:T(8,128)S(1)} %get-tuple-element.85.y_ref, f32[1024,128]{1,0:T(8,128)S(1)} %get-tuple-element.86.z_ref, ...), custom_call_target="tpu_custom_call" | custom-call | flops 8388608 | bytes 1048576 | tf_op jit(solution)/shard_map/pallas_call | solution.py:534
  39.3 1.1 %collective-permute-done.11.theirs_ref = bf16[4,32,128]{2,1,0:T(8,128)(2,1)S(1)} collective-permute-done((bf16[4,32,128]{2,1,0:T(8,128)(2,1)S(1)}, bf16[4,32,128]{2,1,0:T(8,128)(2,1)S(1)}, u32[]{:S(2)}, u32[]{:S(2)}) %collective-permute-start.11) | collective-permute-done | bytes 32800 | tf_op jit(solution)/shard_map/ppermute | solution.py:407
  40.4 2.4 %collective-permute-start.12 = (bf16[4,16,128]{2,1,0:T(8,128)(2,1)S(1)}, bf16[4,16,128]{2,1,0:T(8,128)(2,1)S(1)}, u32[]{:S(2)}, u32[]{:S(2)}) collective-permute-start(bf16[4,16,128]{2,1,0:T(8,128)(2,1)S(1)} %get-tuple-element.104), channel_id=1, source_target_pairs={{0,16},{2,18},{4,20},{6,22},{8,24},{10,26},{12,28},{14,30},{16,0},... | collective-permute-start | bytes 49160 | tf_op jit(solution)/shard_map/ppermute | solution.py:407
  42.8 0.0 collective-permute-done.8.in_ref
  42.8 3.0 %shard_map.114 = (bf16[128,2048]{1,0:T(8,128)(2,1)S(1)}, bf16[128,2048]{1,0:T(8,128)(2,1)S(1)}, bf16[128,2048]{1,0:T(8,128)(2,1)S(1)}, bf16[128,2048]{1,0:T(8,12...) custom-call(s32[1]{0:T(128)} %bitcast.me_ref, ...), custom_call_target="tpu_custom_call", output_to_operand_aliasing={{0}: (10, {}), {1}: (11, {}), {2}: (12, {})} | custom-call | flops 8388608 | bytes 1048576 | tf_op jit(solution)/shard_map/pallas_call | solution.py:537
  45.8 0.0 collective-permute-done.12.theirs_ref
  45.8 0.6 %shard_map.116 = (f32[16,128]{1,0:T(8,128)}, f32[16,128]{1,0:T(8,128)}) custom-call(s32[1]{0:T(128)} %bitcast.me_ref, f32[4,16,128]{2,1,0:T(8,128)S(1)} %get-tuple-element.103.mine_ref, bf16[4,16,128]{2,1,0:T(8,128)(2,1)S(1)} %collective-permute-done.12.theirs_ref, f32[2,128,128]{2,1,0:T(8,128)S(1)} %get-tuple-element.105.sk_ref, ...), custom_call_target="tpu_custom_call" | custom-call | flops 128 | bytes 1048576 | tf_op jit(solution)/shard_map/pallas_call | solution.py:554
  (11 shorter events, 0.2 us)
Async XLA Ops:
  1.3 5.9 %collective-permute-start = (f32[2,16,128]{2,1,0:T(8,128)S(1)}, f32[2,16,128]{2,1,0:T(8,128)S(1)}, u32[]{:S(2)}, u32[]{:S(2)}) collective-permute-start(f32[2,16,128]{2,1,0:T(8,128)S(1)} %pad_maximum_fusion.4.own_ref), channel_id=1, source_target_pairs={{0,16},{2,18},{4,20},{6,22},{8,24},{10,26},{12,28},{14,30},{16,0},... | collective-permute-start | bytes 49160 | tf_op jit(solution)/shard_map/ppermute | solution.py:407
  7.3 4.0 %collective-permute-start.1 = (f32[2,2,16,128]{3,2,1,0:T(8,128)S(1)}, f32[2,2,16,128]{3,2,1,0:T(8,128)S(1)}, u32[]{:S(2)}, u32[]{:S(2)}) collective-permute-start(f32[2,2,16,128]{3,2,1,0:T(8,128)S(1)} %pad_maximum_fusion.3), channel_id=1, source_target_pairs={{0,8},{2,10},{4,12},{6,14},{8,0},{10,2},{12,4},{14,6},{16,24},{18,... | collective-permute-start | bytes 98312 | tf_op jit(solution)/shard_map/ppermute | solution.py:407
  11.3 4.3 %collective-permute-start.2 = (f32[2,2,2,16,128]{4,3,2,0,1:T(8,128)S(1)}, f32[2,2,2,16,128]{4,3,2,0,1:T(8,128)S(1)}, u32[]{:S(2)}, u32[]{:S(2)}) collective-permute-start(f32[2,2,2,16,128]{4,3,2,0,1:T(8,128)S(1)} %pad_maximum_fusion.2), channel_id=1, source_target_pairs={{0,4},{2,6},{4,0},{6,2},{8,12},{10,14},{12,8},{14,10},{16,20},{18,... | collective-permute-start | bytes 196616 | tf_op jit(solution)/shard_map/ppermute | solution.py:407
  15.7 1.4 %collective-permute-start.3 = (f32[2,2,2,2,16,128]{5,4,3,0,1,2:T(8,128)S(1)}, f32[2,2,2,2,16,128]{5,4,3,0,1,2:T(8,128)S(1)}, u32[]{:S(2)}, u32[]{:S(2)}) collective-permute-start(f32[2,2,2,2,16,128]{5,4,3,0,1,2:T(8,128)S(1)} %pad_maximum_fusion.1), channel_id=1, source_target_pairs={{0,2},{2,0},{4,6},{6,4},{8,10},{10,8},{12,14},{14,12},{16,18},{18,... | collective-permute-start | bytes 393224 | tf_op jit(solution)/shard_map/ppermute | solution.py:407
  18.4 1.4 %collective-permute-start.4 = (bf16[2,128,128]{2,1,0:T(8,128)(2,1)S(1)}, bf16[2,128,128]{2,1,0:T(8,128)(2,1)S(1)}, u32[]{:S(2)}, u32[]{:S(2)}) collective-permute-start(bf16[2,128,128]{2,1,0:T(8,128)(2,1)S(1)} %get-tuple-element.69), channel_id=1, source_target_pairs={{0,2},{2,0},{4,6},{6,4},{8,10},{10,8},{12,14},{14,12},{16,18},{18,... | collective-permute-start | bytes 196616 | tf_op jit(solution)/shard_map/ppermute | solution.py:407
  19.9 4.5 %collective-permute-start.5 = (bf16[2,128,128]{2,1,0:T(8,128)(2,1)S(1)}, bf16[2,128,128]{2,1,0:T(8,128)(2,1)S(1)}, u32[]{:S(2)}, u32[]{:S(2)}) collective-permute-start(bf16[2,128,128]{2,1,0:T(8,128)(2,1)S(1)} %get-tuple-element.71), channel_id=1, source_target_pairs={{0,4},{2,6},{4,0},{6,2},{8,12},{10,14},{12,8},{14,10},{16,20},{18,... | collective-permute-start | bytes 196616 | tf_op jit(solution)/shard_map/ppermute | solution.py:407
  24.5 4.6 %collective-permute-start.9 = (bf16[4,128,128]{2,1,0:T(8,128)(2,1)S(1)}, bf16[4,128,128]{2,1,0:T(8,128)(2,1)S(1)}, u32[]{:S(2)}, u32[]{:S(2)}) collective-permute-start(bf16[4,128,128]{2,1,0:T(8,128)(2,1)S(1)} %convert_element_type.3), channel_id=1, source_target_pairs={{0,2},{2,0},{4,6},{6,4},{8,10},{10,8},{12,14},{14,12},{16,18},{18,... | collective-permute-start | bytes 393224 | tf_op jit(solution)/shard_map/ppermute | solution.py:407
  24.7 6.1 %collective-permute-start.6 = (bf16[2,128,128]{2,1,0:T(8,128)(2,1)S(1)}, bf16[2,128,128]{2,1,0:T(8,128)(2,1)S(1)}, u32[]{:S(2)}, u32[]{:S(2)}) collective-permute-start(bf16[2,128,128]{2,1,0:T(8,128)(2,1)S(1)} %get-tuple-element.78), channel_id=1, source_target_pairs={{0,8},{2,10},{4,12},{6,14},{8,0},{10,2},{12,4},{14,6},{16,24},{18,... | collective-permute-start | bytes 196616 | tf_op jit(solution)/shard_map/ppermute | solution.py:407
  29.2 7.0 %collective-permute-start.10 = (bf16[4,64,128]{2,1,0:T(8,128)(2,1)S(1)}, bf16[4,64,128]{2,1,0:T(8,128)(2,1)S(1)}, u32[]{:S(2)}, u32[]{:S(2)}) collective-permute-start(bf16[4,64,128]{2,1,0:T(8,128)(2,1)S(1)} %get-tuple-element.90), channel_id=1, source_target_pairs={{0,4},{2,6},{4,0},{6,2},{8,12},{10,14},{12,8},{14,10},{16,20},{18,... | collective-permute-start | bytes 196616 | tf_op jit(solution)/shard_map/ppermute | solution.py:407
  30.8 5.9 %copy-start.2 = (bf16[128,2048]{1,0:T(8,128)(2,1)S(1)}, bf16[128,2048]{1,0:T(8,128)(2,1)}, u32[]{:S(2)}) copy-start(bf16[128,2048]{1,0:T(8,128)(2,1)} %u_ref.3) | copy-start | bytes 1572868
  30.9 5.2 %collective-permute-start.7 = (bf16[128,128]{1,0:T(8,128)(2,1)S(1)}, bf16[128,128]{1,0:T(8,128)(2,1)S(1)}, u32[]{:S(2)}, u32[]{:S(2)}) collective-permute-start(bf16[128,128]{1,0:T(8,128)(2,1)S(1)} %get-tuple-element.81), channel_id=1, source_target_pairs={{0,16},{2,18},{4,20},{6,22},{8,24},{10,26},{12,28},{14,30},{16,0},... | collective-permute-start | bytes 98312 | tf_op jit(solution)/shard_map/ppermute | solution.py:407
  36.1 1.0 %copy-start = (bf16[128,2048]{1,0:T(8,128)(2,1)S(1)}, bf16[128,2048]{1,0:T(8,128)(2,1)}, u32[]{:S(2)}) copy-start(bf16[128,2048]{1,0:T(8,128)(2,1)} %k_ref.3) | copy-start | bytes 1572868
  36.1 1.2 %copy-start.1 = (bf16[128,2048]{1,0:T(8,128)(2,1)S(1)}, bf16[128,2048]{1,0:T(8,128)(2,1)}, u32[]{:S(2)}) copy-start(bf16[128,2048]{1,0:T(8,128)(2,1)} %v_ref.3) | copy-start | bytes 1572868
  36.2 6.6 %collective-permute-start.8 = (bf16[2,128,128]{2,1,0:T(8,128)(2,1)S(1)}, bf16[2,128,128]{2,1,0:T(8,128)(2,1)S(1)}, u32[]{:S(2)}, u32[]{:S(2)}) collective-permute-start(bf16[2,128,128]{2,1,0:T(8,128)(2,1)S(1)} %get-tuple-element.82), channel_id=1, source_target_pairs={{0,2},{2,0},{4,6},{6,4},{8,10},{10,8},{12,14},{14,12},{16,18},{18,... | collective-permute-start | bytes 196616 | tf_op jit(solution)/shard_map/ppermute | solution.py:407
  36.4 4.0 %collective-permute-start.11 = (bf16[4,32,128]{2,1,0:T(8,128)(2,1)S(1)}, bf16[4,32,128]{2,1,0:T(8,128)(2,1)S(1)}, u32[]{:S(2)}, u32[]{:S(2)}) collective-permute-start(bf16[4,32,128]{2,1,0:T(8,128)(2,1)S(1)} %get-tuple-element.101), channel_id=1, source_target_pairs={{0,8},{2,10},{4,12},{6,14},{8,0},{10,2},{12,4},{14,6},{16,24},{18,... | collective-permute-start | bytes 98312 | tf_op jit(solution)/shard_map/ppermute | solution.py:407
  40.4 5.4 %collective-permute-start.12 = (bf16[4,16,128]{2,1,0:T(8,128)(2,1)S(1)}, bf16[4,16,128]{2,1,0:T(8,128)(2,1)S(1)}, u32[]{:S(2)}, u32[]{:S(2)}) collective-permute-start(bf16[4,16,128]{2,1,0:T(8,128)(2,1)S(1)} %get-tuple-element.104), channel_id=1, source_target_pairs={{0,16},{2,18},{4,20},{6,22},{8,24},{10,26},{12,28},{14,30},{16,0},... | collective-permute-start | bytes 49160 | tf_op jit(solution)/shard_map/ppermute | solution.py:407

commit v3 on v0

v3 whole, which is shorter than its diff:
```python
import functools

import jax
import jax.numpy as jnp
from jax import lax
from jax.experimental import pallas as pl
from jax.experimental.pallas import tpu as pltpu
from jax.sharding import PartitionSpec as P

LANES = 128
SETS = 2
STRETCH = 8
F32 = jnp.float32
BF16 = jnp.bfloat16
VMEM = pl.BlockSpec(memory_space=pltpu.VMEM)
SMEM = pl.BlockSpec(memory_space=pltpu.SMEM)
ANY = pl.BlockSpec(memory_space=pl.ANY)
HBM = pl.BlockSpec(memory_space=pltpu.HBM)


def total(terms):
    terms = list(terms)
    while len(terms) > 1:
        terms = [a + b for a, b in zip(terms[::2], terms[1::2])] + terms[len(terms) & ~1 :]
    return terms[0]


def set_columns(member, which):
    return pl.ds(pl.multiple_of((member * SETS + which) * LANES, LANES), LANES)


def gate_kernel(me_ref, q_hbm, k_hbm, v_hbm, u_hbm, own_ref, send_ref, stage_ref, sems, *, members, pieces):
    tokens = q_hbm.shape[0]
    core = me_ref[0] % SETS
    rows = tokens // pieces
    copies = []
    for piece in range(pieces):
        at = pl.ds(piece * rows, rows)
        for i, ref in enumerate((q_hbm, k_hbm, v_hbm, u_hbm)):
            copies.append(pltpu.make_async_copy(ref.at[at], stage_ref.at[i, at], sems.at[piece, i]))
            copies[-1].start()

    def body(tile, _):
        at = pl.ds(pl.multiple_of(tile * 16, 16), 16)
        for out_ref, which in ((own_ref, core), (send_ref, 1 - core)):
            for member in range(members):
                cols = set_columns(member, which)
                q, k, v, u = (stage_ref[i, at, cols].astype(F32) for i in range(4))
                out_ref[0, member, at, :] = (k * v).astype(BF16)
                out_ref[1, member, at, :] = (u * q).astype(BF16)
        return 0

    for piece in range(pieces):
        for copy in copies[piece * 4 : piece * 4 + 4]:
            copy.wait()
        lax.fori_loop(piece * rows // 16, (piece + 1) * rows // 16, body, 0)


def series_kernel(me_ref, own_ref, got_ref, x_ref, g_ref, lag_ref, *, tokens, members):
    core = me_ref[0] % SETS
    for ref, chunk in ((own_ref, core), (got_ref, 1 - core)):

        def body(tile, _):
            rows = pl.ds(pl.multiple_of(tile * 16, 16), 16)
            for member in range(members):
                for i, out_ref in enumerate((x_ref, g_ref)):
                    value = ref[i, member, rows, :].astype(F32)
                    for half in range(2):
                        start = (chunk * tokens + tile * 16 + half * 8) * members + member
                        out_ref[pl.ds(start, 8, stride=members), :] = value[half * 8 : half * 8 + 8]
            return 0

        lax.fori_loop(0, tokens // 16, body, 0)

    def step(i, lags):
        x = [x_ref[pl.ds((i * STRETCH + t) * members, members), :] for t in range(STRETCH)]
        g = [g_ref[pl.ds((i * STRETCH + t) * members, members), :] for t in range(STRETCH)]
        return tuple(lags[j] + total([g[t] * x[t - j] for t in range(j, STRETCH)]) for j in range(STRETCH))

    zero = tuple(jnp.zeros((members, LANES), F32) for _ in range(STRETCH))
    lags = lax.fori_loop(0, SETS * tokens // STRETCH, step, zero)
    for j in range(STRETCH):
        lag_ref[j] = lags[j]


def param_rows(par_ref, param, mode, modes, members):
    return par_ref[pl.ds(param * modes + mode, members, stride=2 * modes), :]


def rate_block(par_ref, member, modes):
    return par_ref[pl.ds(pl.multiple_of(member * 2 * modes, modes), modes), :]


def state_kernel(x_ref, g_ref, par_ref, sk_ref, hs_ref, ks_ref, xw_ref, gw_ref, *, length, modes, members):
    w = [jnp.exp(-param_rows(par_ref, 0, m, modes, members)) for m in range(modes)]
    stretches = length // STRETCH

    def step(i, carry):
        s, k = carry
        back = stretches - 1 - i
        for m in range(modes):
            hs_ref[i, m] = s[m]
        for t in range(STRETCH):
            at = pl.ds((i * STRETCH + t) * members, members)
            at_back = pl.ds((back * STRETCH + STRETCH - 1 - t) * members, members)
            x, g = x_ref[at, :], g_ref[at_back, :]
            xw_ref[at, :] = x * float(STRETCH - 1 - t)
            gw_ref[at_back, :] = g * float(STRETCH - 1 - t)
            s = tuple(w[m] * s[m] + x for m in range(modes))
            k = tuple(w[m] * k[m] + g for m in range(modes))
        for m in range(modes):
            ks_ref[back, m] = k[m]
        return s, k

    zero = tuple(jnp.zeros((members, LANES), F32) for _ in range(modes))
    for m in range(modes):
        ks_ref[stretches, m] = zero[m]
    s, k = lax.fori_loop(0, stretches, step, (zero, zero), unroll=2)
    for m in range(modes):
        at = pl.ds(m, members, stride=modes)
        sk_ref[0, at, :] = s[m]
        sk_ref[1, at, :] = k[m]


def taps_kernel(x_ref, g_ref, par_ref, y_ref, z_ref, *, length, modes, members):
    rate = [param_rows(par_ref, 0, m, modes, members) for m in range(modes)]
    w = [jnp.exp(-rate[m]) for m in range(modes)]
    power = [param_rows(par_ref, 1, m, modes, members) * jnp.sqrt(rate[m]) for m in range(modes)]
    taps = []
    for j in range(STRETCH):
        taps.append(total(power))
        power = [power[m] * w[m] for m in range(modes)]

    def within(i, _):
        at = [pl.ds((i * STRETCH + t) * members, members) for t in range(STRETCH)]
        x = [x_ref[at[t], :] for t in range(STRETCH)]
        g = [g_ref[at[t], :] for t in range(STRETCH)]
        for t in range(STRETCH):
            y_ref[at[t], :] = total([taps[j] * x[t - j] for j in range(t + 1)])
            z_ref[at[t], :] = total([taps[j] * g[t + j] for j in range(STRETCH - t)])
        return 0

    lax.fori_loop(0, length // STRETCH, within, 0, unroll=2)


def flags(bit):
    bit = bit.astype(F32)
    return bit, 1.0 - bit


def put_states(ref, me, span, member, s, k, modes, members, last):
    at = pl.ds(member * modes, modes)
    if last:
        earlier, later = flags((me // span) % 2 == 1)
        ref[at, :] = (earlier * k + later * s).astype(BF16)
    else:
        ref[at, :] = s.astype(BF16)
        ref[pl.ds((members + member) * modes, modes), :] = k.astype(BF16)


def sums_kernel(
    me_ref, x_ref, g_ref, lag_ref, hs_ref, ks_ref, sk_ref, par_ref, sums_ref, message_ref, *kept,
    length, modes, members, part, unroll, last, tree,
):
    stretches = length // STRETCH
    width = float(STRETCH)
    zero = jnp.zeros((members, LANES), F32)
    for first in range(0, modes, part):
        rate = [param_rows(par_ref, 0, first + m, modes, members) for m in range(part)]
        w = [jnp.exp(-rate[m]) for m in range(part)]
        fade = [jnp.exp(rate[m] * -width) for m in range(part)]

        def step(i, carry):
            back = stretches - 1 - i
            x = [x_ref[pl.ds((i * STRETCH + t) * members, members), :] for t in range(STRETCH - 1)]
            g = [g_ref[pl.ds((back * STRETCH + t) * members, members), :] for t in range(STRETCH)]
            out = []
            for m in range(part):
                same, next_, b_k, b_s, sd, kd = carry[m]
                h, k = hs_ref[i, first + m], ks_ref[i, first + m]
                h_back = hs_ref[back, first + m]
                k_after, k_back = ks_ref[i + 1, first + m], ks_ref[back + 1, first + m]
                s_own = x[0]
                for t in range(1, STRETCH - 1):
                    s_own = s_own * w[m] + x[t]
                s_own = s_own * w[m]
                k_own = g[STRETCH - 1]
                for t in range(STRETCH - 2, 0, -1):
                    k_own = k_own * w[m] + g[t]
                k_own = k_own * w[m]
                out.append(
                    (
                        same + h * k,
                        next_ + h * k_after,
                        b_k + h_back * k_own,
                        b_s + k_after * s_own,
                        fade[m] * (sd + width * h) + s_own,
                        fade[m] * (kd + width * k_back) + k_own,
                    )
                )
            return tuple(out)

        sums = lax.fori_loop(0, stretches, step, ((zero,) * 6,) * part, unroll=unroll)
        for m in range(part):
            same, next_, b_k, b_s, sd, kd = sums[m]
            r, d = lag_ref[STRETCH - 1], (width - 1.0) * lag_ref[STRETCH - 1]
            for j in range(STRETCH - 2, -1, -1):
                r = r * w[m] + lag_ref[j]
                d = d * w[m] + float(j) * lag_ref[j]
            at = pl.ds(first + m, members, stride=modes)
            sums_ref[0, at, :] = r + w[m] * (same - fade[m] * next_)
            sums_ref[1, at, :] = d + w[m] * (b_k + b_s + same + (width - 1.0) * (fade[m] * next_))
            sums_ref[2, at, :] = sd
            sums_ref[3, at, :] = kd

    me = me_ref[0]
    for member in range(members):
        at = pl.ds(member * modes, modes)
        put_states(message_ref, me, SETS, member, sk_ref[0, at, :], sk_ref[1, at, :], modes, members, last)
    if tree:
        side = (me // SETS) % 2
        offset = members * modes * (1 if last else 2)
        for to in range(members // 2):
            for i in range(4):
                index = pl.ds(pl.multiple_of((to * 2 + side) * modes, modes), modes)
                kept[0][i, pl.ds(to * modes, modes), :] = sums_ref[i, index, :]
                index = pl.ds(pl.multiple_of((to * 2 + 1 - side) * modes, modes), modes)
                message_ref[pl.ds(offset + (i * (members // 2) + to) * modes, modes), :] = sums_ref[i, index, :].astype(BF16)


def join(rate, left, right, length):
    r_a, d_a, sd_a, kd_a, s_a, k_a = left
    r_b, d_b, sd_b, kd_b, s_b, k_b = right
    w = jnp.exp(-rate)
    fade = jnp.exp(rate * -length)
    r = r_a + r_b + w * (s_a * k_b)
    d = d_a + d_b + w * (s_a * kd_b + (sd_a + s_a) * k_b)
    sd = fade * (sd_a + length * s_a) + sd_b
    kd = kd_a + fade * (kd_b + length * k_b)
    return r, d, sd, kd


def level_kernel(
    me_ref, tot_ref, got_ref, enter_ref, par_ref, *refs, tokens, modes, members, span, last, tree
):
    if tree:
        kept_ref, out_ref, new_ref, message_ref, keep_ref = refs
    else:
        out_ref, new_ref, message_ref = refs
    me = me_ref[0]
    second = (me // span) % 2
    earlier, later = flags(second == 1)
    inside = (me // 2) % (span // 2) * 2
    gap = earlier * inside.astype(F32) + later * (span - 2 - inside).astype(F32)
    rows = members * modes
    for member in range(members):
        at = pl.ds(member * modes, modes)
        rate = rate_block(par_ref, member, modes)
        far = jnp.exp(rate * -float(tokens * span))
        weight = jnp.exp(rate * (gap * -float(tokens)))
        s, k = tot_ref[0, at, :], tot_ref[1, at, :]
        gs, gk = got_ref[at, :].astype(F32), got_ref[pl.ds(rows + member * modes, modes), :].astype(F32)
        s_sum = earlier * (far * gs + s) + later * (far * s + gs)
        k_sum = earlier * (gk + far * k) + later * (k + far * gk)
        out_ref[0, at, :] = s_sum
        out_ref[1, at, :] = k_sum
        before = earlier * (weight * gs)
        after = later * (weight * gk)
        if span > 2:
            before += enter_ref[0, at, :]
            after += enter_ref[1, at, :]
        new_ref[0, at, :] = before
        new_ref[1, at, :] = after
        put_states(message_ref, me, span * 2, member, s_sum, k_sum, modes, members, last)
    if not tree:
        return
    side = (me // (span * 2)) % 2
    own = (me // 2) % span
    count = members // span
    offset = rows * (1 if last else 2)
    for parity in (0, 1):
        for to in range(count // 2):
            index = to * 2 + (side if parity == 0 else 1 - side)
            member = index * span + own
            src = pl.ds(pl.multiple_of(index * modes, modes), modes)
            at = pl.ds(pl.multiple_of(member * modes, modes), modes)
            at_k = pl.ds(pl.multiple_of((members + member) * modes, modes), modes)
            mine = tuple(kept_ref[i, src, :] for i in range(4)) + (tot_ref[0, at, :], tot_ref[1, at, :])
            theirs = tuple(
                got_ref[pl.ds(pl.multiple_of(rows * 2 + (i * count + index) * modes, modes), modes), :].astype(F32) for i in range(4)
            ) + (got_ref[at, :].astype(F32), got_ref[at_k, :].astype(F32))
            left = tuple(earlier * b + later * a for a, b in zip(mine, theirs))
            right = tuple(earlier * a + later * b for a, b in zip(mine, theirs))
            for i, value in enumerate(join(rate_block(par_ref, member, modes), left, right, float(tokens * span))):
                if parity == 0:
                    keep_ref[i, pl.ds(to * modes, modes), :] = value
                else:
                    message_ref[pl.ds(offset + (i * (count // 2) + to) * modes, modes), :] = value.astype(BF16)


def enter_kernel(me_ref, enter_ref, far_ref, par_ref, in_ref, *, tokens, modes, members, span):
    me = me_ref[0]
    earlier, later = flags((me // span) % 2 == 1)
    inside = (me // 2) % (span // 2) * 2
    gap = earlier * inside.astype(F32) + later * (span - 2 - inside).astype(F32)
    for member in range(members):
        at = pl.ds(member * modes, modes)
        value = jnp.exp(rate_block(par_ref, member, modes) * (gap * -float(tokens))) * far_ref[at, :].astype(F32)
        before, after = earlier * value, later * value
        if span > 2:
            before += enter_ref[0, at, :]
            after += enter_ref[1, at, :]
        in_ref[0, at, :] = before
        in_ref[1, at, :] = after


def finish_kernel(me_ref, y_ref, z_ref, hs_ref, ks_ref, par_ref, in_ref, *refs, tokens, modes, members, own):
    if own:
        k_ref, v_ref, u_ref, dq_ref, dk_ref, dv_ref, yo_ref, zo_ref = refs
    else:
        send_ref, yo_ref, zo_ref = refs
    core = me_ref[0] % SETS
    chunk = core if own else 1 - core
    second, first = flags(chunk == 1)
    stretches = tokens // STRETCH
    base = chunk * stretches
    rate = [param_rows(par_ref, 0, m, modes, members) for m in range(modes)]
    w = [jnp.exp(-rate[m]) for m in range(modes)]
    fade = [jnp.exp(rate[m] * -float(STRETCH)) for m in range(modes)]
    amp = [param_rows(par_ref, 1, m, modes, members) * jnp.sqrt(rate[m]) * w[m] for m in range(modes)]
    h = tuple(
        in_ref[0, pl.ds(m, members, stride=modes), :] * jnp.exp(rate[m] * (second * -float(tokens))) for m in range(modes)
    )
    k = tuple(
        in_ref[1, pl.ds(m, members, stride=modes), :] * jnp.exp(rate[m] * (first * -float(tokens))) for m in range(modes)
    )

    def forward(i, h):
        p = [amp[m] * (h[m] + hs_ref[base + i, m]) for m in range(modes)]
        for t in range(STRETCH):
            at = pl.ds((i * STRETCH + t) * members, members)
            yo_ref[at, :] = y_ref[pl.ds(((base + i) * STRETCH + t) * members, members), :] + total(p)
            if t < STRETCH - 1:
                p = [w[m] * p[m] for m in range(modes)]
        return tuple(fade[m] * h[m] for m in range(modes))

    def backward(i, k):
        back = stretches - 1 - i
        q = [amp[m] * (k[m] + ks_ref[base + back + 1, m]) for m in range(modes)]
        for t in range(STRETCH):
            row = back * STRETCH + STRETCH - 1 - t
            zo_ref[pl.ds(row * members, members), :] = z_ref[pl.ds((base * STRETCH + row) * members, members), :] + total(q)
            if t < STRETCH - 1:
                q = [w[m] * q[m] for m in range(modes)]
        return tuple(fade[m] * k[m] for m in range(modes))

    def put(source, store):
        for tile in range(tokens // 16):
            rows = pl.ds(tile * 16, 16)
            for member in range(members):
                halves = [pl.ds((tile * 16 + half * 8) * members + member, 8, stride=members) for half in range(2)]
                store(rows, member, jnp.concatenate([source[at, :] for at in halves], axis=0).astype(BF16))

    def store_y(rows, member, value):
        if own:
            cols = set_columns(member, core)
            dq_ref[rows, cols] = (u_ref[rows, cols].astype(F32) * value.astype(F32)).astype(BF16)
        else:
            send_ref[0, member, rows, :] = value

    def store_z(rows, member, value):
        if own:
            cols = set_columns(member, core)
            value = value.astype(F32)
            dk_ref[rows, cols] = (value * v_ref[rows, cols].astype(F32)).astype(BF16)
            dv_ref[rows, cols] = (value * k_ref[rows, cols].astype(F32)).astype(BF16)
        else:
            send_ref[1, member, rows, :] = value

    lax.fori_loop(0, stretches, forward, h)
    put(yo_ref, store_y)
    lax.fori_loop(0, stretches, backward, k)
    put(zo_ref, store_z)


def last_kernel(me_ref, got_ref, k_ref, v_ref, u_ref, *refs, tokens, modes, members, span, scale, tree):
    refs = list(refs)
    if tree:
        kept_ref, far_ref, tot_ref, own_ref = refs[:4]
        refs = refs[4:]
    dq_ref, dk_ref, dv_ref, dq_hbm, dk_hbm, dv_hbm = refs[3:9]
    me = me_ref[0]
    core = me % SETS
    copies = []
    if tree:
        r_hbm, log_hbm, sems, par_sems, out_ref = refs[9:]
        earlier, later = flags((me // span) % 2 == 1)
        at = pl.ds(pl.multiple_of(me // 2 * modes, modes), modes)
        rows = members * modes
        r_m, d_m, sd_m, kd_m = (kept_ref[i] for i in range(4))
        r_t, d_t, sd_t, kd_t = (far_ref[pl.ds(rows + i * modes, modes), :].astype(F32) for i in range(4))
        far = far_ref[at, :].astype(F32)
        s_a = earlier * far + later * tot_ref[0, at, :]
        k_b = earlier * tot_ref[1, at, :] + later * far
        sd_a = earlier * sd_t + later * sd_m
        kd_b = earlier * kd_m + later * kd_t
        rate, residue = own_ref[0], own_ref[1]
        w = jnp.exp(-rate)
        r = r_m + r_t + w * (s_a * k_b)
        d = d_m + d_t + w * (s_a * kd_b + (sd_a + s_a) * k_b)
        root = jnp.sqrt(rate) * scale
        out_ref[0] = root * r
        out_ref[1] = root * residue * (0.5 * r - rate * d)
        for i, ref in enumerate((r_hbm, log_hbm)):
            copies.append(pltpu.make_async_copy(out_ref.at[i], ref, par_sems.at[i]))
            copies[-1].start()
    else:
        (sems,) = refs[9:]
    for tile in range(tokens // 16):
        rows = pl.ds(tile * 16, 16)
        for member in range(members):
            cols = set_columns(member, 1 - core)
            y = got_ref[0, member, rows, :].astype(F32)
            z = got_ref[1, member, rows, :].astype(F32)
            dq_ref[rows, cols] = (u_ref[rows, cols].astype(F32) * y).astype(BF16)
            dk_ref[rows, cols] = (z * v_ref[rows, cols].astype(F32)).astype(BF16)
            dv_ref[rows, cols] = (z * k_ref[rows, cols].astype(F32)).astype(BF16)
        for i, (ref, out) in enumerate(((dq_ref, dq_hbm), (dk_ref, dk_hbm), (dv_ref, dv_hbm))):
            copies.append(pltpu.make_async_copy(ref.at[rows], out.at[rows], sems.at[i, tile]))
            copies[-1].start()
    for copy in copies:
        copy.wait()


def call(body, out_shape, in_specs, flops, out_specs=None, scratch=(), aliases=None):
    return pl.pallas_call(
        body,
        out_shape=out_shape,
        in_specs=in_specs,
        out_specs=jax.tree.map(lambda _: VMEM, out_shape) if out_specs is None else out_specs,
        scratch_shapes=scratch,
        input_output_aliases=aliases or {},
        compiler_params=pltpu.CompilerParams(vmem_limit_bytes=16 * 1024 * 1024),
        cost_estimate=pl.CostEstimate(flops=flops, bytes_accessed=1024 * 1024, transcendentals=0),
    )


def exchange(value, distance, count):
    return lax.ppermute(value, "ctx", [(i, i ^ distance) for i in range(count)])


def tie(*values):
    return lax.optimization_barrier(values)


def local(query_proj, key_proj, value_proj, output_grad, residue, decay_rate):
    tokens, channels = query_proj.shape
    own_channels, modes = residue.shape
    count = lax.axis_size("ctx")
    groups = channels // LANES
    members = groups // SETS
    rows = members * modes
    length = tokens * SETS
    top = count // 2
    tree = groups == count and own_channels == LANES and top > SETS
    work = tokens * channels * modes
    index = lax.axis_index("ctx")
    core = index % SETS
    me = index.astype(jnp.int32).reshape(1)

    def shape(*dims, dtype=F32):
        return jax.ShapeDtypeStruct(dims, dtype)

    half = shape(2, members, tokens, LANES, dtype=BF16)
    series = shape(length * members, LANES)
    pieces = 4
    own_gates, send_gates = call(
        functools.partial(gate_kernel, members=members, pieces=pieces),
        (half, half),
        [SMEM] + [HBM] * 4,
        work,
        scratch=(pltpu.VMEM((4, tokens, channels), BF16), pltpu.SemaphoreType.DMA((pieces, 4))),
    )(me, *(pltpu.with_memory_space_constraint(a, pltpu.HBM) for a in (query_proj, key_proj, value_proj, output_grad)))

    (own,) = tie(jnp.stack([decay_rate.T, residue.T]))
    params, axis = own, 0
    distance = count // 2
    while distance > (1 if tree else 0):
        other = exchange(params, distance, count)
        if axis == 0:
            other, own_gates, send_gates = tie(other, own_gates, send_gates)
            got_gates = exchange(send_gates, 1, count)
            gated, gate_grad, lags = call(
                functools.partial(series_kernel, tokens=tokens, members=members),
                (series, series, shape(STRETCH, members, LANES)),
                [SMEM] + [VMEM] * 2,
                work,
            )(me, own_gates, got_gates)
        if axis == 2:
            other, gated, gate_grad, lags = tie(other, gated, gate_grad, lags)
        upper = (index // distance) % 2 == 1
        params = jnp.stack([jnp.where(upper, other, params), jnp.where(upper, params, other)], axis=axis)
        distance //= 2
        axis += 1
    if tree:
        params = params.reshape((members,) + own.shape)
    else:
        params = params.reshape((count,) + own.shape).transpose(1, 2, 0, 3).reshape(2, modes, members, SETS, LANES)
        params = lax.dynamic_index_in_dim(params, core, 3, keepdims=False).transpose(2, 0, 1, 3)
    par = params.reshape(members * 2 * modes, LANES)

    stretches = length // STRETCH
    pair = shape(2, rows, LANES)
    sk, hs, ks, x_weighted, g_weighted = call(
        functools.partial(state_kernel, length=length, modes=modes, members=members),
        (pair, shape(stretches, modes, members, LANES), shape(stretches + 1, modes, members, LANES), series, series),
        [VMEM] * 3,
        work * 4,
    )(gated, gate_grad, par)

    def message_shape(span):
        return shape(rows * (1 if span == top else 2) + (4 * rows // span if tree else 0), LANES, dtype=BF16)

    sums, message, *kept = call(
        functools.partial(
            sums_kernel, length=length, modes=modes, members=members, part=min(4, modes), unroll=4, last=top == SETS, tree=tree
        ),
        (shape(4, rows, LANES), message_shape(SETS)) + ((shape(4, rows // 2, LANES),) if tree else ()),
        [SMEM] + [VMEM] * 7,
        work * 6,
    )(me, x_weighted, g_weighted, lags, hs, ks, sk, par)

    tot, enter, span = sk, sk, SETS
    while span < top:
        got = exchange(message, span, count)
        last = span * 2 == top
        tot, enter, message, *kept = call(
            functools.partial(level_kernel, tokens=tokens, modes=modes, members=members, span=span, last=last, tree=tree),
            (pair, pair, message_shape(span * 2)) + ((shape(4, rows // span // 2, LANES),) if tree else ()),
            [SMEM] + [VMEM] * (5 if tree else 4),
            rows,
        )(me, tot, got, enter, par, *kept)
        if span == SETS:
            tot, gated, gate_grad = tie(tot, gated, gate_grad)
        span *= 2
    far = exchange(message, top, count)
    y, z = call(
        functools.partial(taps_kernel, length=length, modes=modes, members=members), (series, series), [VMEM] * 3, work
    )(gated, gate_grad, par)
    (states_in,) = call(
        functools.partial(enter_kernel, tokens=tokens, modes=modes, members=members, span=top), (pair,), [SMEM] + [VMEM] * 3, rows
    )(me, enter, far, par)

    scratch = (pltpu.VMEM((tokens * members, LANES), F32),) * 2
    finish = functools.partial(finish_kernel, tokens=tokens, modes=modes, members=members)
    (send_conv,) = call(functools.partial(finish, own=False), (half,), [SMEM] + [VMEM] * 6, work * 2, scratch=scratch)(
        me, y, z, hs, ks, par, states_in
    )
    got_conv = exchange(send_conv, 1, count)
    grads = (shape(tokens, channels, dtype=BF16),) * 3
    done = call(functools.partial(finish, own=True), grads, [SMEM] + [VMEM] * 9, work * 2, scratch=scratch)(
        me, y, z, hs, ks, par, states_in, key_proj, value_proj, output_grad
    )
    scale = float(tokens * count) ** (-0.5)
    extra = (*kept, far, tot, own) if tree else ()
    first = 5 + len(extra)
    out = call(
        functools.partial(last_kernel, tokens=tokens, modes=modes, members=members, span=top, scale=scale, tree=tree),
        grads + grads + ((shape(modes, LANES),) * 2 if tree else ()),
        [SMEM] + [VMEM] * (first + 2),
        work,
        (VMEM,) * 3 + (ANY,) * (5 if tree else 3),
        (pltpu.SemaphoreType.DMA((3, tokens // 16)),)
        + ((pltpu.SemaphoreType.DMA((2,)), pltpu.VMEM((2, modes, LANES), F32)) if tree else ()),
        {first: 0, first + 1: 1, first + 2: 2},
    )(me, got_conv, key_proj, value_proj, output_grad, *extra, *done)

    if tree:
        residue_grad, log_grad = out[6].T, out[7].T
    else:
        dims = (members, modes, LANES)
        h_in, k_in = (a.reshape(dims) for a in states_in)
        s, k = (a.reshape(dims) for a in sk)
        r, d, s_d, k_d = (a.reshape(dims) for a in sums)
        rate = params[:, 0]
        w = jnp.exp(-rate)
        r = r + w * h_in * k
        d = d + w * (h_in * k_d + k_in * (s_d + s)) + float(length) * jnp.exp(-rate * float(length + 1)) * h_in * k_in
        parts = jnp.stack([r, d], axis=1)
        parts = jnp.stack([jnp.where(core == 0, parts, 0.0), jnp.where(core == 1, parts, 0.0)], axis=1)
        parts = parts.reshape(groups, 2, modes, LANES).transpose(1, 2, 0, 3)
        parts = parts.reshape(2, modes, count, own_channels).transpose(2, 0, 1, 3)
        sums = lax.all_to_all(parts, "ctx", split_axis=0, concat_axis=0, tiled=True).sum(axis=0)
        root = scale * jnp.sqrt(decay_rate)
        residue_grad = root * sums[0].T
        log_grad = root * residue * (0.5 * sums[0].T - decay_rate * sums[1].T)
    return out[3], out[4], out[5], residue_grad, log_grad


def solution(mesh):
    in_specs = (P("ctx", "ch"),) * 4 + (P(("ch", "ctx"), None),) * 2
    out_specs = (P("ctx", "ch"),) * 3 + (P(("ch", "ctx"), None),) * 2
    return jax.shard_map(local, mesh=mesh, in_specs=in_specs, out_specs=out_specs, check_vma=False)
```

time: 278 us -> 43.7 us (0.16); the launches traced: 273 us -> 43.3 us
  matrix products: 149 us -> 0 us
  waiting for transfers between devices: 51.6 us -> 12.8 us
  starting transfers between devices: 34.9 us -> 13.3 us
  local copies, waits for them, and re-layouts: 18.8 us -> 0.03 us
  Pallas kernels: 0 us -> 15.6 us
  other arithmetic: 15.5 us -> 0.77 us
    dot_general x36 -> x0, matrix products: 149 us -> none  [the longest x24 78.1 us: inner_product(): return jnp.einsum('ckb,bj->ckj', spectrum, table, precision=HIGHEST)]
    all_to_all x7 -> x0, waiting for transfers between devices: 51.6 us -> none  [the longest x1 13.4 us: local(): lax.all_to_all(to_channels(query_proj), 'ctx', split_axis=0, concat_axis=...]
    all_to_all x7 -> x0, starting transfers between devices: 34.9 us -> none  [the longest x1 7.52 us: local(): lax.all_to_all(to_channels(query_proj), 'ctx', split_axis=0, concat_axis=...]
    pallas_call x0 -> x11, Pallas kernels: none -> 15.6 us  [the longest x1 4.17 us: local(): call(functools.partial(sums_kernel, length=length, modes=modes, members=m...]
    ppermute x0 -> x8, starting transfers between devices: none -> 13.3 us  [exchange(): return lax.ppermute(value, 'ctx', [(i, i ^ distance) for i in range(count)])]
    ppermute x0 -> x8, waiting for transfers between devices: none -> 12.8 us  [exchange(): return lax.ppermute(value, 'ctx', [(i, i ^ distance) for i in range(count)])]
    unnamed x219 -> x6, local copies, waits for them, and re-layouts: 10.9 us -> 0.02 us
    convert_element_type x6 -> x0, local copies, waits for them, and re-layouts: 7.67 us -> none  [the longest x2 4.12 us: times_bf16(): left.astype(jnp.float32) * right.astype(jnp.float32)]
  transfers between devices with their start and end apart: 7 -> 8, of which waited for: 6 -> 5; matrix products, arithmetic and copies ran while one was open for 26% -> 0% of each run, Pallas kernels for 0% -> 13%
where the time goes in v3:
time: 43.7 us; the launch traced here: 43.3 us
  Pallas kernels  15.6 us (36%)
  starting transfers between devices  13.3 us (30%)
  waiting for transfers between devices  12.8 us (29%)
  between operations  0.81 us (2%)
  other arithmetic  0.77 us (2%)
    ppermute x8, starting transfers between devices, exchange(): return lax.ppermute(value, 'ctx', [(i, i ^ distance) for i in range(count)])  13.3 us
    ppermute x8, waiting for transfers between devices, exchange(): return lax.ppermute(value, 'ctx', [(i, i ^ distance) for i in range(count)])  12.8 us
    pallas_call x1, Pallas kernels, local(): call(functools.partial(sums_kernel, length=length, modes=modes, members=m...  4.17 us
    pallas_call x1, Pallas kernels, local(): call(functools.partial(state_kernel, length=length, modes=modes, members=...  2.46 us
    pallas_call x1, Pallas kernels, local(): call(functools.partial(finish, own=True), grads, [SMEM] + [VMEM] * 9, wor...  1.99 us
    pallas_call x1, Pallas kernels, local(): call(functools.partial(gate_kernel, members=members, pieces=pieces), (hal...  1.87 us
    pallas_call x1, Pallas kernels, local(): call(functools.partial(finish, own=False), (half,), [SMEM] + [VMEM] * 6,...  1.77 us
    pallas_call x1, Pallas kernels, local(): call(functools.partial(last_kernel, tokens=tokens, modes=modes, members=m...  1.44 us
  transfers between devices with their start and end apart: 8, of which 5 were waited for; matrix products, arithmetic and copies ran while one was open for 0% of the time, Pallas kernels for 13%

profile of v3, /device:TPU:0, one launch (start us, length us, event | category | flops | bytes accessed | tf_op | source)
XLA Modules:
  0.0 43.3 jit_solution(12545127647516834423)
XLA Ops:
  0.6 0.7 %pad_maximum_fusion.3.refs_3_ = f32[2,16,128]{2,1,0:T(8,128)S(1)} fusion(f32[1,16,128]{2,1,0:T(8,128)} %bitcast.30, f32[1,16,128]{2,1,0:T(8,128)} %bitcast.31), kind=kLoop, calls=%fused_computation.7 | loop fusion | flops 4096 | bytes 32768 | tf_op jit(solution)/shard_map/stack | solution.py:485
  1.3 4.0 %collective-permute-start = (f32[2,16,128]{2,1,0:T(8,128)S(1)}, f32[2,16,128]{2,1,0:T(8,128)S(1)}, u32[]{:S(2)}, u32[]{:S(2)}) collective-permute-start(f32[2,16,128]{2,1,0:T(8,128)S(1)} %pad_maximum_fusion.3.refs_3_), channel_id=1, source_target_pairs={{0,16},{2,18},{4,20},{6,22},{8,24},{10,26},{12,28},{14,30},{16,0},... | collective-permute-start | bytes 49160 | tf_op jit(solution)/shard_map/ppermute | solution.py:449
  5.4 1.9 %shard_map.101 = (bf16[2,8,128,128]{3,2,1,0:T(8,128)(2,1)S(1)}, bf16[2,8,128,128]{3,2,1,0:T(8,128)(2,1)S(1)}) custom-call(s32[1]{0:T(128)} %bitcast.me_ref, bf16[128,2048]{1,0:T(8,128)(2,1)} %q_hbm.1, bf16[128,2048]{1,0:T(8,128)(2,1)} %k_ref.1, bf16[128,2048]{1,0:T(8,128)(2,1)} %v_ref.1, bf16[128,2048]{1,0:T(8,128)(2,1)} %u_ref.1), custom_call_target="tpu_custom_call" | custom-call | flops 4194304 | bytes 1048576 | tf_op jit(solution)/shard_map/pallas_call | solution.py:477
  7.3 0.0 collective-permute-done
  7.3 0.1 collective-permute-start.3
  7.4 1.7 %collective-permute-start.1 = (f32[2,2,16,128]{3,2,1,0:T(8,128)S(1)}, f32[2,2,16,128]{3,2,1,0:T(8,128)S(1)}, u32[]{:S(2)}, u32[]{:S(2)}) collective-permute-start(f32[2,2,16,128]{3,2,1,0:T(8,128)S(1)} %pad_maximum_fusion.2), channel_id=1, source_target_pairs={{0,8},{2,10},{4,12},{6,14},{8,0},{10,2},{12,4},{14,6},{16,24},{18,... | collective-permute-start | bytes 98312 | tf_op jit(solution)/shard_map/ppermute | solution.py:449
  9.1 2.3 %collective-permute-done.1 = f32[2,2,16,128]{3,2,1,0:T(8,128)S(1)} collective-permute-done((f32[2,2,16,128]{3,2,1,0:T(8,128)S(1)}, f32[2,2,16,128]{3,2,1,0:T(8,128)S(1)}, u32[]{:S(2)}, u32[]{:S(2)}) %collective-permute-start.1) | collective-permute-done | bytes 32800 | tf_op jit(solution)/shard_map/ppermute | solution.py:449
  11.4 1.7 %collective-permute-start.2 = (f32[2,2,2,16,128]{4,3,2,0,1:T(8,128)S(1)}, f32[2,2,2,16,128]{4,3,2,0,1:T(8,128)S(1)}, u32[]{:S(2)}, u32[]{:S(2)}) collective-permute-start(f32[2,2,2,16,128]{4,3,2,0,1:T(8,128)S(1)} %pad_maximum_fusion.1), channel_id=1, source_target_pairs={{0,4},{2,6},{4,0},{6,2},{8,12},{10,14},{12,8},{14,10},{16,20},{18,... | collective-permute-start | bytes 196616 | tf_op jit(solution)/shard_map/ppermute | solution.py:449
  13.1 0.0 collective-permute-done.3.got_ref
  13.1 0.9 %shard_map.102 = (f32[2048,128]{1,0:T(8,128)S(1)}, f32[2048,128]{1,0:T(8,128)S(1)}, f32[8,8,128]{2,1,0:T(8,128)S(1)}) custom-call(s32[1]{0:T(128)} %bitcast.me_ref, bf16[2,8,128,128]{3,2,1,0:T(8,128)(2,1)S(1)} %get-tuple-element.48.own_ref, bf16[2,8,128,128]{3,2,1,0:T(8,128)(2,1)S(1)} %collective-permute-done.3.got_ref), custom_call_target="tpu_custom_call" | custom-call | flops 4194304 | bytes 1048576 | tf_op jit(solution)/shard_map/pallas_call | solution.py:493
  14.0 1.7 %collective-permute-done.2 = f32[2,2,2,16,128]{4,3,2,0,1:T(8,128)S(1)} collective-permute-done((f32[2,2,2,16,128]{4,3,2,0,1:T(8,128)S(1)}, f32[2,2,2,16,128]{4,3,2,0,1:T(8,128)S(1)}, u32[]{:S(2)}, u32[]{:S(2)}) %collective-permute-start.2) | collective-permute-done | bytes 65568 | tf_op jit(solution)/shard_map/ppermute | solution.py:449
  15.8 2.5 %shard_map.103 = (f32[2,128,128]{2,1,0:T(8,128)S(1)}, f32[32,16,8,128]{3,2,1,0:T(8,128)S(1)}, f32[33,16,8,128]{3,2,1,0:T(8,128)S(1)}, f32[2048,128]{1,0:T(8,128)S(1)}, f32[2048,128]{1,0:T(8,128)S(1)}) custom-call(f32[2048,128]{1,0:T(8,128)S(1)} %get-tuple-element.65.x_ref, f32[2048,128]{1,0:T(8,128)S(1)} %get-tuple-element.66.g_ref, f32[256,128]{1,0:T(8,128)S(1)} %bitcast.22), custom_call_target="tpu_custom_call" | custom-call | flops 16777216 | bytes 1048576 | tf_op jit(solution)/shard_map/pallas_call | solution.py:514
  18.2 4.2 %shard_map.104 = (f32[4,128,128]{2,1,0:T(8,128)}, bf16[512,128]{1,0:T(8,128)(2,1)S(1)}, f32[4,64,128]{2,1,0:T(8,128)S(1)}) custom-call(s32[1]{0:T(128)} %bitcast.me_ref, f32[2048,128]{1,0:T(8,128)S(1)} %get-tuple-element.57.x_ref, f32[2048,128]{1,0:T(8,128)S(1)} %get-tuple-element.58.g_ref, f32[8,8,128]{2,1,0:T(8,128)S(1)} %get-tuple-element.59.lag_ref, ...), custom_call_target="tpu_custom_call" | custom-call | flops 25165824 | bytes 1048576 | tf_op jit(solution)/shard_map/pallas_call | solution.py:524
  22.4 1.6 %collective-permute-start.4 = (bf16[512,128]{1,0:T(8,128)(2,1)S(1)}, bf16[512,128]{1,0:T(8,128)(2,1)S(1)}, u32[]{:S(2)}, u32[]{:S(2)}) collective-permute-start(bf16[512,128]{1,0:T(8,128)(2,1)S(1)} %get-tuple-element.62), channel_id=1, source_target_pairs={{0,4},{2,6},{4,0},{6,2},{8,12},{10,14},{12,8},{14,10},{16,20},{18,... | collective-permute-start | bytes 393224 | tf_op jit(solution)/shard_map/ppermute | solution.py:449
  24.1 3.3 %collective-permute-done.4.got_ref = bf16[512,128]{1,0:T(8,128)(2,1)S(1)} collective-permute-done((bf16[512,128]{1,0:T(8,128)(2,1)S(1)}, bf16[512,128]{1,0:T(8,128)(2,1)S(1)}, u32[]{:S(2)}, u32[]{:S(2)}) %collective-permute-start.4) | collective-permute-done | bytes 131104 | tf_op jit(solution)/shard_map/ppermute | solution.py:449
  27.4 0.1 shard_map.105
  27.5 1.7 %collective-permute-start.5 = (bf16[384,128]{1,0:T(8,128)(2,1)S(1)}, bf16[384,128]{1,0:T(8,128)(2,1)S(1)}, u32[]{:S(2)}, u32[]{:S(2)}) collective-permute-start(bf16[384,128]{1,0:T(8,128)(2,1)S(1)} %get-tuple-element.70), channel_id=1, source_target_pairs={{0,8},{2,10},{4,12},{6,14},{8,0},{10,2},{12,4},{14,6},{16,24},{18,... | collective-permute-start | bytes 294920 | tf_op jit(solution)/shard_map/ppermute | solution.py:449
  29.2 3.5 %collective-permute-done.5.got_ref = bf16[384,128]{1,0:T(8,128)(2,1)S(1)} collective-permute-done((bf16[384,128]{1,0:T(8,128)(2,1)S(1)}, bf16[384,128]{1,0:T(8,128)(2,1)S(1)}, u32[]{:S(2)}, u32[]{:S(2)}) %collective-permute-start.5) | collective-permute-done | bytes 98336 | tf_op jit(solution)/shard_map/ppermute | solution.py:449
  32.7 0.1 shard_map.107
  32.8 2.4 %collective-permute-start.6 = (bf16[192,128]{1,0:T(8,128)(2,1)S(1)}, bf16[192,128]{1,0:T(8,128)(2,1)S(1)}, u32[]{:S(2)}, u32[]{:S(2)}) collective-permute-start(bf16[192,128]{1,0:T(8,128)(2,1)S(1)} %get-tuple-element.74), channel_id=1, source_target_pairs={{0,16},{2,18},{4,20},{6,22},{8,24},{10,26},{12,28},{14,30},{16,0},... | collective-permute-start | bytes 147464 | tf_op jit(solution)/shard_map/ppermute | solution.py:449
  35.2 0.7 %shard_map.106 = (f32[2048,128]{1,0:T(8,128)S(1)}, f32[2048,128]{1,0:T(8,128)S(1)}) custom-call(f32[2048,128]{1,0:T(8,128)S(1)} %get-tuple-element.65.x_ref, f32[2048,128]{1,0:T(8,128)S(1)} %get-tuple-element.66.g_ref, f32[256,128]{1,0:T(8,128)S(1)} %bitcast.26), custom_call_target="tpu_custom_call" | custom-call | flops 4194304 | bytes 1048576 | tf_op jit(solution)/shard_map/pallas_call | solution.py:547
  35.9 2.0 %collective-permute-done.6.far_ref.refs_1_ = bf16[192,128]{1,0:T(8,128)(2,1)S(1)} collective-permute-done((bf16[192,128]{1,0:T(8,128)(2,1)S(1)}, bf16[192,128]{1,0:T(8,128)(2,1)S(1)}, u32[]{:S(2)}, u32[]{:S(2)}) %collective-permute-start.6) | collective-permute-done | bytes 49184 | tf_op jit(solution)/shard_map/ppermute | solution.py:449
  37.9 0.0 copy-start
  37.9 0.0 copy-start.1
  38.0 0.0 copy-start.2
  38.0 1.8 %shard_map.109 = bf16[2,8,128,128]{3,2,1,0:T(8,128)(2,1)S(1)} custom-call(s32[1]{0:T(128)} %bitcast.me_ref, f32[2048,128]{1,0:T(8,128)S(1)} %get-tuple-element.67.y_ref, f32[2048,128]{1,0:T(8,128)S(1)} %get-tuple-element.68.z_ref, f32[32,16,8,128]{3,2,1,0:T(8,128)S(1)} %get-tuple-element.60.hs_ref, f32[33,16,8,128]{3,2,1,0:T(8,128)S(1)} %get-tuple-element.61.ks_ref, ...), custom_call_target="tpu_custom_call" | custom-call | flops 8388608 | bytes 1048576 | tf_op jit(solution)/shard_map/pallas_call | solution.py:556
  39.7 0.1 collective-permute-start.7
  39.8 0.0 copy-done
  39.8 0.0 copy-done.1
  39.8 0.0 copy-done.2
  39.9 2.0 %shard_map.110 = (bf16[128,2048]{1,0:T(8,128)(2,1)S(1)}, bf16[128,2048]{1,0:T(8,128)(2,1)S(1)}, bf16[128,2048]{1,0:T(8,128)(2,1)S(1)}) custom-call(s32[1]{0:T(128)} %bitcast.me_ref, f32[2048,128]{1,0:T(8,128)S(1)} %get-tuple-element.67.y_ref, f32[2048,128]{1,0:T(8,128)S(1)} %get-tuple-element.68.z_ref, f32[32,16,8,128]{3,2,1,0:T(8,128)S(1)} %get-tuple-element.60.hs_ref, ...), custom_call_target="tpu_custom_call" | custom-call | flops 8388608 | bytes 1048576 | tf_op jit(solution)/shard_map/pallas_call | solution.py:561
  41.8 0.0 collective-permute-done.7.got_ref
  41.9 1.4 %shard_map.111 = (bf16[128,2048]{1,0:T(8,128)(2,1)S(1)}, bf16[128,2048]{1,0:T(8,128)(2,1)S(1)}, bf16[128,2048]{1,0:T(8,128)(2,1)S(1)}, bf16[128,2048]{1,0:T(8,12...) custom-call(s32[1]{0:T(128)} %bitcast.me_ref, ...), custom_call_target="tpu_custom_call", output_to_operand_aliasing={{0}: (9, {}), {1}: (10, {}), {2}: (11, {})} | custom-call | flops 4194304 | bytes 1048576 | tf_op jit(solution)/shard_map/pallas_call | solution.py:567
  (8 shorter events, 0.1 us)
Async XLA Ops:
  1.3 5.9 %collective-permute-start = (f32[2,16,128]{2,1,0:T(8,128)S(1)}, f32[2,16,128]{2,1,0:T(8,128)S(1)}, u32[]{:S(2)}, u32[]{:S(2)}) collective-permute-start(f32[2,16,128]{2,1,0:T(8,128)S(1)} %pad_maximum_fusion.3.refs_3_), channel_id=1, source_target_pairs={{0,16},{2,18},{4,20},{6,22},{8,24},{10,26},{12,28},{14,30},{16,0},... | collective-permute-start | bytes 49160 | tf_op jit(solution)/shard_map/ppermute | solution.py:449
  7.3 5.8 %collective-permute-start.3 = (bf16[2,8,128,128]{3,2,1,0:T(8,128)(2,1)S(1)}, bf16[2,8,128,128]{3,2,1,0:T(8,128)(2,1)S(1)}, u32[]{:S(2)}, u32[]{:S(2)}) collective-permute-start(bf16[2,8,128,128]{3,2,1,0:T(8,128)(2,1)S(1)} %get-tuple-element.49), channel_id=1, source_target_pairs={{0,2},{2,0},{4,6},{6,4},{8,10},{10,8},{12,14},{14,12},{16,18},{18,... | collective-permute-start | bytes 1572872 | tf_op jit(solution)/shard_map/ppermute | solution.py:449
  7.4 4.0 %collective-permute-start.1 = (f32[2,2,16,128]{3,2,1,0:T(8,128)S(1)}, f32[2,2,16,128]{3,2,1,0:T(8,128)S(1)}, u32[]{:S(2)}, u32[]{:S(2)}) collective-permute-start(f32[2,2,16,128]{3,2,1,0:T(8,128)S(1)} %pad_maximum_fusion.2), channel_id=1, source_target_pairs={{0,8},{2,10},{4,12},{6,14},{8,0},{10,2},{12,4},{14,6},{16,24},{18,... | collective-permute-start | bytes 98312 | tf_op jit(solution)/shard_map/ppermute | solution.py:449
  11.4 4.3 %collective-permute-start.2 = (f32[2,2,2,16,128]{4,3,2,0,1:T(8,128)S(1)}, f32[2,2,2,16,128]{4,3,2,0,1:T(8,128)S(1)}, u32[]{:S(2)}, u32[]{:S(2)}) collective-permute-start(f32[2,2,2,16,128]{4,3,2,0,1:T(8,128)S(1)} %pad_maximum_fusion.1), channel_id=1, source_target_pairs={{0,4},{2,6},{4,0},{6,2},{8,12},{10,14},{12,8},{14,10},{16,20},{18,... | collective-permute-start | bytes 196616 | tf_op jit(solution)/shard_map/ppermute | solution.py:449
  22.4 5.0 %collective-permute-start.4 = (bf16[512,128]{1,0:T(8,128)(2,1)S(1)}, bf16[512,128]{1,0:T(8,128)(2,1)S(1)}, u32[]{:S(2)}, u32[]{:S(2)}) collective-permute-start(bf16[512,128]{1,0:T(8,128)(2,1)S(1)} %get-tuple-element.62), channel_id=1, source_target_pairs={{0,4},{2,6},{4,0},{6,2},{8,12},{10,14},{12,8},{14,10},{16,20},{18,... | collective-permute-start | bytes 393224 | tf_op jit(solution)/shard_map/ppermute | solution.py:449
  27.5 5.2 %collective-permute-start.5 = (bf16[384,128]{1,0:T(8,128)(2,1)S(1)}, bf16[384,128]{1,0:T(8,128)(2,1)S(1)}, u32[]{:S(2)}, u32[]{:S(2)}) collective-permute-start(bf16[384,128]{1,0:T(8,128)(2,1)S(1)} %get-tuple-element.70), channel_id=1, source_target_pairs={{0,8},{2,10},{4,12},{6,14},{8,0},{10,2},{12,4},{14,6},{16,24},{18,... | collective-permute-start | bytes 294920 | tf_op jit(solution)/shard_map/ppermute | solution.py:449
  32.8 5.1 %collective-permute-start.6 = (bf16[192,128]{1,0:T(8,128)(2,1)S(1)}, bf16[192,128]{1,0:T(8,128)(2,1)S(1)}, u32[]{:S(2)}, u32[]{:S(2)}) collective-permute-start(bf16[192,128]{1,0:T(8,128)(2,1)S(1)} %get-tuple-element.74), channel_id=1, source_target_pairs={{0,16},{2,18},{4,20},{6,22},{8,24},{10,26},{12,28},{14,30},{16,0},... | collective-permute-start | bytes 147464 | tf_op jit(solution)/shard_map/ppermute | solution.py:449
  37.9 1.9 %copy-start = (bf16[128,2048]{1,0:T(8,128)(2,1)S(1)}, bf16[128,2048]{1,0:T(8,128)(2,1)}, u32[]{:S(2)}) copy-start(bf16[128,2048]{1,0:T(8,128)(2,1)} %k_ref.1) | copy-start | bytes 1572868
  37.9 1.9 %copy-start.1 = (bf16[128,2048]{1,0:T(8,128)(2,1)S(1)}, bf16[128,2048]{1,0:T(8,128)(2,1)}, u32[]{:S(2)}) copy-start(bf16[128,2048]{1,0:T(8,128)(2,1)} %v_ref.1) | copy-start | bytes 1572868
  38.0 1.9 %copy-start.2 = (bf16[128,2048]{1,0:T(8,128)(2,1)S(1)}, bf16[128,2048]{1,0:T(8,128)(2,1)}, u32[]{:S(2)}) copy-start(bf16[128,2048]{1,0:T(8,128)(2,1)} %u_ref.1) | copy-start | bytes 1572868
  39.7 2.1 %collective-permute-start.7 = (bf16[2,8,128,128]{3,2,1,0:T(8,128)(2,1)S(1)}, bf16[2,8,128,128]{3,2,1,0:T(8,128)(2,1)S(1)}, u32[]{:S(2)}, u32[]{:S(2)}) collective-permute-start(bf16[2,8,128,128]{3,2,1,0:T(8,128)(2,1)S(1)} %shard_map.109), channel_id=1, source_target_pairs={{0,2},{2,0},{4,6},{6,4},{8,10},{10,8},{12,14},{14,12},{16,18},{18,... | collective-permute-start | bytes 1572872 | tf_op jit(solution)/shard_map/ppermute | solution.py:449

commit v4 on v3

--- a/solution.py
+++ b/solution.py
@@ -58,6 +58,7 @@
 
 def series_kernel(me_ref, own_ref, got_ref, x_ref, g_ref, lag_ref, *, tokens, members):
     core = me_ref[0] % SETS
+    half = members // 2
     for ref, chunk in ((own_ref, core), (got_ref, 1 - core)):
 
         def body(tile, _):
@@ -65,22 +66,24 @@
             for member in range(members):
                 for i, out_ref in enumerate((x_ref, g_ref)):
                     value = ref[i, member, rows, :].astype(F32)
-                    for half in range(2):
-                        start = (chunk * tokens + tile * 16 + half * 8) * members + member
-                        out_ref[pl.ds(start, 8, stride=members), :] = value[half * 8 : half * 8 + 8]
+                    for part in range(2):
+                        start = (tile * 16 + part * 8) * members + chunk * half + member // 2
+                        out_ref[member % 2, pl.ds(start, 8, stride=members), :] = value[part * 8 : part * 8 + 8]
             return 0
 
         lax.fori_loop(0, tokens // 16, body, 0)
 
-    def step(i, lags):
-        x = [x_ref[pl.ds((i * STRETCH + t) * members, members), :] for t in range(STRETCH)]
-        g = [g_ref[pl.ds((i * STRETCH + t) * members, members), :] for t in range(STRETCH)]
-        return tuple(lags[j] + total([g[t] * x[t - j] for t in range(j, STRETCH)]) for j in range(STRETCH))
-
-    zero = tuple(jnp.zeros((members, LANES), F32) for _ in range(STRETCH))
-    lags = lax.fori_loop(0, SETS * tokens // STRETCH, step, zero)
-    for j in range(STRETCH):
-        lag_ref[j] = lags[j]
+    for side in range(2):
+
+        def step(i, lags):
+            x = [x_ref[side, pl.ds((i * STRETCH + t) * members, members), :] for t in range(STRETCH)]
+            g = [g_ref[side, pl.ds((i * STRETCH + t) * members, members), :] for t in range(STRETCH)]
+            return tuple(lags[j] + total([g[t] * x[t - j] for t in range(j, STRETCH)]) for j in range(STRETCH))
+
+        zero = tuple(jnp.zeros((members, LANES), F32) for _ in range(STRETCH))
+        lags = lax.fori_loop(0, tokens // STRETCH, step, zero)
+        for j in range(STRETCH):
+            lag_ref[side, j] = lags[j]
 
 
 def param_rows(par_ref, param, mode, modes, members):
@@ -91,9 +94,21 @@
     return par_ref[pl.ds(pl.multiple_of(member * 2 * modes, modes), modes), :]
 
 
-def state_kernel(x_ref, g_ref, par_ref, sk_ref, hs_ref, ks_ref, xw_ref, gw_ref, *, length, modes, members):
-    w = [jnp.exp(-param_rows(par_ref, 0, m, modes, members)) for m in range(modes)]
-    stretches = length // STRETCH
+def half_rows(par_ref, start, stride, members):
+    rows = par_ref[pl.ds(start, members // 2, stride=stride), :]
+    return jnp.concatenate([rows, rows], axis=0)
+
+
+def chosen_half(me_ref, flip):
+    side = (me_ref[0] // SETS) % 2
+    return 1 - side if flip else side
+
+
+def state_kernel(me_ref, x_ref, g_ref, par_ref, sk_ref, hs_ref, ks_ref, xw_ref, gw_ref, *, tokens, modes, members, flip):
+    side = chosen_half(me_ref, flip)
+    half = members // 2
+    w = [jnp.exp(-half_rows(par_ref, m, 2 * modes, members)) for m in range(modes)]
+    stretches = tokens // STRETCH
 
     def step(i, carry):
         s, k = carry
@@ -103,7 +118,7 @@
         for t in range(STRETCH):
             at = pl.ds((i * STRETCH + t) * members, members)
             at_back = pl.ds((back * STRETCH + STRETCH - 1 - t) * members, members)
-            x, g = x_ref[at, :], g_ref[at_back, :]
+            x, g = x_ref[side, at, :], g_ref[side, at_back, :]
             xw_ref[at, :] = x * float(STRETCH - 1 - t)
             gw_ref[at_back, :] = g * float(STRETCH - 1 - t)
             s = tuple(w[m] * s[m] + x for m in range(modes))
@@ -117,30 +132,52 @@
         ks_ref[stretches, m] = zero[m]
     s, k = lax.fori_loop(0, stretches, step, (zero, zero), unroll=2)
     for m in range(modes):
-        at = pl.ds(m, members, stride=modes)
-        sk_ref[0, at, :] = s[m]
-        sk_ref[1, at, :] = k[m]
-
-
-def taps_kernel(x_ref, g_ref, par_ref, y_ref, z_ref, *, length, modes, members):
-    rate = [param_rows(par_ref, 0, m, modes, members) for m in range(modes)]
-    w = [jnp.exp(-rate[m]) for m in range(modes)]
-    power = [param_rows(par_ref, 1, m, modes, members) * jnp.sqrt(rate[m]) for m in range(modes)]
-    taps = []
-    for j in range(STRETCH):
-        taps.append(total(power))
-        power = [power[m] * w[m] for m in range(modes)]
-
-    def within(i, _):
-        at = [pl.ds((i * STRETCH + t) * members, members) for t in range(STRETCH)]
-        x = [x_ref[at[t], :] for t in range(STRETCH)]
-        g = [g_ref[at[t], :] for t in range(STRETCH)]
-        for t in range(STRETCH):
-            y_ref[at[t], :] = total([taps[j] * x[t - j] for j in range(t + 1)])
-            z_ref[at[t], :] = total([taps[j] * g[t + j] for j in range(STRETCH - t)])
-        return 0
-
-    lax.fori_loop(0, length // STRETCH, within, 0, unroll=2)
+        at = pl.ds(m, half, stride=modes)
+        for i, value in enumerate((s[m], k[m])):
+            sk_ref[i, 0, at, :] = value[:half]
+            sk_ref[i, 1, at, :] = value[half:]
+
+
+def taps_kernel(x_ref, g_ref, par_ref, y_ref, z_ref, *, tokens, modes, members):
+    half = members // 2
+    for side in range(2):
+        rate = [half_rows(par_ref, side * 2 * modes + m, 4 * modes, members) for m in range(modes)]
+        w = [jnp.exp(-rate[m]) for m in range(modes)]
+        power = [half_rows(par_ref, (side * 2 + 1) * modes + m, 4 * modes, members) * jnp.sqrt(rate[m]) for m in range(modes)]
+        taps = []
+        for j in range(STRETCH):
+            taps.append(total(power))
+            power = [power[m] * w[m] for m in range(modes)]
+
+        def within(i, _):
+            at = [pl.ds((i * STRETCH + t) * members, members) for t in range(STRETCH)]
+            x = [x_ref[side, at[t], :] for t in range(STRETCH)]
+            g = [g_ref[side, at[t], :] for t in range(STRETCH)]
+            for t in range(STRETCH):
+                y = total([taps[j] * x[t - j] for j in range(t + 1)])
+                z = total([taps[j] * g[t + j] for j in range(STRETCH - t)])
+                for chunk in range(2):
+                    to = pl.ds((chunk * tokens + i * STRETCH + t) * members + side, half, stride=2)
+                    y_ref[to, :] = y[chunk * half : (chunk + 1) * half]
+                    z_ref[to, :] = z[chunk * half : (chunk + 1) * half]
+            return 0
+
+        lax.fori_loop(0, tokens // STRETCH, within, 0, unroll=2)
+
+
+def order_kernel(me_ref, hs_own, ks_own, hs_far, ks_far, hs_ref, ks_ref, *, tokens, modes, members):
+    half = members // 2
+    for src, out, count in ((0, hs_ref, tokens // STRETCH), (1, ks_ref, tokens // STRETCH + 1)):
+
+        def body(i, _):
+            for flip, ref in ((False, (hs_own, ks_own)[src]), (True, (hs_far, ks_far)[src])):
+                side = chosen_half(me_ref, flip)
+                for m in range(modes):
+                    for chunk in range(2):
+                        out[chunk, i, pl.ds(m * members + side, half, stride=2), :] = ref[i, m, chunk * half : (chunk + 1) * half, :]
+            return 0
+
+        lax.fori_loop(0, count, body, 0)
 
 
 def flags(bit):
@@ -148,25 +185,33 @@
     return bit, 1.0 - bit
 
 
-def put_states(ref, me, span, member, s, k, modes, members, last):
-    at = pl.ds(member * modes, modes)
+def put_states(ref, me, span, at, at_k, s, k, last):
     if last:
         earlier, later = flags((me // span) % 2 == 1)
         ref[at, :] = (earlier * k + later * s).astype(BF16)
     else:
         ref[at, :] = s.astype(BF16)
-        ref[pl.ds((members + member) * modes, modes), :] = k.astype(BF16)
-
-
-def sums_kernel(
-    me_ref, x_ref, g_ref, lag_ref, hs_ref, ks_ref, sk_ref, par_ref, sums_ref, message_ref, *kept,
-    length, modes, members, part, unroll, last, tree,
-):
-    stretches = length // STRETCH
+        ref[at_k, :] = k.astype(BF16)
+
+
+def blocks(member, modes, members):
+    if isinstance(member, int):
+        return pl.ds(member * modes, modes), pl.ds((members + member) * modes, modes)
+    return tuple(pl.ds(pl.multiple_of(m * modes, modes), modes) for m in (member, members + member))
+
+
+def sums_kernel(me_ref, x_ref, g_ref, lag_ref, hs_ref, ks_ref, sk_ref, par_ref, *refs, tokens, modes, members, part, unroll, flip, last, tree):
+    if flip:
+        sk_own, par_own, sums_ref, tot_ref, message_ref, work_ref = refs
+    else:
+        sums_ref, work_ref = refs
+    side = chosen_half(me_ref, flip)
+    half = members // 2
+    stretches = tokens // STRETCH
     width = float(STRETCH)
     zero = jnp.zeros((members, LANES), F32)
     for first in range(0, modes, part):
-        rate = [param_rows(par_ref, 0, first + m, modes, members) for m in range(part)]
+        rate = [half_rows(par_ref, first + m, 2 * modes, members) for m in range(part)]
         w = [jnp.exp(-rate[m]) for m in range(part)]
         fade = [jnp.exp(rate[m] * -width) for m in range(part)]
 
@@ -201,31 +246,40 @@
             return tuple(out)
 
         sums = lax.fori_loop(0, stretches, step, ((zero,) * 6,) * part, unroll=unroll)
+        lags = [lag_ref[side, j] for j in range(STRETCH)]
         for m in range(part):
             same, next_, b_k, b_s, sd, kd = sums[m]
-            r, d = lag_ref[STRETCH - 1], (width - 1.0) * lag_ref[STRETCH - 1]
+            r, d = lags[STRETCH - 1], (width - 1.0) * lags[STRETCH - 1]
             for j in range(STRETCH - 2, -1, -1):
-                r = r * w[m] + lag_ref[j]
-                d = d * w[m] + float(j) * lag_ref[j]
-            at = pl.ds(first + m, members, stride=modes)
-            sums_ref[0, at, :] = r + w[m] * (same - fade[m] * next_)
-            sums_ref[1, at, :] = d + w[m] * (b_k + b_s + same + (width - 1.0) * (fade[m] * next_))
-            sums_ref[2, at, :] = sd
-            sums_ref[3, at, :] = kd
+                r = r * w[m] + lags[j]
+                d = d * w[m] + float(j) * lags[j]
+            r = r + w[m] * (same - fade[m] * next_)
+            d = d + w[m] * (b_k + b_s + same + (width - 1.0) * (fade[m] * next_))
+            at = pl.ds(first + m, half, stride=modes)
+            for i, value in enumerate((r, d, sd, kd)):
+                work_ref[i, 0, at, :] = value[:half]
+                work_ref[i, 1, at, :] = value[half:]
 
     me = me_ref[0]
-    for member in range(members):
-        at = pl.ds(member * modes, modes)
-        put_states(message_ref, me, SETS, member, sk_ref[0, at, :], sk_ref[1, at, :], modes, members, last)
-    if tree:
-        side = (me // SETS) % 2
-        offset = members * modes * (1 if last else 2)
-        for to in range(members // 2):
-            for i in range(4):
-                index = pl.ds(pl.multiple_of((to * 2 + side) * modes, modes), modes)
-                kept[0][i, pl.ds(to * modes, modes), :] = sums_ref[i, index, :]
-                index = pl.ds(pl.multiple_of((to * 2 + 1 - side) * modes, modes), modes)
-                message_ref[pl.ds(offset + (i * (members // 2) + to) * modes, modes), :] = sums_ref[i, index, :].astype(BF16)
+    rows = members * modes
+    for z in range(half):
+        at = pl.ds(z * modes, modes)
+        left, right = (tuple(work_ref[i, c, at, :] for i in range(4)) + (sk_ref[0, c, at, :], sk_ref[1, c, at, :]) for c in range(2))
+        rate = par_ref[pl.ds(z * 2 * modes, modes), :]
+        for i, value in enumerate(join(rate, left, right, float(tokens))):
+            sums_ref[i, at, :] = value
+            if flip and tree:
+                offset = rows * (1 if last else 2)
+                message_ref[pl.ds(offset + (i * half + z) * modes, modes), :] = value.astype(BF16)
+        if flip:
+            for ref, member, par in ((sk_ref, z * 2 + side, par_ref), (sk_own, z * 2 + 1 - side, par_own)):
+                fade = jnp.exp(par[pl.ds(z * 2 * modes, modes), :] * -float(tokens))
+                s = fade * ref[0, 0, at, :] + ref[0, 1, at, :]
+                k = ref[1, 0, at, :] + fade * ref[1, 1, at, :]
+                to, to_k = blocks(member, modes, members)
+                tot_ref[0, to, :] = s
+                tot_ref[1, to, :] = k
+                put_states(message_ref, me, SETS, to, to_k, s, k, last)
 
 
 def join(rate, left, right, length):
@@ -271,7 +325,7 @@
             after += enter_ref[1, at, :]
         new_ref[0, at, :] = before
         new_ref[1, at, :] = after
-        put_states(message_ref, me, span * 2, member, s_sum, k_sum, modes, members, last)
+        put_states(message_ref, me, span * 2, *blocks(member, modes, members), s_sum, k_sum, last)
     if not tree:
         return
     side = (me // (span * 2)) % 2
@@ -298,20 +352,27 @@
                     message_ref[pl.ds(offset + (i * (count // 2) + to) * modes, modes), :] = value.astype(BF16)
 
 
-def enter_kernel(me_ref, enter_ref, far_ref, par_ref, in_ref, *, tokens, modes, members, span):
+def enter_kernel(me_ref, enter_ref, far_ref, par_ref, sk_own, sk_far, in_ref, *, tokens, modes, members, span):
     me = me_ref[0]
     earlier, later = flags((me // span) % 2 == 1)
     inside = (me // 2) % (span // 2) * 2
     gap = earlier * inside.astype(F32) + later * (span - 2 - inside).astype(F32)
-    for member in range(members):
-        at = pl.ds(member * modes, modes)
-        value = jnp.exp(rate_block(par_ref, member, modes) * (gap * -float(tokens))) * far_ref[at, :].astype(F32)
-        before, after = earlier * value, later * value
-        if span > 2:
-            before += enter_ref[0, at, :]
-            after += enter_ref[1, at, :]
-        in_ref[0, at, :] = before
-        in_ref[1, at, :] = after
+    for ref, flip in ((sk_own, False), (sk_far, True)):
+        side = chosen_half(me_ref, flip)
+        for z in range(members // 2):
+            src = pl.ds(z * modes, modes)
+            at, _ = blocks(z * 2 + side, modes, members)
+            rate = rate_block(par_ref, z * 2 + side, modes)
+            value = jnp.exp(rate * (gap * -float(tokens))) * far_ref[at, :].astype(F32)
+            fade = jnp.exp(rate * -float(tokens))
+            before, after = earlier * value, later * value
+            if span > 2:
+                before += enter_ref[0, at, :]
+                after += enter_ref[1, at, :]
+            in_ref[0, 0, at, :] = before
+            in_ref[0, 1, at, :] = ref[1, 1, src, :] + fade * after
+            in_ref[1, 0, at, :] = ref[0, 0, src, :] + fade * before
+            in_ref[1, 1, at, :] = after
 
 
 def finish_kernel(me_ref, y_ref, z_ref, hs_ref, ks_ref, par_ref, in_ref, *refs, tokens, modes, members, own):
@@ -321,22 +382,17 @@
         send_ref, yo_ref, zo_ref = refs
     core = me_ref[0] % SETS
     chunk = core if own else 1 - core
-    second, first = flags(chunk == 1)
     stretches = tokens // STRETCH
     base = chunk * stretches
     rate = [param_rows(par_ref, 0, m, modes, members) for m in range(modes)]
     w = [jnp.exp(-rate[m]) for m in range(modes)]
     fade = [jnp.exp(rate[m] * -float(STRETCH)) for m in range(modes)]
     amp = [param_rows(par_ref, 1, m, modes, members) * jnp.sqrt(rate[m]) * w[m] for m in range(modes)]
-    h = tuple(
-        in_ref[0, pl.ds(m, members, stride=modes), :] * jnp.exp(rate[m] * (second * -float(tokens))) for m in range(modes)
-    )
-    k = tuple(
-        in_ref[1, pl.ds(m, members, stride=modes), :] * jnp.exp(rate[m] * (first * -float(tokens))) for m in range(modes)
-    )
+    h = tuple(in_ref[chunk, 0, pl.ds(m, members, stride=modes), :] for m in range(modes))
+    k = tuple(in_ref[chunk, 1, pl.ds(m, members, stride=modes), :] for m in range(modes))
 
     def forward(i, h):
-        p = [amp[m] * (h[m] + hs_ref[base + i, m]) for m in range(modes)]
+        p = [amp[m] * (h[m] + hs_ref[chunk, i, pl.ds(m * members, members), :]) for m in range(modes)]
         for t in range(STRETCH):
             at = pl.ds((i * STRETCH + t) * members, members)
             yo_ref[at, :] = y_ref[pl.ds(((base + i) * STRETCH + t) * members, members), :] + total(p)
@@ -346,7 +402,7 @@
 
     def backward(i, k):
         back = stretches - 1 - i
-        q = [amp[m] * (k[m] + ks_ref[base + back + 1, m]) for m in range(modes)]
+        q = [amp[m] * (k[m] + ks_ref[chunk, back + 1, pl.ds(m * members, members), :]) for m in range(modes)]
         for t in range(STRETCH):
             row = back * STRETCH + STRETCH - 1 - t
             zo_ref[pl.ds(row * members, members), :] = z_ref[pl.ds((base * STRETCH + row) * members, members), :] + total(q)
@@ -466,6 +522,7 @@
     work = tokens * channels * modes
     index = lax.axis_index("ctx")
     core = index % SETS
+    side = (index // SETS) % 2
     me = index.astype(jnp.int32).reshape(1)
 
     def shape(*dims, dtype=F32):
@@ -473,7 +530,19 @@
 
     half = shape(2, members, tokens, LANES, dtype=BF16)
     series = shape(length * members, LANES)
+    half_series = shape(tokens * members, LANES)
     pieces = 4
+    pair = shape(2, rows, LANES)
+    stretches = tokens // STRETCH
+    sizes = dict(tokens=tokens, modes=modes, members=members)
+
+    def chip_states(flip, gated, gate_grad, par):
+        states = shape(2, 2, rows // 2, LANES), shape(stretches, modes, members, LANES), shape(stretches + 1, modes, members, LANES)
+        out = call(
+            functools.partial(state_kernel, flip=flip, **sizes), states + (half_series,) * 2, [SMEM] + [VMEM] * 3, work * 2
+        )(me, gated, gate_grad, par)
+        return list(out)
+
     own_gates, send_gates = call(
         functools.partial(gate_kernel, members=members, pieces=pieces),
         (half, half),
@@ -492,12 +561,16 @@
             got_gates = exchange(send_gates, 1, count)
             gated, gate_grad, lags = call(
                 functools.partial(series_kernel, tokens=tokens, members=members),
-                (series, series, shape(STRETCH, members, LANES)),
+                (shape(2, tokens * members, LANES),) * 2 + (shape(2, STRETCH, members, LANES),),
                 [SMEM] + [VMEM] * 2,
                 work,
             )(me, own_gates, got_gates)
-        if axis == 2:
+        if axis == 1:
             other, gated, gate_grad, lags = tie(other, gated, gate_grad, lags)
+        if tree and distance == SETS:
+            par_own, par_far = (a.reshape(rows, LANES) for a in (params, other))
+            states_own = chip_states(False, gated, gate_grad, par_own)
+            par_far, states_own[0] = tie(par_far, states_own[0])
         upper = (index // distance) % 2 == 1
         params = jnp.stack([jnp.where(upper, other, params), jnp.where(upper, params, other)], axis=axis)
         distance //= 2
@@ -507,30 +580,35 @@
     else:
         params = params.reshape((count,) + own.shape).transpose(1, 2, 0, 3).reshape(2, modes, members, SETS, LANES)
         params = lax.dynamic_index_in_dim(params, core, 3, keepdims=False).transpose(2, 0, 1, 3)
+        halves = params.reshape(members // 2, 2, 2, modes, LANES)
+        par_own, par_far = (
+            lax.dynamic_index_in_dim(halves, s, 1, keepdims=False).reshape(rows, LANES) for s in (side, 1 - side)
+        )
+        states_own = chip_states(False, gated, gate_grad, par_own)
     par = params.reshape(members * 2 * modes, LANES)
 
-    stretches = length // STRETCH
-    pair = shape(2, rows, LANES)
-    sk, hs, ks, x_weighted, g_weighted = call(
-        functools.partial(state_kernel, length=length, modes=modes, members=members),
-        (pair, shape(stretches, modes, members, LANES), shape(stretches + 1, modes, members, LANES), series, series),
-        [VMEM] * 3,
-        work * 4,
-    )(gated, gate_grad, par)
+    sk_far, hs_far, ks_far, *weighted_far = chip_states(True, gated, gate_grad, par_far)
+    sk_own, hs_own, ks_own, *weighted_own = states_own
 
     def message_shape(span):
         return shape(rows * (1 if span == top else 2) + (4 * rows // span if tree else 0), LANES, dtype=BF16)
 
-    sums, message, *kept = call(
-        functools.partial(
-            sums_kernel, length=length, modes=modes, members=members, part=min(4, modes), unroll=4, last=top == SETS, tree=tree
-        ),
-        (shape(4, rows, LANES), message_shape(SETS)) + ((shape(4, rows // 2, LANES),) if tree else ()),
-        [SMEM] + [VMEM] * 7,
-        work * 6,
-    )(me, x_weighted, g_weighted, lags, hs, ks, sk, par)
-
-    tot, enter, span = sk, sk, SETS
+    def chip_sums(flip, outs, weighted, hs, ks, sk, *par):
+        return call(
+            functools.partial(sums_kernel, part=min(4, modes), unroll=4, flip=flip, last=top == SETS, tree=tree, **sizes),
+            (shape(4, rows // 2, LANES),) + outs,
+            [SMEM] + [VMEM] * (6 + len(par)),
+            work * 3,
+            scratch=(pltpu.VMEM((4, 2, rows // 2, LANES), F32),),
+        )(me, *weighted, lags, hs, ks, sk, *par)
+
+    sums_far, tot, message = chip_sums(
+        True, (pair, message_shape(SETS)), weighted_far, hs_far, ks_far, sk_far, par_far, sk_own, par_own
+    )
+    tot, weighted_own[0] = tie(tot, weighted_own[0])
+    (sums_own,) = chip_sums(False, (), weighted_own, hs_own, ks_own, sk_own, par_own)
+
+    enter, span, pair_tot, kept = tot, SETS, tot, [sums_own] if tree else []
     while span < top:
         got = exchange(message, span, count)
         last = span * 2 == top
@@ -541,15 +619,20 @@
             rows,
         )(me, tot, got, enter, par, *kept)
         if span == SETS:
-            tot, gated, gate_grad = tie(tot, gated, gate_grad)
+            tot, hs_own, gated, gate_grad = tie(tot, hs_own, gated, gate_grad)
         span *= 2
     far = exchange(message, top, count)
-    y, z = call(
-        functools.partial(taps_kernel, length=length, modes=modes, members=members), (series, series), [VMEM] * 3, work
-    )(gated, gate_grad, par)
+    hs, ks = call(
+        functools.partial(order_kernel, **sizes),
+        (shape(2, stretches, modes * members, LANES), shape(2, stretches + 1, modes * members, LANES)),
+        [SMEM] + [VMEM] * 4,
+        work,
+    )(me, hs_own, ks_own, hs_far, ks_far)
+    y, z = call(functools.partial(taps_kernel, **sizes), (series, series), [VMEM] * 3, work)(gated, gate_grad, par)
+    far, y, hs = tie(far, y, hs)
     (states_in,) = call(
-        functools.partial(enter_kernel, tokens=tokens, modes=modes, members=members, span=top), (pair,), [SMEM] + [VMEM] * 3, rows
-    )(me, enter, far, par)
+        functools.partial(enter_kernel, span=top, **sizes), (shape(2, 2, rows, LANES),), [SMEM] + [VMEM] * 5, rows
+    )(me, enter, far, par, sk_own, sk_far)
 
     scratch = (pltpu.VMEM((tokens * members, LANES), F32),) * 2
     finish = functools.partial(finish_kernel, tokens=tokens, modes=modes, members=members)
@@ -579,9 +662,11 @@
         residue_grad, log_grad = out[6].T, out[7].T
     else:
         dims = (members, modes, LANES)
-        h_in, k_in = (a.reshape(dims) for a in states_in)
-        s, k = (a.reshape(dims) for a in sk)
-        r, d, s_d, k_d = (a.reshape(dims) for a in sums)
+        h_in, k_in = states_in[0, 0].reshape(dims), states_in[1, 1].reshape(dims)
+        s, k = (a.reshape(dims) for a in pair_tot)
+        own_half, far_half = (a.reshape(4, members // 2, modes, LANES) for a in (sums_own, sums_far))
+        ordered = jnp.where(side == 0, jnp.stack([own_half, far_half], 2), jnp.stack([far_half, own_half], 2))
+        r, d, s_d, k_d = ordered.reshape((4,) + dims)
         rate = params[:, 0]
         w = jnp.exp(-rate)
         r = r + w * h_in * k

time: 43.7 us -> 40.8 us (0.934)
  waiting for transfers between devices: 12.8 us -> 8.3 us
  Pallas kernels: 15.6 us -> 17.3 us
    ppermute x8, waiting for transfers between devices: 12.8 us -> 8.3 us  [exchange(): return lax.ppermute(value, 'ctx', [(i, i ^ distance) for i in range(count)])]
    pallas_call x4 -> x7, Pallas kernels: 7.39 us -> 9 us  [the longest x2 4.29 us: chip_sums(): call(functools.partial(sums_kernel, part=min(4, modes), unroll=4, flip=fl...]
  transfers between devices with their start and end apart: 8 -> 8, of which waited for: 5 -> 6; matrix products, arithmetic and copies ran while one was open for 0% -> 0% of each run, Pallas kernels for 13% -> 25%
where the time goes in v4:
time: 40.8 us; the launch traced here: 40.4 us
  Pallas kernels  17.3 us (42%)
  starting transfers between devices  13.2 us (32%)
  waiting for transfers between devices  8.3 us (20%)
  between operations  0.87 us (2%)
  other arithmetic  0.77 us (2%)
    ppermute x8, starting transfers between devices, exchange(): return lax.ppermute(value, 'ctx', [(i, i ^ distance) for i in range(count)])  13.2 us
    ppermute x8, waiting for transfers between devices, exchange(): return lax.ppermute(value, 'ctx', [(i, i ^ distance) for i in range(count)])  8.3 us
    pallas_call x2, Pallas kernels, chip_sums(): call(functools.partial(sums_kernel, part=min(4, modes), unroll=4, flip=fl...  4.29 us
    pallas_call x2, Pallas kernels, chip_states(): call(functools.partial(state_kernel, flip=flip, **sizes), states + (half_...  2.54 us
    pallas_call x1, Pallas kernels, local(): call(functools.partial(finish, own=True), grads, [SMEM] + [VMEM] * 9, wor...  1.98 us
    pallas_call x1, Pallas kernels, local(): call(functools.partial(gate_kernel, members=members, pieces=pieces), (hal...  1.87 us
    pallas_call x1, Pallas kernels, local(): call(functools.partial(finish, own=False), (half,), [SMEM] + [VMEM] * 6,...  1.78 us
    pallas_call x1, Pallas kernels, local(): call(functools.partial(last_kernel, tokens=tokens, modes=modes, members=m...  1.44 us
  transfers between devices with their start and end apart: 8, of which 6 were waited for; matrix products, arithmetic and copies ran while one was open for 0% of the time, Pallas kernels for 25%

profile of v4, /device:TPU:0, one launch (start us, length us, event | category | flops | bytes accessed | tf_op | source)
XLA Modules:
  0.0 40.4 jit_solution(6128087132977488485)
XLA Ops:
  0.6 0.7 %pad_maximum_fusion.3.refs_3_ = f32[2,16,128]{2,1,0:T(8,128)S(1)} fusion(f32[1,16,128]{2,1,0:T(8,128)} %bitcast.35, f32[1,16,128]{2,1,0:T(8,128)} %bitcast.36), kind=kLoop, calls=%fused_computation.7 | loop fusion | flops 4096 | bytes 32768 | tf_op jit(solution)/shard_map/stack | solution.py:554
  1.3 4.0 %collective-permute-start = (f32[2,16,128]{2,1,0:T(8,128)S(1)}, f32[2,16,128]{2,1,0:T(8,128)S(1)}, u32[]{:S(2)}, u32[]{:S(2)}) collective-permute-start(f32[2,16,128]{2,1,0:T(8,128)S(1)} %pad_maximum_fusion.3.refs_3_), channel_id=1, source_target_pairs={{0,16},{2,18},{4,20},{6,22},{8,24},{10,26},{12,28},{14,30},{16,0},... | collective-permute-start | bytes 49160 | tf_op jit(solution)/shard_map/ppermute | solution.py:505
  5.4 1.9 %shard_map.101 = (bf16[2,8,128,128]{3,2,1,0:T(8,128)(2,1)S(1)}, bf16[2,8,128,128]{3,2,1,0:T(8,128)(2,1)S(1)}) custom-call(s32[1]{0:T(128)} %bitcast.me_ref, bf16[128,2048]{1,0:T(8,128)(2,1)} %q_hbm.1, bf16[128,2048]{1,0:T(8,128)(2,1)} %k_ref.1, bf16[128,2048]{1,0:T(8,128)(2,1)} %v_ref.1, bf16[128,2048]{1,0:T(8,128)(2,1)} %u_ref.1), custom_call_target="tpu_custom_call" | custom-call | flops 4194304 | bytes 1048576 | tf_op jit(solution)/shard_map/pallas_call | solution.py:546
  7.3 0.0 collective-permute-done
  7.3 0.1 collective-permute-start.2
  7.4 1.7 %collective-permute-start.1 = (f32[2,2,16,128]{3,2,1,0:T(8,128)S(1)}, f32[2,2,16,128]{3,2,1,0:T(8,128)S(1)}, u32[]{:S(2)}, u32[]{:S(2)}) collective-permute-start(f32[2,2,16,128]{3,2,1,0:T(8,128)S(1)} %pad_maximum_fusion.2), channel_id=1, source_target_pairs={{0,8},{2,10},{4,12},{6,14},{8,0},{10,2},{12,4},{14,6},{16,24},{18,... | collective-permute-start | bytes 98312 | tf_op jit(solution)/shard_map/ppermute | solution.py:505
  9.1 0.2 collective-permute-done.2.got_ref
  9.3 1.0 %shard_map.102 = (f32[2,1024,128]{2,1,0:T(8,128)S(1)}, f32[2,1024,128]{2,1,0:T(8,128)S(1)}, f32[2,8,8,128]{3,2,1,0:T(8,128)S(1)}) custom-call(s32[1]{0:T(128)} %bitcast.me_ref, bf16[2,8,128,128]{3,2,1,0:T(8,128)(2,1)S(1)} %get-tuple-element.63.own_ref, bf16[2,8,128,128]{3,2,1,0:T(8,128)(2,1)S(1)} %collective-permute-done.2.got_ref), custom_call_target="tpu_custom_call" | custom-call | flops 4194304 | bytes 1048576 | tf_op jit(solution)/shard_map/pallas_call | solution.py:562
  10.2 1.2 %collective-permute-done.1 = f32[2,2,16,128]{3,2,1,0:T(8,128)S(1)} collective-permute-done((f32[2,2,16,128]{3,2,1,0:T(8,128)S(1)}, f32[2,2,16,128]{3,2,1,0:T(8,128)S(1)}, u32[]{:S(2)}, u32[]{:S(2)}) %collective-permute-start.1) | collective-permute-done | bytes 32800 | tf_op jit(solution)/shard_map/ppermute | solution.py:505
  11.4 1.7 %collective-permute-start.3 = (f32[2,2,2,16,128]{4,3,2,0,1:T(8,128)S(1)}, f32[2,2,2,16,128]{4,3,2,0,1:T(8,128)S(1)}, u32[]{:S(2)}, u32[]{:S(2)}) collective-permute-start(f32[2,2,2,16,128]{4,3,2,0,1:T(8,128)S(1)} %pad_maximum_fusion.1), channel_id=1, source_target_pairs={{0,4},{2,6},{4,0},{6,2},{8,12},{10,14},{12,8},{14,10},{16,20},{18,... | collective-permute-start | bytes 196616 | tf_op jit(solution)/shard_map/ppermute | solution.py:505
  13.1 1.3 %shard_map.103 = (f32[2,2,64,128]{3,2,1,0:T(8,128)S(1)}, f32[16,16,8,128]{3,2,1,0:T(8,128)S(1)}, f32[17,16,8,128]{3,2,1,0:T(8,128)S(1)}, f32[1024,128]{1,0:T(8,128)S(1)}, f32[1024,128]{1,0:T(8,128)S(1)}) custom-call(s32[1]{0:T(128)} %bitcast.me_ref, f32[2,1024,128]{2,1,0:T(8,128)S(1)} %get-tuple-element.94.x_ref, ...), custom_call_target="tpu_custom_call" | custom-call | flops 8388608 | bytes 1048576 | tf_op jit(solution)/shard_map/pallas_call | solution.py:541
  14.4 1.4 %collective-permute-done.3 = f32[2,2,2,16,128]{4,3,2,0,1:T(8,128)S(1)} collective-permute-done((f32[2,2,2,16,128]{4,3,2,0,1:T(8,128)S(1)}, f32[2,2,2,16,128]{4,3,2,0,1:T(8,128)S(1)}, u32[]{:S(2)}, u32[]{:S(2)}) %collective-permute-start.3) | collective-permute-done | bytes 65568 | tf_op jit(solution)/shard_map/ppermute | solution.py:505
  15.8 1.3 %shard_map.104 = (f32[2,2,64,128]{3,2,1,0:T(8,128)S(1)}, f32[16,16,8,128]{3,2,1,0:T(8,128)S(1)}, f32[17,16,8,128]{3,2,1,0:T(8,128)S(1)}, f32[1024,128]{1,0:T(8,128)S(1)}, f32[1024,128]{1,0:T(8,128)S(1)}) custom-call(s32[1]{0:T(128)} %bitcast.me_ref, f32[2,1024,128]{2,1,0:T(8,128)S(1)} %get-tuple-element.94.x_ref, ...), custom_call_target="tpu_custom_call" | custom-call | flops 8388608 | bytes 1048576 | tf_op jit(solution)/shard_map/pallas_call | solution.py:541
  17.0 2.5 %shard_map.105 = (f32[4,64,128]{2,1,0:T(8,128)}, f32[2,128,128]{2,1,0:T(8,128)S(1)}, bf16[512,128]{1,0:T(8,128)(2,1)S(1)}) custom-call(s32[1]{0:T(128)} %bitcast.me_ref, f32[1024,128]{1,0:T(8,128)S(1)} %get-tuple-element.73.x_ref, f32[1024,128]{1,0:T(8,128)S(1)} %get-tuple-element.74.g_ref, f32[2,8,8,128]{3,2,1,0:T(8,128)S(1)} %get-tuple-element.75.lag_ref, ...), custom_call_target="tpu_custom_call" | custom-call | flops 12582912 | bytes 1048576 | tf_op jit(solution)/shard_map/pallas_call | solution.py:597
  19.5 1.6 %collective-permute-start.4 = (bf16[512,128]{1,0:T(8,128)(2,1)S(1)}, bf16[512,128]{1,0:T(8,128)(2,1)S(1)}, u32[]{:S(2)}, u32[]{:S(2)}) collective-permute-start(bf16[512,128]{1,0:T(8,128)(2,1)S(1)} %get-tuple-element.83), channel_id=1, source_target_pairs={{0,4},{2,6},{4,0},{6,2},{8,12},{10,14},{12,8},{14,10},{16,20},{18,... | collective-permute-start | bytes 393224 | tf_op jit(solution)/shard_map/ppermute | solution.py:505
  21.2 1.8 %shard_map.106.refs_0_ = f32[4,64,128]{2,1,0:T(8,128)S(1)} custom-call(s32[1]{0:T(128)} %bitcast.me_ref, f32[1024,128]{1,0:T(8,128)S(1)} %get-tuple-element.84.x_ref, f32[1024,128]{1,0:T(8,128)S(1)} %get-tuple-element.85.g_ref, f32[2,8,8,128]{3,2,1,0:T(8,128)S(1)} %get-tuple-element.75.lag_ref, f32[16,16,8,128]{3,2,1,0:T(8,128)S(1)} %get-tuple-element.97.hs_ref.hs_own, ...), custom_call_target="tpu_custom_call" | custom-call | flops 12582912 | bytes 1048576 | tf_op jit(solution)/shard_map/pallas_call | solution.py:597
  23.0 1.5 %collective-permute-done.4.got_ref = bf16[512,128]{1,0:T(8,128)(2,1)S(1)} collective-permute-done((bf16[512,128]{1,0:T(8,128)(2,1)S(1)}, bf16[512,128]{1,0:T(8,128)(2,1)S(1)}, u32[]{:S(2)}, u32[]{:S(2)}) %collective-permute-start.4) | collective-permute-done | bytes 131104 | tf_op jit(solution)/shard_map/ppermute | solution.py:505
  24.5 0.1 shard_map.107
  24.6 1.7 %collective-permute-start.5 = (bf16[384,128]{1,0:T(8,128)(2,1)S(1)}, bf16[384,128]{1,0:T(8,128)(2,1)S(1)}, u32[]{:S(2)}, u32[]{:S(2)}) collective-permute-start(bf16[384,128]{1,0:T(8,128)(2,1)S(1)} %get-tuple-element.90), channel_id=1, source_target_pairs={{0,8},{2,10},{4,12},{6,14},{8,0},{10,2},{12,4},{14,6},{16,24},{18,... | collective-permute-start | bytes 294920 | tf_op jit(solution)/shard_map/ppermute | solution.py:505
  26.3 3.5 %collective-permute-done.5.got_ref = bf16[384,128]{1,0:T(8,128)(2,1)S(1)} collective-permute-done((bf16[384,128]{1,0:T(8,128)(2,1)S(1)}, bf16[384,128]{1,0:T(8,128)(2,1)S(1)}, u32[]{:S(2)}, u32[]{:S(2)}) %collective-permute-start.5) | collective-permute-done | bytes 98336 | tf_op jit(solution)/shard_map/ppermute | solution.py:505
  29.8 0.1 shard_map.108
  29.9 2.3 %collective-permute-start.6 = (bf16[192,128]{1,0:T(8,128)(2,1)S(1)}, bf16[192,128]{1,0:T(8,128)(2,1)S(1)}, u32[]{:S(2)}, u32[]{:S(2)}) collective-permute-start(bf16[192,128]{1,0:T(8,128)(2,1)S(1)} %get-tuple-element.93), channel_id=1, source_target_pairs={{0,16},{2,18},{4,20},{6,22},{8,24},{10,26},{12,28},{14,30},{16,0},... | collective-permute-start | bytes 147464 | tf_op jit(solution)/shard_map/ppermute | solution.py:505
  32.3 1.2 %shard_map.110 = (f32[2,16,128,128]{3,2,1,0:T(8,128)S(1)}, f32[2,17,128,128]{3,2,1,0:T(8,128)S(1)}) custom-call(s32[1]{0:T(128)} %bitcast.me_ref, f32[16,16,8,128]{3,2,1,0:T(8,128)S(1)} %get-tuple-element.97.hs_ref.hs_own, f32[17,16,8,128]{3,2,1,0:T(8,128)S(1)} %get-tuple-element.87.ks_ref.ks_own, f32[16,16,8,128]{3,2,1,0:T(8,128)S(1)} %get-tuple-element.76.hs_ref.hs_far, ...), custom_call_target="tpu_custom_call" | custom-call | flops 4194304 | bytes 1048576 | tf_op jit(solution)/shard_map/pallas_call | solution.py:625
  33.5 0.9 %shard_map.109 = (f32[2048,128]{1,0:T(8,128)S(1)}, f32[2048,128]{1,0:T(8,128)S(1)}) custom-call(f32[2,1024,128]{2,1,0:T(8,128)S(1)} %get-tuple-element.94.x_ref, f32[2,1024,128]{2,1,0:T(8,128)S(1)} %get-tuple-element.95.g_ref, f32[256,128]{1,0:T(8,128)S(1)} %bitcast.26), custom_call_target="tpu_custom_call" | custom-call | flops 4194304 | bytes 1048576 | tf_op jit(solution)/shard_map/pallas_call | solution.py:631
  34.4 0.6 %collective-permute-done.6.far_ref.refs_1_ = bf16[192,128]{1,0:T(8,128)(2,1)S(1)} collective-permute-done((bf16[192,128]{1,0:T(8,128)(2,1)S(1)}, bf16[192,128]{1,0:T(8,128)(2,1)S(1)}, u32[]{:S(2)}, u32[]{:S(2)}) %collective-permute-start.6) | collective-permute-done | bytes 49184 | tf_op jit(solution)/shard_map/ppermute | solution.py:505
  35.0 0.0 copy-start
  35.1 0.0 copy-start.1
  35.1 0.0 copy-start.2
  35.1 1.8 %shard_map.112 = bf16[2,8,128,128]{3,2,1,0:T(8,128)(2,1)S(1)} custom-call(s32[1]{0:T(128)} %bitcast.me_ref, f32[2048,128]{1,0:T(8,128)S(1)} %get-tuple-element.99.y_ref, f32[2048,128]{1,0:T(8,128)S(1)} %get-tuple-element.100.z_ref, f32[2,16,128,128]{3,2,1,0:T(8,128)S(1)} %get-tuple-element.101.hs_ref, f32[2,17,128,128]{3,2,1,0:T(8,128)S(1)} %get-tuple-element.102.ks_ref, ...), custom_call_target="tpu_custom_call" | custom-call | flops 8388608 | bytes 1048576 | tf_op jit(solution)/shard_map/pallas_call | solution.py:639
  36.9 0.1 collective-permute-start.7
  37.0 0.0 copy-done
  37.0 0.0 copy-done.1
  37.0 0.0 copy-done.2
  37.0 2.0 %shard_map.113 = (bf16[128,2048]{1,0:T(8,128)(2,1)S(1)}, bf16[128,2048]{1,0:T(8,128)(2,1)S(1)}, bf16[128,2048]{1,0:T(8,128)(2,1)S(1)}) custom-call(s32[1]{0:T(128)} %bitcast.me_ref, f32[2048,128]{1,0:T(8,128)S(1)} %get-tuple-element.99.y_ref, f32[2048,128]{1,0:T(8,128)S(1)} %get-tuple-element.100.z_ref, f32[2,16,128,128]{3,2,1,0:T(8,128)S(1)} %get-tuple-element.101.hs_ref, ...), custom_call_target="tpu_custom_call" | custom-call | flops 8388608 | bytes 1048576 | tf_op jit(solution)/shard_map/pallas_call | solution.py:644
  39.0 0.0 collective-permute-done.7.got_ref
  39.0 1.4 %shard_map.114 = (bf16[128,2048]{1,0:T(8,128)(2,1)S(1)}, bf16[128,2048]{1,0:T(8,128)(2,1)S(1)}, bf16[128,2048]{1,0:T(8,128)(2,1)S(1)}, bf16[128,2048]{1,0:T(8,12...) custom-call(s32[1]{0:T(128)} %bitcast.me_ref, ...), custom_call_target="tpu_custom_call", output_to_operand_aliasing={{0}: (9, {}), {1}: (10, {}), {2}: (11, {})} | custom-call | flops 4194304 | bytes 1048576 | tf_op jit(solution)/shard_map/pallas_call | solution.py:650
  (10 shorter events, 0.1 us)
Async XLA Ops:
  1.3 5.9 %collective-permute-start = (f32[2,16,128]{2,1,0:T(8,128)S(1)}, f32[2,16,128]{2,1,0:T(8,128)S(1)}, u32[]{:S(2)}, u32[]{:S(2)}) collective-permute-start(f32[2,16,128]{2,1,0:T(8,128)S(1)} %pad_maximum_fusion.3.refs_3_), channel_id=1, source_target_pairs={{0,16},{2,18},{4,20},{6,22},{8,24},{10,26},{12,28},{14,30},{16,0},... | collective-permute-start | bytes 49160 | tf_op jit(solution)/shard_map/ppermute | solution.py:505
  7.3 2.0 %collective-permute-start.2 = (bf16[2,8,128,128]{3,2,1,0:T(8,128)(2,1)S(1)}, bf16[2,8,128,128]{3,2,1,0:T(8,128)(2,1)S(1)}, u32[]{:S(2)}, u32[]{:S(2)}) collective-permute-start(bf16[2,8,128,128]{3,2,1,0:T(8,128)(2,1)S(1)} %get-tuple-element.64), channel_id=1, source_target_pairs={{0,2},{2,0},{4,6},{6,4},{8,10},{10,8},{12,14},{14,12},{16,18},{18,... | collective-permute-start | bytes 1572872 | tf_op jit(solution)/shard_map/ppermute | solution.py:505
  7.4 4.0 %collective-permute-start.1 = (f32[2,2,16,128]{3,2,1,0:T(8,128)S(1)}, f32[2,2,16,128]{3,2,1,0:T(8,128)S(1)}, u32[]{:S(2)}, u32[]{:S(2)}) collective-permute-start(f32[2,2,16,128]{3,2,1,0:T(8,128)S(1)} %pad_maximum_fusion.2), channel_id=1, source_target_pairs={{0,8},{2,10},{4,12},{6,14},{8,0},{10,2},{12,4},{14,6},{16,24},{18,... | collective-permute-start | bytes 98312 | tf_op jit(solution)/shard_map/ppermute | solution.py:505
  11.4 4.3 %collective-permute-start.3 = (f32[2,2,2,16,128]{4,3,2,0,1:T(8,128)S(1)}, f32[2,2,2,16,128]{4,3,2,0,1:T(8,128)S(1)}, u32[]{:S(2)}, u32[]{:S(2)}) collective-permute-start(f32[2,2,2,16,128]{4,3,2,0,1:T(8,128)S(1)} %pad_maximum_fusion.1), channel_id=1, source_target_pairs={{0,4},{2,6},{4,0},{6,2},{8,12},{10,14},{12,8},{14,10},{16,20},{18,... | collective-permute-start | bytes 196616 | tf_op jit(solution)/shard_map/ppermute | solution.py:505
  19.5 5.0 %collective-permute-start.4 = (bf16[512,128]{1,0:T(8,128)(2,1)S(1)}, bf16[512,128]{1,0:T(8,128)(2,1)S(1)}, u32[]{:S(2)}, u32[]{:S(2)}) collective-permute-start(bf16[512,128]{1,0:T(8,128)(2,1)S(1)} %get-tuple-element.83), channel_id=1, source_target_pairs={{0,4},{2,6},{4,0},{6,2},{8,12},{10,14},{12,8},{14,10},{16,20},{18,... | collective-permute-start | bytes 393224 | tf_op jit(solution)/shard_map/ppermute | solution.py:505
  24.6 5.2 %collective-permute-start.5 = (bf16[384,128]{1,0:T(8,128)(2,1)S(1)}, bf16[384,128]{1,0:T(8,128)(2,1)S(1)}, u32[]{:S(2)}, u32[]{:S(2)}) collective-permute-start(bf16[384,128]{1,0:T(8,128)(2,1)S(1)} %get-tuple-element.90), channel_id=1, source_target_pairs={{0,8},{2,10},{4,12},{6,14},{8,0},{10,2},{12,4},{14,6},{16,24},{18,... | collective-permute-start | bytes 294920 | tf_op jit(solution)/shard_map/ppermute | solution.py:505
  29.9 5.1 %collective-permute-start.6 = (bf16[192,128]{1,0:T(8,128)(2,1)S(1)}, bf16[192,128]{1,0:T(8,128)(2,1)S(1)}, u32[]{:S(2)}, u32[]{:S(2)}) collective-permute-start(bf16[192,128]{1,0:T(8,128)(2,1)S(1)} %get-tuple-element.93), channel_id=1, source_target_pairs={{0,16},{2,18},{4,20},{6,22},{8,24},{10,26},{12,28},{14,30},{16,0},... | collective-permute-start | bytes 147464 | tf_op jit(solution)/shard_map/ppermute | solution.py:505
  35.0 1.9 %copy-start = (bf16[128,2048]{1,0:T(8,128)(2,1)S(1)}, bf16[128,2048]{1,0:T(8,128)(2,1)}, u32[]{:S(2)}) copy-start(bf16[128,2048]{1,0:T(8,128)(2,1)} %k_ref.1) | copy-start | bytes 1572868
  35.1 1.9 %copy-start.1 = (bf16[128,2048]{1,0:T(8,128)(2,1)S(1)}, bf16[128,2048]{1,0:T(8,128)(2,1)}, u32[]{:S(2)}) copy-start(bf16[128,2048]{1,0:T(8,128)(2,1)} %v_ref.1) | copy-start | bytes 1572868
  35.1 1.9 %copy-start.2 = (bf16[128,2048]{1,0:T(8,128)(2,1)S(1)}, bf16[128,2048]{1,0:T(8,128)(2,1)}, u32[]{:S(2)}) copy-start(bf16[128,2048]{1,0:T(8,128)(2,1)} %u_ref.1) | copy-start | bytes 1572868
  36.9 2.1 %collective-permute-start.7 = (bf16[2,8,128,128]{3,2,1,0:T(8,128)(2,1)S(1)}, bf16[2,8,128,128]{3,2,1,0:T(8,128)(2,1)S(1)}, u32[]{:S(2)}, u32[]{:S(2)}) collective-permute-start(bf16[2,8,128,128]{3,2,1,0:T(8,128)(2,1)S(1)} %shard_map.112), channel_id=1, source_target_pairs={{0,2},{2,0},{4,6},{6,4},{8,10},{10,8},{12,14},{14,12},{16,18},{18,... | collective-permute-start | bytes 1572872 | tf_op jit(solution)/shard_map/ppermute | solution.py:505

commit v5 on v4

--- a/solution.py
+++ b/solution.py
@@ -10,6 +10,8 @@
 LANES = 128
 SETS = 2
 STRETCH = 8
+WAYS = 4
+HOPS = (3, 1, 2)
 F32 = jnp.float32
 BF16 = jnp.bfloat16
 VMEM = pl.BlockSpec(memory_space=pltpu.VMEM)
@@ -90,10 +92,6 @@
     return par_ref[pl.ds(param * modes + mode, members, stride=2 * modes), :]
 
 
-def rate_block(par_ref, member, modes):
-    return par_ref[pl.ds(pl.multiple_of(member * 2 * modes, modes), modes), :]
-
-
 def half_rows(par_ref, start, stride, members):
     rows = par_ref[pl.ds(start, members // 2, stride=stride), :]
     return jnp.concatenate([rows, rows], axis=0)
@@ -102,6 +100,11 @@
 def chosen_half(me_ref, flip):
     side = (me_ref[0] // SETS) % 2
     return 1 - side if flip else side
+
+
+def ranked(me_ref, rank, members):
+    half = members // 2
+    return rank % half * 2 + chosen_half(me_ref, rank >= half)
 
 
 def state_kernel(me_ref, x_ref, g_ref, par_ref, sk_ref, hs_ref, ks_ref, xw_ref, gw_ref, *, tokens, modes, members, flip):
@@ -138,12 +141,14 @@
             sk_ref[i, 1, at, :] = value[half:]
 
 
-def taps_kernel(x_ref, g_ref, par_ref, y_ref, z_ref, *, tokens, modes, members):
+def taps_kernel(me_ref, x_ref, g_ref, par_ref, y_ref, z_ref, *, tokens, modes, members):
     half = members // 2
-    for side in range(2):
-        rate = [half_rows(par_ref, side * 2 * modes + m, 4 * modes, members) for m in range(modes)]
+    for flip in (0, 1):
+        side = chosen_half(me_ref, flip)
+        start = flip * half * 2 * modes
+        rate = [half_rows(par_ref, start + m, 2 * modes, members) for m in range(modes)]
         w = [jnp.exp(-rate[m]) for m in range(modes)]
-        power = [half_rows(par_ref, (side * 2 + 1) * modes + m, 4 * modes, members) * jnp.sqrt(rate[m]) for m in range(modes)]
+        power = [half_rows(par_ref, start + modes + m, 2 * modes, members) * jnp.sqrt(rate[m]) for m in range(modes)]
         taps = []
         for j in range(STRETCH):
             taps.append(total(power))
@@ -157,7 +162,7 @@
                 y = total([taps[j] * x[t - j] for j in range(t + 1)])
                 z = total([taps[j] * g[t + j] for j in range(STRETCH - t)])
                 for chunk in range(2):
-                    to = pl.ds((chunk * tokens + i * STRETCH + t) * members + side, half, stride=2)
+                    to = pl.ds((chunk * tokens + i * STRETCH + t) * members + flip * half, half)
                     y_ref[to, :] = y[chunk * half : (chunk + 1) * half]
                     z_ref[to, :] = z[chunk * half : (chunk + 1) * half]
             return 0
@@ -165,16 +170,15 @@
         lax.fori_loop(0, tokens // STRETCH, within, 0, unroll=2)
 
 
-def order_kernel(me_ref, hs_own, ks_own, hs_far, ks_far, hs_ref, ks_ref, *, tokens, modes, members):
+def order_kernel(hs_own, ks_own, hs_far, ks_far, hs_ref, ks_ref, *, tokens, modes, members):
     half = members // 2
     for src, out, count in ((0, hs_ref, tokens // STRETCH), (1, ks_ref, tokens // STRETCH + 1)):
 
         def body(i, _):
-            for flip, ref in ((False, (hs_own, ks_own)[src]), (True, (hs_far, ks_far)[src])):
-                side = chosen_half(me_ref, flip)
+            for flip, ref in ((0, (hs_own, ks_own)[src]), (1, (hs_far, ks_far)[src])):
                 for m in range(modes):
                     for chunk in range(2):
-                        out[chunk, i, pl.ds(m * members + side, half, stride=2), :] = ref[i, m, chunk * half : (chunk + 1) * half, :]
+                        out[chunk, i, pl.ds(m * members + flip * half, half), :] = ref[i, m, chunk * half : (chunk + 1) * half, :]
             return 0
 
         lax.fori_loop(0, count, body, 0)
@@ -185,26 +189,26 @@
     return bit, 1.0 - bit
 
 
-def put_states(ref, me, span, at, at_k, s, k, last):
+def put_states(refs, me, span, at, at_k, s, k, last):
     if last:
-        earlier, later = flags((me // span) % 2 == 1)
-        ref[at, :] = (earlier * k + later * s).astype(BF16)
+        place = me // span
+        for hop, ref in zip(HOPS, refs):
+            earlier, later = flags((place ^ hop) < place)
+            ref[at, :] = (earlier * k + later * s).astype(BF16)
     else:
-        ref[at, :] = s.astype(BF16)
-        ref[at_k, :] = k.astype(BF16)
-
-
-def blocks(member, modes, members):
-    if isinstance(member, int):
-        return pl.ds(member * modes, modes), pl.ds((members + member) * modes, modes)
-    return tuple(pl.ds(pl.multiple_of(m * modes, modes), modes) for m in (member, members + member))
-
-
-def sums_kernel(me_ref, x_ref, g_ref, lag_ref, hs_ref, ks_ref, sk_ref, par_ref, *refs, tokens, modes, members, part, unroll, flip, last, tree):
+        refs[0][at, :] = s.astype(BF16)
+        refs[0][at_k, :] = k.astype(BF16)
+
+
+def blocks(rank, modes, members):
+    return pl.ds(rank * modes, modes), pl.ds((members + rank) * modes, modes)
+
+
+def sums_kernel(me_ref, x_ref, g_ref, lag_ref, hs_ref, ks_ref, sk_ref, par_ref, *refs, tokens, modes, members, part, unroll, flip, tree):
     if flip:
-        sk_own, par_own, sums_ref, tot_ref, message_ref, work_ref = refs
+        sk_own, par_own, *sums_ref, tot_ref, message_ref, work_ref = refs
     else:
-        sums_ref, work_ref = refs
+        *sums_ref, work_ref = refs
     side = chosen_half(me_ref, flip)
     half = members // 2
     stretches = tokens // STRETCH
@@ -267,19 +271,19 @@
         left, right = (tuple(work_ref[i, c, at, :] for i in range(4)) + (sk_ref[0, c, at, :], sk_ref[1, c, at, :]) for c in range(2))
         rate = par_ref[pl.ds(z * 2 * modes, modes), :]
         for i, value in enumerate(join(rate, left, right, float(tokens))):
-            sums_ref[i, at, :] = value
+            for ref in sums_ref:
+                ref[i, at, :] = value
             if flip and tree:
-                offset = rows * (1 if last else 2)
-                message_ref[pl.ds(offset + (i * half + z) * modes, modes), :] = value.astype(BF16)
+                message_ref[pl.ds(rows * 2 + (i * half + z) * modes, modes), :] = value.astype(BF16)
         if flip:
-            for ref, member, par in ((sk_ref, z * 2 + side, par_ref), (sk_own, z * 2 + 1 - side, par_own)):
+            for ref, rank, par in ((sk_ref, half + z, par_ref), (sk_own, z, par_own)):
                 fade = jnp.exp(par[pl.ds(z * 2 * modes, modes), :] * -float(tokens))
                 s = fade * ref[0, 0, at, :] + ref[0, 1, at, :]
                 k = ref[1, 0, at, :] + fade * ref[1, 1, at, :]
-                to, to_k = blocks(member, modes, members)
+                to, to_k = blocks(rank, modes, members)
                 tot_ref[0, to, :] = s
                 tot_ref[1, to, :] = k
-                put_states(message_ref, me, SETS, to, to_k, s, k, last)
+                put_states([message_ref], me, SETS, to, to_k, s, k, False)
 
 
 def join(rate, left, right, length):
@@ -297,27 +301,36 @@
 def level_kernel(
     me_ref, tot_ref, got_ref, enter_ref, par_ref, *refs, tokens, modes, members, span, last, tree
 ):
+    refs = list(refs)
     if tree:
-        kept_ref, out_ref, new_ref, message_ref, keep_ref = refs
-    else:
-        out_ref, new_ref, message_ref = refs
+        kept_ref, work_ref, keep_ref = refs.pop(0), refs.pop(), refs.pop()
+    out_ref = None if last else refs.pop(0)
+    new_ref, *messages = refs
     me = me_ref[0]
     second = (me // span) % 2
     earlier, later = flags(second == 1)
     inside = (me // 2) % (span // 2) * 2
     gap = earlier * inside.astype(F32) + later * (span - 2 - inside).astype(F32)
     rows = members * modes
-    for member in range(members):
-        at = pl.ds(member * modes, modes)
-        rate = rate_block(par_ref, member, modes)
+    half = members // 2
+
+    def received(rank):
+        at, at_k = blocks((rank + half) % members if span == 2 else rank, modes, members)
+        return got_ref[at, :].astype(F32), got_ref[at_k, :].astype(F32)
+
+    sums = []
+    for rank in range(members):
+        at, at_k = blocks(rank, modes, members)
+        rate = par_ref[pl.ds(rank * 2 * modes, modes), :]
         far = jnp.exp(rate * -float(tokens * span))
         weight = jnp.exp(rate * (gap * -float(tokens)))
         s, k = tot_ref[0, at, :], tot_ref[1, at, :]
-        gs, gk = got_ref[at, :].astype(F32), got_ref[pl.ds(rows + member * modes, modes), :].astype(F32)
+        gs, gk = received(rank)
         s_sum = earlier * (far * gs + s) + later * (far * s + gs)
         k_sum = earlier * (gk + far * k) + later * (k + far * gk)
-        out_ref[0, at, :] = s_sum
-        out_ref[1, at, :] = k_sum
+        if not last:
+            out_ref[0, at, :] = s_sum
+            out_ref[1, at, :] = k_sum
         before = earlier * (weight * gs)
         after = later * (weight * gk)
         if span > 2:
@@ -325,50 +338,46 @@
             after += enter_ref[1, at, :]
         new_ref[0, at, :] = before
         new_ref[1, at, :] = after
-        put_states(message_ref, me, span * 2, *blocks(member, modes, members), s_sum, k_sum, last)
-    if not tree:
-        return
-    side = (me // (span * 2)) % 2
-    own = (me // 2) % span
-    count = members // span
-    offset = rows * (1 if last else 2)
-    for parity in (0, 1):
-        for to in range(count // 2):
-            index = to * 2 + (side if parity == 0 else 1 - side)
-            member = index * span + own
-            src = pl.ds(pl.multiple_of(index * modes, modes), modes)
-            at = pl.ds(pl.multiple_of(member * modes, modes), modes)
-            at_k = pl.ds(pl.multiple_of((members + member) * modes, modes), modes)
-            mine = tuple(kept_ref[i, src, :] for i in range(4)) + (tot_ref[0, at, :], tot_ref[1, at, :])
-            theirs = tuple(
-                got_ref[pl.ds(pl.multiple_of(rows * 2 + (i * count + index) * modes, modes), modes), :].astype(F32) for i in range(4)
-            ) + (got_ref[at, :].astype(F32), got_ref[at_k, :].astype(F32))
+        put_states(messages, me, span * 2, at, at_k, s_sum, k_sum, last)
+        if tree and span == 2 and rank < half:
+            block = pl.ds(rank * modes, modes)
+            mine = tuple(kept_ref[i, block, :] for i in range(4)) + (s, k)
+            theirs = tuple(got_ref[pl.ds(rows * 2 + (i * half + rank) * modes, modes), :].astype(F32) for i in range(4)) + (gs, gk)
             left = tuple(earlier * b + later * a for a, b in zip(mine, theirs))
             right = tuple(earlier * a + later * b for a, b in zip(mine, theirs))
-            for i, value in enumerate(join(rate_block(par_ref, member, modes), left, right, float(tokens * span))):
-                if parity == 0:
-                    keep_ref[i, pl.ds(to * modes, modes), :] = value
-                else:
-                    message_ref[pl.ds(offset + (i * (count // 2) + to) * modes, modes), :] = value.astype(BF16)
-
-
-def enter_kernel(me_ref, enter_ref, far_ref, par_ref, sk_own, sk_far, in_ref, *, tokens, modes, members, span):
+            for i, value in enumerate(join(rate, left, right, float(tokens * span)) + (s_sum, k_sum)):
+                work_ref[rank, i] = value
+    if tree:
+        place = me // (span * 2)
+        keep_ref[...] = work_ref[place]
+        for hop, ref in zip(HOPS, messages):
+            for i in range(6):
+                ref[pl.ds(rows + i * modes, modes), :] = work_ref[place ^ hop, i].astype(BF16)
+
+
+def enter_kernel(me_ref, enter_ref, a_ref, b_ref, c_ref, par_ref, sk_own, sk_far, in_ref, *, tokens, modes, members, span):
     me = me_ref[0]
-    earlier, later = flags((me // span) % 2 == 1)
+    place = me // span
     inside = (me // 2) % (span // 2) * 2
-    gap = earlier * inside.astype(F32) + later * (span - 2 - inside).astype(F32)
-    for ref, flip in ((sk_own, False), (sk_far, True)):
-        side = chosen_half(me_ref, flip)
+    partners = []
+    for hop, ref in zip(HOPS, (a_ref, b_ref, c_ref)):
+        partner = place ^ hop
+        earlier, later = flags(partner < place)
+        gap = earlier * (span * (place - partner - 1) + inside).astype(F32)
+        gap += later * (span * (partner - place - 1) + (span - 2 - inside)).astype(F32)
+        partners.append((ref, earlier, later, gap * -float(tokens)))
+    for ref, flip in ((sk_own, 0), (sk_far, 1)):
         for z in range(members // 2):
             src = pl.ds(z * modes, modes)
-            at, _ = blocks(z * 2 + side, modes, members)
-            rate = rate_block(par_ref, z * 2 + side, modes)
-            value = jnp.exp(rate * (gap * -float(tokens))) * far_ref[at, :].astype(F32)
+            rank = flip * (members // 2) + z
+            at, _ = blocks(rank, modes, members)
+            rate = par_ref[pl.ds(rank * 2 * modes, modes), :]
+            before, after = enter_ref[0, at, :], enter_ref[1, at, :]
+            for got_ref, earlier, later, gap in partners:
+                value = jnp.exp(rate * gap) * got_ref[at, :].astype(F32)
+                before += earlier * value
+                after += later * value
             fade = jnp.exp(rate * -float(tokens))
-            before, after = earlier * value, later * value
-            if span > 2:
-                before += enter_ref[0, at, :]
-                after += enter_ref[1, at, :]
             in_ref[0, 0, at, :] = before
             in_ref[0, 1, at, :] = ref[1, 1, src, :] + fade * after
             in_ref[1, 0, at, :] = ref[0, 0, src, :] + fade * before
@@ -419,14 +428,14 @@
 
     def store_y(rows, member, value):
         if own:
-            cols = set_columns(member, core)
+            cols = set_columns(ranked(me_ref, member, members), core)
             dq_ref[rows, cols] = (u_ref[rows, cols].astype(F32) * value.astype(F32)).astype(BF16)
         else:
             send_ref[0, member, rows, :] = value
 
     def store_z(rows, member, value):
         if own:
-            cols = set_columns(member, core)
+            cols = set_columns(ranked(me_ref, member, members), core)
             value = value.astype(F32)
             dk_ref[rows, cols] = (value * v_ref[rows, cols].astype(F32)).astype(BF16)
             dv_ref[rows, cols] = (value * k_ref[rows, cols].astype(F32)).astype(BF16)
@@ -442,28 +451,30 @@
 def last_kernel(me_ref, got_ref, k_ref, v_ref, u_ref, *refs, tokens, modes, members, span, scale, tree):
     refs = list(refs)
     if tree:
-        kept_ref, far_ref, tot_ref, own_ref = refs[:4]
-        refs = refs[4:]
+        kept_ref, a_ref, b_ref, c_ref, own_ref = refs[:5]
+        refs = refs[5:]
     dq_ref, dk_ref, dv_ref, dq_hbm, dk_hbm, dv_hbm = refs[3:9]
     me = me_ref[0]
     core = me % SETS
     copies = []
     if tree:
-        r_hbm, log_hbm, sems, par_sems, out_ref = refs[9:]
-        earlier, later = flags((me // span) % 2 == 1)
-        at = pl.ds(pl.multiple_of(me // 2 * modes, modes), modes)
-        rows = members * modes
-        r_m, d_m, sd_m, kd_m = (kept_ref[i] for i in range(4))
-        r_t, d_t, sd_t, kd_t = (far_ref[pl.ds(rows + i * modes, modes), :].astype(F32) for i in range(4))
-        far = far_ref[at, :].astype(F32)
-        s_a = earlier * far + later * tot_ref[0, at, :]
-        k_b = earlier * tot_ref[1, at, :] + later * far
-        sd_a = earlier * sd_t + later * sd_m
-        kd_b = earlier * kd_m + later * kd_t
+        r_hbm, log_hbm, sems, par_sems, out_ref, group_ref = refs[9:]
+        place = me // span
+        group_ref[place] = kept_ref[...]
+        for hop, ref in zip(HOPS, (a_ref, b_ref, c_ref)):
+            for i in range(6):
+                group_ref[place ^ hop, i] = ref[pl.ds((members + i) * modes, modes), :].astype(F32)
         rate, residue = own_ref[0], own_ref[1]
         w = jnp.exp(-rate)
-        r = r_m + r_t + w * (s_a * k_b)
-        d = d_m + d_t + w * (s_a * kd_b + (sd_a + s_a) * k_b)
+        width = float(tokens * span)
+        fade = jnp.exp(rate * -width)
+        r, d, sd, _, s, _ = (group_ref[0, i] for i in range(6))
+        for z in range(1, WAYS):
+            r_b, d_b, sd_b, kd_b, s_b, k_b = (group_ref[z, i] for i in range(6))
+            r = r + r_b + w * (s * k_b)
+            d = d + d_b + w * (s * kd_b + (sd + s) * k_b)
+            sd = fade * (sd + width * s) + sd_b
+            s = fade * s + s_b
         root = jnp.sqrt(rate) * scale
         out_ref[0] = root * r
         out_ref[1] = root * residue * (0.5 * r - rate * d)
@@ -475,7 +486,7 @@
     for tile in range(tokens // 16):
         rows = pl.ds(tile * 16, 16)
         for member in range(members):
-            cols = set_columns(member, 1 - core)
+            cols = set_columns(ranked(me_ref, member, members), 1 - core)
             y = got_ref[0, member, rows, :].astype(F32)
             z = got_ref[1, member, rows, :].astype(F32)
             dq_ref[rows, cols] = (u_ref[rows, cols].astype(F32) * y).astype(BF16)
@@ -517,8 +528,8 @@
     members = groups // SETS
     rows = members * modes
     length = tokens * SETS
-    top = count // 2
-    tree = groups == count and own_channels == LANES and top > SETS
+    top = count // WAYS
+    tree = groups == count == SETS * 2 * WAYS and own_channels == LANES
     work = tokens * channels * modes
     index = lax.axis_index("ctx")
     core = index % SETS
@@ -571,13 +582,12 @@
             par_own, par_far = (a.reshape(rows, LANES) for a in (params, other))
             states_own = chip_states(False, gated, gate_grad, par_own)
             par_far, states_own[0] = tie(par_far, states_own[0])
+            break
         upper = (index // distance) % 2 == 1
         params = jnp.stack([jnp.where(upper, other, params), jnp.where(upper, params, other)], axis=axis)
         distance //= 2
         axis += 1
-    if tree:
-        params = params.reshape((members,) + own.shape)
-    else:
+    if not tree:
         params = params.reshape((count,) + own.shape).transpose(1, 2, 0, 3).reshape(2, modes, members, SETS, LANES)
         params = lax.dynamic_index_in_dim(params, core, 3, keepdims=False).transpose(2, 0, 1, 3)
         halves = params.reshape(members // 2, 2, 2, modes, LANES)
@@ -585,54 +595,66 @@
             lax.dynamic_index_in_dim(halves, s, 1, keepdims=False).reshape(rows, LANES) for s in (side, 1 - side)
         )
         states_own = chip_states(False, gated, gate_grad, par_own)
-    par = params.reshape(members * 2 * modes, LANES)
+    par = jnp.concatenate([par_own, par_far])
 
     sk_far, hs_far, ks_far, *weighted_far = chip_states(True, gated, gate_grad, par_far)
     sk_own, hs_own, ks_own, *weighted_own = states_own
 
-    def message_shape(span):
-        return shape(rows * (1 if span == top else 2) + (4 * rows // span if tree else 0), LANES, dtype=BF16)
+    def message_shapes(span):
+        if span == top:
+            return (shape(rows + (6 * modes if tree else 0), LANES, dtype=BF16),) * (WAYS - 1)
+        return (shape(rows * 2 + (4 * rows // span if tree else 0), LANES, dtype=BF16),)
 
     def chip_sums(flip, outs, weighted, hs, ks, sk, *par):
         return call(
-            functools.partial(sums_kernel, part=min(4, modes), unroll=4, flip=flip, last=top == SETS, tree=tree, **sizes),
-            (shape(4, rows // 2, LANES),) + outs,
+            functools.partial(sums_kernel, part=min(4, modes), unroll=4, flip=flip, tree=tree, **sizes),
+            (() if flip and tree else (shape(4, rows // 2, LANES),)) + outs,
             [SMEM] + [VMEM] * (6 + len(par)),
             work * 3,
             scratch=(pltpu.VMEM((4, 2, rows // 2, LANES), F32),),
         )(me, *weighted, lags, hs, ks, sk, *par)
 
-    sums_far, tot, message = chip_sums(
-        True, (pair, message_shape(SETS)), weighted_far, hs_far, ks_far, sk_far, par_far, sk_own, par_own
+    *sums_far, tot, message = chip_sums(
+        True, (pair, *message_shapes(SETS)), weighted_far, hs_far, ks_far, sk_far, par_far, sk_own, par_own
     )
+    messages = [message]
     tot, weighted_own[0] = tie(tot, weighted_own[0])
     (sums_own,) = chip_sums(False, (), weighted_own, hs_own, ks_own, sk_own, par_own)
 
     enter, span, pair_tot, kept = tot, SETS, tot, [sums_own] if tree else []
     while span < top:
-        got = exchange(message, span, count)
+        got = exchange(messages[0], span, count)
         last = span * 2 == top
-        tot, enter, message, *kept = call(
-            functools.partial(level_kernel, tokens=tokens, modes=modes, members=members, span=span, last=last, tree=tree),
-            (pair, pair, message_shape(span * 2)) + ((shape(4, rows // span // 2, LANES),) if tree else ()),
+        extra = (shape(6, modes, LANES) if last else shape(4, rows // span // 2, LANES),) if tree else ()
+        out = call(
+            functools.partial(level_kernel, span=span, last=last, tree=tree, **sizes),
+            (pair,) * (1 if last else 2) + message_shapes(span * 2) + extra,
             [SMEM] + [VMEM] * (5 if tree else 4),
             rows,
+            scratch=(pltpu.VMEM((members // 2, 6, modes, LANES), F32),) if tree else (),
         )(me, tot, got, enter, par, *kept)
+        if not last:
+            tot, *out = out
+        enter, *messages = out
+        if tree:
+            kept = [messages.pop()]
         if span == SETS:
-            tot, hs_own, gated, gate_grad = tie(tot, hs_own, gated, gate_grad)
+            enter, hs_own, gated, gate_grad = tie(enter, hs_own, gated, gate_grad)
         span *= 2
-    far = exchange(message, top, count)
+    far = [exchange(message, hop * top, count) for hop, message in zip(HOPS, messages)]
     hs, ks = call(
         functools.partial(order_kernel, **sizes),
         (shape(2, stretches, modes * members, LANES), shape(2, stretches + 1, modes * members, LANES)),
-        [SMEM] + [VMEM] * 4,
+        [VMEM] * 4,
         work,
-    )(me, hs_own, ks_own, hs_far, ks_far)
-    y, z = call(functools.partial(taps_kernel, **sizes), (series, series), [VMEM] * 3, work)(gated, gate_grad, par)
-    far, y, hs = tie(far, y, hs)
+    )(hs_own, ks_own, hs_far, ks_far)
+    y, z = call(functools.partial(taps_kernel, **sizes), (series, series), [SMEM] + [VMEM] * 3, work)(
+        me, gated, gate_grad, par
+    )
+    far[0], y, hs = tie(far[0], y, hs)
     (states_in,) = call(
-        functools.partial(enter_kernel, span=top, **sizes), (shape(2, 2, rows, LANES),), [SMEM] + [VMEM] * 5, rows
-    )(me, enter, far, par, sk_own, sk_far)
+        functools.partial(enter_kernel, span=top, **sizes), (shape(2, 2, rows, LANES),), [SMEM] + [VMEM] * 7, rows
+    )(me, enter, *far, par, sk_own, sk_far)
 
     scratch = (pltpu.VMEM((tokens * members, LANES), F32),) * 2
     finish = functools.partial(finish_kernel, tokens=tokens, modes=modes, members=members)
@@ -645,7 +667,7 @@
         me, y, z, hs, ks, par, states_in, key_proj, value_proj, output_grad
     )
     scale = float(tokens * count) ** (-0.5)
-    extra = (*kept, far, tot, own) if tree else ()
+    extra = (*kept, *far, own) if tree else ()
     first = 5 + len(extra)
     out = call(
         functools.partial(last_kernel, tokens=tokens, modes=modes, members=members, span=top, scale=scale, tree=tree),
@@ -654,7 +676,7 @@
         work,
         (VMEM,) * 3 + (ANY,) * (5 if tree else 3),
         (pltpu.SemaphoreType.DMA((3, tokens // 16)),)
-        + ((pltpu.SemaphoreType.DMA((2,)), pltpu.VMEM((2, modes, LANES), F32)) if tree else ()),
+        + ((pltpu.SemaphoreType.DMA((2,)), pltpu.VMEM((2, modes, LANES), F32), pltpu.VMEM((WAYS, 6, modes, LANES), F32)) if tree else ()),
         {first: 0, first + 1: 1, first + 2: 2},
     )(me, got_conv, key_proj, value_proj, output_grad, *extra, *done)
 
@@ -662,11 +684,14 @@
         residue_grad, log_grad = out[6].T, out[7].T
     else:
         dims = (members, modes, LANES)
-        h_in, k_in = states_in[0, 0].reshape(dims), states_in[1, 1].reshape(dims)
-        s, k = (a.reshape(dims) for a in pair_tot)
-        own_half, far_half = (a.reshape(4, members // 2, modes, LANES) for a in (sums_own, sums_far))
-        ordered = jnp.where(side == 0, jnp.stack([own_half, far_half], 2), jnp.stack([far_half, own_half], 2))
-        r, d, s_d, k_d = ordered.reshape((4,) + dims)
+
+        def by_member(a):
+            a = a.reshape(2, members // 2, modes, LANES)
+            return jnp.where(side == 0, a, a[::-1]).transpose(1, 0, 2, 3).reshape(dims)
+
+        h_in, k_in = by_member(states_in[0, 0]), by_member(states_in[1, 1])
+        s, k = (by_member(a) for a in pair_tot)
+        r, d, s_d, k_d = (by_member(jnp.stack([a, b])) for a, b in zip(sums_own, sums_far[0]))
         rate = params[:, 0]
         w = jnp.exp(-rate)
         r = r + w * h_in * k

time: 40.8 us -> 38.8 us (0.951)
  waiting for transfers between devices: 8.3 us -> 6.88 us
  Pallas kernels: 17.3 us -> 16.3 us
  starting transfers between devices: 13.2 us -> 13.7 us
    ppermute x8 -> x9, waiting for transfers between devices: 8.3 us -> 6.88 us  [exchange(): return lax.ppermute(value, 'ctx', [(i, i ^ distance) for i in range(count)])]
    pallas_call x2, Pallas kernels: 4.29 us -> 3.71 us  [chip_sums(): call(functools.partial(sums_kernel, part=min(4, modes), unroll=4, flip=fl...]
    ppermute x8 -> x9, starting transfers between devices: 13.2 us -> 13.7 us  [exchange(): return lax.ppermute(value, 'ctx', [(i, i ^ distance) for i in range(count)])]
    pallas_call x3 -> x2, Pallas kernels: 1.13 us -> 1.01 us  [the longest x1 0.86 us: local(): call(functools.partial(taps_kernel, **sizes), (series, series), [SMEM] +...]
  transfers between devices with their start and end apart: 8 -> 9, of which waited for: 6 -> 7; matrix products, arithmetic and copies ran while one was open for 0% -> 0% of each run, Pallas kernels for 25% -> 25%
where the time goes in v5:
time: 38.8 us; the launch traced here: 38.5 us
  Pallas kernels  16.3 us (42%)
  starting transfers between devices  13.7 us (35%)
  waiting for transfers between devices  6.88 us (18%)
  between operations  0.86 us (2%)
  other arithmetic  0.75 us (2%)
    ppermute x9, starting transfers between devices, exchange(): return lax.ppermute(value, 'ctx', [(i, i ^ distance) for i in range(count)])  13.7 us
    ppermute x9, waiting for transfers between devices, exchange(): return lax.ppermute(value, 'ctx', [(i, i ^ distance) for i in range(count)])  6.88 us
    pallas_call x2, Pallas kernels, chip_sums(): call(functools.partial(sums_kernel, part=min(4, modes), unroll=4, flip=fl...  3.71 us
    pallas_call x2, Pallas kernels, chip_states(): call(functools.partial(state_kernel, flip=flip, **sizes), states + (half_...  2.54 us
    pallas_call x1, Pallas kernels, local(): call(functools.partial(finish, own=True), grads, [SMEM] + [VMEM] * 9, wor...  2 us
    pallas_call x1, Pallas kernels, local(): call(functools.partial(gate_kernel, members=members, pieces=pieces), (hal...  1.87 us
    pallas_call x1, Pallas kernels, local(): call(functools.partial(finish, own=False), (half,), [SMEM] + [VMEM] * 6,...  1.77 us
    pallas_call x1, Pallas kernels, local(): call(functools.partial(last_kernel, tokens=tokens, modes=modes, members=m...  1.43 us
  transfers between devices with their start and end apart: 9, of which 7 were waited for; matrix products, arithmetic and copies ran while one was open for 0% of the time, Pallas kernels for 25%

profile of v5, /device:TPU:0, one launch (start us, length us, event | category | flops | bytes accessed | tf_op | source)
XLA Modules:
  0.0 38.5 jit_solution(9447117074790577272)
XLA Ops:
  0.6 0.7 %pad_maximum_fusion.3.refs_4_ = f32[2,16,128]{2,1,0:T(8,128)S(1)} fusion(f32[1,16,128]{2,1,0:T(8,128)} %bitcast.26, f32[1,16,128]{2,1,0:T(8,128)} %bitcast.27), kind=kLoop, calls=%fused_computation.5 | loop fusion | flops 4096 | bytes 32768 | tf_op jit(solution)/shard_map/stack | solution.py:565
  1.3 4.0 %collective-permute-start = (f32[2,16,128]{2,1,0:T(8,128)S(1)}, f32[2,16,128]{2,1,0:T(8,128)S(1)}, u32[]{:S(2)}, u32[]{:S(2)}) collective-permute-start(f32[2,16,128]{2,1,0:T(8,128)S(1)} %pad_maximum_fusion.3.refs_4_), channel_id=1, source_target_pairs={{0,16},{2,18},{4,20},{6,22},{8,24},{10,26},{12,28},{14,30},{16,0},... | collective-permute-start | bytes 49160 | tf_op jit(solution)/shard_map/ppermute | solution.py:516
  5.4 1.9 %shard_map.101 = (bf16[2,8,128,128]{3,2,1,0:T(8,128)(2,1)S(1)}, bf16[2,8,128,128]{3,2,1,0:T(8,128)(2,1)S(1)}) custom-call(s32[1]{0:T(128)} %bitcast.me_ref, bf16[128,2048]{1,0:T(8,128)(2,1)} %q_hbm.1, bf16[128,2048]{1,0:T(8,128)(2,1)} %k_ref.1, bf16[128,2048]{1,0:T(8,128)(2,1)} %v_ref.1, bf16[128,2048]{1,0:T(8,128)(2,1)} %u_ref.1), custom_call_target="tpu_custom_call" | custom-call | flops 4194304 | bytes 1048576 | tf_op jit(solution)/shard_map/pallas_call | solution.py:557
  7.3 0.0 collective-permute-done
  7.3 0.1 collective-permute-start.2
  7.4 1.7 %collective-permute-start.1 = (f32[2,2,16,128]{3,2,1,0:T(8,128)S(1)}, f32[2,2,16,128]{3,2,1,0:T(8,128)S(1)}, u32[]{:S(2)}, u32[]{:S(2)}) collective-permute-start(f32[2,2,16,128]{3,2,1,0:T(8,128)S(1)} %pad_maximum_fusion.2), channel_id=1, source_target_pairs={{0,8},{2,10},{4,12},{6,14},{8,0},{10,2},{12,4},{14,6},{16,24},{18,... | collective-permute-start | bytes 98312 | tf_op jit(solution)/shard_map/ppermute | solution.py:516
  9.1 0.2 collective-permute-done.2.got_ref
  9.3 1.0 %shard_map.102 = (f32[2,1024,128]{2,1,0:T(8,128)S(1)}, f32[2,1024,128]{2,1,0:T(8,128)S(1)}, f32[2,8,8,128]{3,2,1,0:T(8,128)S(1)}) custom-call(s32[1]{0:T(128)} %bitcast.me_ref, bf16[2,8,128,128]{3,2,1,0:T(8,128)(2,1)S(1)} %get-tuple-element.60.own_ref, bf16[2,8,128,128]{3,2,1,0:T(8,128)(2,1)S(1)} %collective-permute-done.2.got_ref), custom_call_target="tpu_custom_call" | custom-call | flops 4194304 | bytes 1048576 | tf_op jit(solution)/shard_map/pallas_call | solution.py:573
  10.2 1.2 %collective-permute-done.1 = f32[2,2,16,128]{3,2,1,0:T(8,128)S(1)} collective-permute-done((f32[2,2,16,128]{3,2,1,0:T(8,128)S(1)}, f32[2,2,16,128]{3,2,1,0:T(8,128)S(1)}, u32[]{:S(2)}, u32[]{:S(2)}) %collective-permute-start.1) | collective-permute-done | bytes 32800 | tf_op jit(solution)/shard_map/ppermute | solution.py:516
  11.4 1.7 %collective-permute-start.3 = (f32[2,2,2,16,128]{4,3,2,0,1:T(8,128)S(1)}, f32[2,2,2,16,128]{4,3,2,0,1:T(8,128)S(1)}, u32[]{:S(2)}, u32[]{:S(2)}) collective-permute-start(f32[2,2,2,16,128]{4,3,2,0,1:T(8,128)S(1)} %pad_maximum_fusion.1), channel_id=1, source_target_pairs={{0,4},{2,6},{4,0},{6,2},{8,12},{10,14},{12,8},{14,10},{16,20},{18,... | collective-permute-start | bytes 196616 | tf_op jit(solution)/shard_map/ppermute | solution.py:516
  13.1 1.3 %shard_map.103 = (f32[2,2,64,128]{3,2,1,0:T(8,128)S(1)}, f32[16,16,8,128]{3,2,1,0:T(8,128)S(1)}, f32[17,16,8,128]{3,2,1,0:T(8,128)S(1)}, f32[1024,128]{1,0:T(8,128)S(1)}, f32[1024,128]{1,0:T(8,128)S(1)}) custom-call(s32[1]{0:T(128)} %bitcast.me_ref, f32[2,1024,128]{2,1,0:T(8,128)S(1)} %get-tuple-element.87.x_ref, ...), custom_call_target="tpu_custom_call" | custom-call | flops 8388608 | bytes 1048576 | tf_op jit(solution)/shard_map/pallas_call | solution.py:552
  14.4 1.4 %collective-permute-done.3 = f32[2,2,2,16,128]{4,3,2,0,1:T(8,128)S(1)} collective-permute-done((f32[2,2,2,16,128]{4,3,2,0,1:T(8,128)S(1)}, f32[2,2,2,16,128]{4,3,2,0,1:T(8,128)S(1)}, u32[]{:S(2)}, u32[]{:S(2)}) %collective-permute-start.3) | collective-permute-done | bytes 65568 | tf_op jit(solution)/shard_map/ppermute | solution.py:516
  15.8 1.3 %shard_map.104 = (f32[2,2,64,128]{3,2,1,0:T(8,128)S(1)}, f32[16,16,8,128]{3,2,1,0:T(8,128)S(1)}, f32[17,16,8,128]{3,2,1,0:T(8,128)S(1)}, f32[1024,128]{1,0:T(8,128)S(1)}, f32[1024,128]{1,0:T(8,128)S(1)}) custom-call(s32[1]{0:T(128)} %bitcast.me_ref, f32[2,1024,128]{2,1,0:T(8,128)S(1)} %get-tuple-element.87.x_ref, ...), custom_call_target="tpu_custom_call" | custom-call | flops 8388608 | bytes 1048576 | tf_op jit(solution)/shard_map/pallas_call | solution.py:552
  17.0 1.9 %shard_map.105 = (f32[2,128,128]{2,1,0:T(8,128)S(1)}, bf16[512,128]{1,0:T(8,128)(2,1)S(1)}) custom-call(s32[1]{0:T(128)} %bitcast.me_ref, f32[1024,128]{1,0:T(8,128)S(1)} %get-tuple-element.70.x_ref, f32[1024,128]{1,0:T(8,128)S(1)} %get-tuple-element.71.g_ref, f32[2,8,8,128]{3,2,1,0:T(8,128)S(1)} %get-tuple-element.72.lag_ref, ...), custom_call_target="tpu_custom_call" | custom-call | flops 12582912 | bytes 1048576 | tf_op jit(solution)/shard_map/pallas_call | solution.py:609
  18.9 1.7 %collective-permute-start.4 = (bf16[512,128]{1,0:T(8,128)(2,1)S(1)}, bf16[512,128]{1,0:T(8,128)(2,1)S(1)}, u32[]{:S(2)}, u32[]{:S(2)}) collective-permute-start(bf16[512,128]{1,0:T(8,128)(2,1)S(1)} %get-tuple-element.80), channel_id=1, source_target_pairs={{0,4},{2,6},{4,0},{6,2},{8,12},{10,14},{12,8},{14,10},{16,20},{18,... | collective-permute-start | bytes 393224 | tf_op jit(solution)/shard_map/ppermute | solution.py:516
  20.6 1.8 %shard_map.106.refs_0_ = f32[4,64,128]{2,1,0:T(8,128)S(1)} custom-call(s32[1]{0:T(128)} %bitcast.me_ref, f32[1024,128]{1,0:T(8,128)S(1)} %get-tuple-element.81.x_ref, f32[1024,128]{1,0:T(8,128)S(1)} %get-tuple-element.82.g_ref, f32[2,8,8,128]{3,2,1,0:T(8,128)S(1)} %get-tuple-element.72.lag_ref, f32[16,16,8,128]{3,2,1,0:T(8,128)S(1)} %get-tuple-element.90.hs_ref.hs_own, ...), custom_call_target="tpu_custom_call" | custom-call | flops 12582912 | bytes 1048576 | tf_op jit(solution)/shard_map/pallas_call | solution.py:609
  22.5 1.5 %collective-permute-done.4.got_ref = bf16[512,128]{1,0:T(8,128)(2,1)S(1)} collective-permute-done((bf16[512,128]{1,0:T(8,128)(2,1)S(1)}, bf16[512,128]{1,0:T(8,128)(2,1)S(1)}, u32[]{:S(2)}, u32[]{:S(2)}) %collective-permute-start.4) | collective-permute-done | bytes 131104 | tf_op jit(solution)/shard_map/ppermute | solution.py:516
  24.0 0.2 shard_map.107
  24.1 3.8 %collective-permute-start.5 = (bf16[224,128]{1,0:T(8,128)(2,1)S(1)}, bf16[224,128]{1,0:T(8,128)(2,1)S(1)}, u32[]{:S(2)}, u32[]{:S(2)}) collective-permute-start(bf16[224,128]{1,0:T(8,128)(2,1)S(1)} %get-tuple-element.85), channel_id=1, source_target_pairs={{0,24},{2,26},{4,28},{6,30},{8,16},{10,18},{12,20},{14,22},{16,8},... | collective-permute-start | bytes 172040 | tf_op jit(solution)/shard_map/ppermute | solution.py:516
  27.9 0.0 collective-permute-start.6
  27.9 0.7 %collective-permute-start.7 = (bf16[224,128]{1,0:T(8,128)(2,1)S(1)}, bf16[224,128]{1,0:T(8,128)(2,1)S(1)}, u32[]{:S(2)}, u32[]{:S(2)}) collective-permute-start(bf16[224,128]{1,0:T(8,128)(2,1)S(1)} %get-tuple-element.99), channel_id=1, source_target_pairs={{0,16},{2,18},{4,20},{6,22},{8,24},{10,26},{12,28},{14,30},{16,0},... | collective-permute-start | bytes 172040 | tf_op jit(solution)/shard_map/ppermute | solution.py:516
  28.6 0.9 %shard_map.109 = (f32[2,16,128,128]{3,2,1,0:T(8,128)S(1)}, f32[2,17,128,128]{3,2,1,0:T(8,128)S(1)}) custom-call(f32[16,16,8,128]{3,2,1,0:T(8,128)S(1)} %get-tuple-element.90.hs_ref.hs_own, f32[17,16,8,128]{3,2,1,0:T(8,128)S(1)} %get-tuple-element.84.ks_ref.ks_own, f32[16,16,8,128]{3,2,1,0:T(8,128)S(1)} %get-tuple-element.73.hs_ref.hs_far, ...), custom_call_target="tpu_custom_call" | custom-call | flops 4194304 | bytes 1048576 | tf_op jit(solution)/shard_map/pallas_call | solution.py:645
  29.5 0.9 %shard_map.108 = (f32[2048,128]{1,0:T(8,128)S(1)}, f32[2048,128]{1,0:T(8,128)S(1)}) custom-call(s32[1]{0:T(128)} %bitcast.me_ref, f32[2,1024,128]{2,1,0:T(8,128)S(1)} %get-tuple-element.87.x_ref, f32[2,1024,128]{2,1,0:T(8,128)S(1)} %get-tuple-element.88.g_ref, f32[256,128]{1,0:T(8,128)S(1)} %pad_maximum_fusion.par_ref), custom_call_target="tpu_custom_call" | custom-call | flops 4194304 | bytes 1048576 | tf_op jit(solution)/shard_map/pallas_call | solution.py:651
  30.3 0.3 collective-permute-done.5.a_ref.refs_1_
  30.7 1.4 %collective-permute-done.6.b_ref.refs_2_ = bf16[224,128]{1,0:T(8,128)(2,1)S(1)} collective-permute-done((bf16[224,128]{1,0:T(8,128)(2,1)S(1)}, bf16[224,128]{1,0:T(8,128)(2,1)S(1)}, u32[]{:S(2)}, u32[]{:S(2)}) %collective-permute-start.6) | collective-permute-done | bytes 57376 | tf_op jit(solution)/shard_map/ppermute | solution.py:516
  32.1 0.9 %collective-permute-done.7.c_ref.refs_3_ = bf16[224,128]{1,0:T(8,128)(2,1)S(1)} collective-permute-done((bf16[224,128]{1,0:T(8,128)(2,1)S(1)}, bf16[224,128]{1,0:T(8,128)(2,1)S(1)}, u32[]{:S(2)}, u32[]{:S(2)}) %collective-permute-start.7) | collective-permute-done | bytes 57376 | tf_op jit(solution)/shard_map/ppermute | solution.py:516
  33.0 0.1 shard_map.110.in_ref
  33.1 0.0 copy-start
  33.1 0.0 copy-start.1
  33.1 0.0 copy-start.2
  33.1 1.8 %shard_map.111 = bf16[2,8,128,128]{3,2,1,0:T(8,128)(2,1)S(1)} custom-call(s32[1]{0:T(128)} %bitcast.me_ref, f32[2048,128]{1,0:T(8,128)S(1)} %get-tuple-element.92.y_ref, f32[2048,128]{1,0:T(8,128)S(1)} %get-tuple-element.93.z_ref, f32[2,16,128,128]{3,2,1,0:T(8,128)S(1)} %get-tuple-element.94.hs_ref, f32[2,17,128,128]{3,2,1,0:T(8,128)S(1)} %get-tuple-element.95.ks_ref, ...), custom_call_target="tpu_custom_call" | custom-call | flops 8388608 | bytes 1048576 | tf_op jit(solution)/shard_map/pallas_call | solution.py:661
  34.9 0.1 collective-permute-start.8
  35.0 0.0 copy-done
  35.0 0.0 copy-done.1
  35.0 0.0 copy-done.2
  35.0 2.0 %shard_map.112 = (bf16[128,2048]{1,0:T(8,128)(2,1)S(1)}, bf16[128,2048]{1,0:T(8,128)(2,1)S(1)}, bf16[128,2048]{1,0:T(8,128)(2,1)S(1)}) custom-call(s32[1]{0:T(128)} %bitcast.me_ref, f32[2048,128]{1,0:T(8,128)S(1)} %get-tuple-element.92.y_ref, f32[2048,128]{1,0:T(8,128)S(1)} %get-tuple-element.93.z_ref, f32[2,16,128,128]{3,2,1,0:T(8,128)S(1)} %get-tuple-element.94.hs_ref, ...), custom_call_target="tpu_custom_call" | custom-call | flops 8388608 | bytes 1048576 | tf_op jit(solution)/shard_map/pallas_call | solution.py:666
  37.0 0.0 collective-permute-done.8.got_ref
  37.0 1.4 %shard_map.113 = (bf16[128,2048]{1,0:T(8,128)(2,1)S(1)}, bf16[128,2048]{1,0:T(8,128)(2,1)S(1)}, bf16[128,2048]{1,0:T(8,128)(2,1)S(1)}, bf16[128,2048]{1,0:T(8,12...) custom-call(s32[1]{0:T(128)} %bitcast.me_ref, ...), custom_call_target="tpu_custom_call", output_to_operand_aliasing={{0}: (10, {}), {1}: (11, {}), {2}: (12, {})} | custom-call | flops 4194304 | bytes 1048576 | tf_op jit(solution)/shard_map/pallas_call | solution.py:672
  (7 shorter events, 0.0 us)
Async XLA Ops:
  1.3 5.9 %collective-permute-start = (f32[2,16,128]{2,1,0:T(8,128)S(1)}, f32[2,16,128]{2,1,0:T(8,128)S(1)}, u32[]{:S(2)}, u32[]{:S(2)}) collective-permute-start(f32[2,16,128]{2,1,0:T(8,128)S(1)} %pad_maximum_fusion.3.refs_4_), channel_id=1, source_target_pairs={{0,16},{2,18},{4,20},{6,22},{8,24},{10,26},{12,28},{14,30},{16,0},... | collective-permute-start | bytes 49160 | tf_op jit(solution)/shard_map/ppermute | solution.py:516
  7.3 2.0 %collective-permute-start.2 = (bf16[2,8,128,128]{3,2,1,0:T(8,128)(2,1)S(1)}, bf16[2,8,128,128]{3,2,1,0:T(8,128)(2,1)S(1)}, u32[]{:S(2)}, u32[]{:S(2)}) collective-permute-start(bf16[2,8,128,128]{3,2,1,0:T(8,128)(2,1)S(1)} %get-tuple-element.61), channel_id=1, source_target_pairs={{0,2},{2,0},{4,6},{6,4},{8,10},{10,8},{12,14},{14,12},{16,18},{18,... | collective-permute-start | bytes 1572872 | tf_op jit(solution)/shard_map/ppermute | solution.py:516
  7.4 4.0 %collective-permute-start.1 = (f32[2,2,16,128]{3,2,1,0:T(8,128)S(1)}, f32[2,2,16,128]{3,2,1,0:T(8,128)S(1)}, u32[]{:S(2)}, u32[]{:S(2)}) collective-permute-start(f32[2,2,16,128]{3,2,1,0:T(8,128)S(1)} %pad_maximum_fusion.2), channel_id=1, source_target_pairs={{0,8},{2,10},{4,12},{6,14},{8,0},{10,2},{12,4},{14,6},{16,24},{18,... | collective-permute-start | bytes 98312 | tf_op jit(solution)/shard_map/ppermute | solution.py:516
  11.4 4.3 %collective-permute-start.3 = (f32[2,2,2,16,128]{4,3,2,0,1:T(8,128)S(1)}, f32[2,2,2,16,128]{4,3,2,0,1:T(8,128)S(1)}, u32[]{:S(2)}, u32[]{:S(2)}) collective-permute-start(f32[2,2,2,16,128]{4,3,2,0,1:T(8,128)S(1)} %pad_maximum_fusion.1), channel_id=1, source_target_pairs={{0,4},{2,6},{4,0},{6,2},{8,12},{10,14},{12,8},{14,10},{16,20},{18,... | collective-permute-start | bytes 196616 | tf_op jit(solution)/shard_map/ppermute | solution.py:516
  18.9 5.0 %collective-permute-start.4 = (bf16[512,128]{1,0:T(8,128)(2,1)S(1)}, bf16[512,128]{1,0:T(8,128)(2,1)S(1)}, u32[]{:S(2)}, u32[]{:S(2)}) collective-permute-start(bf16[512,128]{1,0:T(8,128)(2,1)S(1)} %get-tuple-element.80), channel_id=1, source_target_pairs={{0,4},{2,6},{4,0},{6,2},{8,12},{10,14},{12,8},{14,10},{16,20},{18,... | collective-permute-start | bytes 393224 | tf_op jit(solution)/shard_map/ppermute | solution.py:516
  24.1 6.5 %collective-permute-start.5 = (bf16[224,128]{1,0:T(8,128)(2,1)S(1)}, bf16[224,128]{1,0:T(8,128)(2,1)S(1)}, u32[]{:S(2)}, u32[]{:S(2)}) collective-permute-start(bf16[224,128]{1,0:T(8,128)(2,1)S(1)} %get-tuple-element.85), channel_id=1, source_target_pairs={{0,24},{2,26},{4,28},{6,30},{8,16},{10,18},{12,20},{14,22},{16,8},... | collective-permute-start | bytes 172040 | tf_op jit(solution)/shard_map/ppermute | solution.py:516
  27.9 4.2 %collective-permute-start.6 = (bf16[224,128]{1,0:T(8,128)(2,1)S(1)}, bf16[224,128]{1,0:T(8,128)(2,1)S(1)}, u32[]{:S(2)}, u32[]{:S(2)}) collective-permute-start(bf16[224,128]{1,0:T(8,128)(2,1)S(1)} %get-tuple-element.98), channel_id=1, source_target_pairs={{0,8},{2,10},{4,12},{6,14},{8,0},{10,2},{12,4},{14,6},{16,24},{18,... | collective-permute-start | bytes 172040 | tf_op jit(solution)/shard_map/ppermute | solution.py:516
  27.9 5.1 %collective-permute-start.7 = (bf16[224,128]{1,0:T(8,128)(2,1)S(1)}, bf16[224,128]{1,0:T(8,128)(2,1)S(1)}, u32[]{:S(2)}, u32[]{:S(2)}) collective-permute-start(bf16[224,128]{1,0:T(8,128)(2,1)S(1)} %get-tuple-element.99), channel_id=1, source_target_pairs={{0,16},{2,18},{4,20},{6,22},{8,24},{10,26},{12,28},{14,30},{16,0},... | collective-permute-start | bytes 172040 | tf_op jit(solution)/shard_map/ppermute | solution.py:516
  33.1 1.9 %copy-start = (bf16[128,2048]{1,0:T(8,128)(2,1)S(1)}, bf16[128,2048]{1,0:T(8,128)(2,1)}, u32[]{:S(2)}) copy-start(bf16[128,2048]{1,0:T(8,128)(2,1)} %k_ref.1) | copy-start | bytes 1572868
  33.1 1.9 %copy-start.1 = (bf16[128,2048]{1,0:T(8,128)(2,1)S(1)}, bf16[128,2048]{1,0:T(8,128)(2,1)}, u32[]{:S(2)}) copy-start(bf16[128,2048]{1,0:T(8,128)(2,1)} %v_ref.1) | copy-start | bytes 1572868
  33.1 1.9 %copy-start.2 = (bf16[128,2048]{1,0:T(8,128)(2,1)S(1)}, bf16[128,2048]{1,0:T(8,128)(2,1)}, u32[]{:S(2)}) copy-start(bf16[128,2048]{1,0:T(8,128)(2,1)} %u_ref.1) | copy-start | bytes 1572868
  34.9 2.1 %collective-permute-start.8 = (bf16[2,8,128,128]{3,2,1,0:T(8,128)(2,1)S(1)}, bf16[2,8,128,128]{3,2,1,0:T(8,128)(2,1)S(1)}, u32[]{:S(2)}, u32[]{:S(2)}) collective-permute-start(bf16[2,8,128,128]{3,2,1,0:T(8,128)(2,1)S(1)} %shard_map.111), channel_id=1, source_target_pairs={{0,2},{2,0},{4,6},{6,4},{8,10},{10,8},{12,14},{14,12},{16,18},{18,... | collective-permute-start | bytes 1572872 | tf_op jit(solution)/shard_map/ppermute | solution.py:516

commit v6 on v5

--- a/solution.py
+++ b/solution.py
@@ -170,15 +170,28 @@
         lax.fori_loop(0, tokens // STRETCH, within, 0, unroll=2)
 
 
-def order_kernel(hs_own, ks_own, hs_far, ks_far, hs_ref, ks_ref, *, tokens, modes, members):
+def order_kernel(hs_own, ks_own, hs_far, ks_far, par_ref, hs_ref, ks_ref, const_ref, *, tokens, modes, members):
     half = members // 2
+    for m in range(modes):
+        rate = param_rows(par_ref, 0, m, modes, members)
+        w = jnp.exp(-rate)
+        const_ref[0, m] = w
+        const_ref[1, m] = jnp.exp(rate * -float(STRETCH))
+        const_ref[2, m] = param_rows(par_ref, 1, m, modes, members) * jnp.sqrt(rate) * w
+    amp = []
+    for flip in range(2):
+        start = flip * half * 2 * modes
+        rates = [half_rows(par_ref, start + m, 2 * modes, members) for m in range(modes)]
+        residues = [half_rows(par_ref, start + modes + m, 2 * modes, members) for m in range(modes)]
+        amp.append([residues[m] * jnp.sqrt(rates[m]) * jnp.exp(-rates[m]) for m in range(modes)])
     for src, out, count in ((0, hs_ref, tokens // STRETCH), (1, ks_ref, tokens // STRETCH + 1)):
 
         def body(i, _):
             for flip, ref in ((0, (hs_own, ks_own)[src]), (1, (hs_far, ks_far)[src])):
                 for m in range(modes):
+                    value = ref[i, m] * amp[flip][m]
                     for chunk in range(2):
-                        out[chunk, i, pl.ds(m * members + flip * half, half), :] = ref[i, m, chunk * half : (chunk + 1) * half, :]
+                        out[chunk, i, pl.ds(m * members + flip * half, half), :] = value[chunk * half : (chunk + 1) * half]
             return 0
 
         lax.fori_loop(0, count, body, 0)
@@ -384,7 +397,7 @@
             in_ref[1, 1, at, :] = after
 
 
-def finish_kernel(me_ref, y_ref, z_ref, hs_ref, ks_ref, par_ref, in_ref, *refs, tokens, modes, members, own):
+def finish_kernel(me_ref, y_ref, z_ref, hs_ref, ks_ref, const_ref, in_ref, *refs, tokens, modes, members, own):
     if own:
         k_ref, v_ref, u_ref, dq_ref, dk_ref, dv_ref, yo_ref, zo_ref = refs
     else:
@@ -393,15 +406,12 @@
     chunk = core if own else 1 - core
     stretches = tokens // STRETCH
     base = chunk * stretches
-    rate = [param_rows(par_ref, 0, m, modes, members) for m in range(modes)]
-    w = [jnp.exp(-rate[m]) for m in range(modes)]
-    fade = [jnp.exp(rate[m] * -float(STRETCH)) for m in range(modes)]
-    amp = [param_rows(par_ref, 1, m, modes, members) * jnp.sqrt(rate[m]) * w[m] for m in range(modes)]
-    h = tuple(in_ref[chunk, 0, pl.ds(m, members, stride=modes), :] for m in range(modes))
-    k = tuple(in_ref[chunk, 1, pl.ds(m, members, stride=modes), :] for m in range(modes))
+    w, fade, amp = ([const_ref[i, m] for m in range(modes)] for i in range(3))
+    h = tuple(amp[m] * in_ref[chunk, 0, pl.ds(m, members, stride=modes), :] for m in range(modes))
+    k = tuple(amp[m] * in_ref[chunk, 1, pl.ds(m, members, stride=modes), :] for m in range(modes))
 
     def forward(i, h):
-        p = [amp[m] * (h[m] + hs_ref[chunk, i, pl.ds(m * members, members), :]) for m in range(modes)]
+        p = [h[m] + hs_ref[chunk, i, pl.ds(m * members, members), :] for m in range(modes)]
         for t in range(STRETCH):
             at = pl.ds((i * STRETCH + t) * members, members)
             yo_ref[at, :] = y_ref[pl.ds(((base + i) * STRETCH + t) * members, members), :] + total(p)
@@ -411,7 +421,7 @@
 
     def backward(i, k):
         back = stretches - 1 - i
-        q = [amp[m] * (k[m] + ks_ref[chunk, back + 1, pl.ds(m * members, members), :]) for m in range(modes)]
+        q = [k[m] + ks_ref[chunk, back + 1, pl.ds(m * members, members), :] for m in range(modes)]
         for t in range(STRETCH):
             row = back * STRETCH + STRETCH - 1 - t
             zo_ref[pl.ds(row * members, members), :] = z_ref[pl.ds((base * STRETCH + row) * members, members), :] + total(q)
@@ -442,9 +452,9 @@
         else:
             send_ref[1, member, rows, :] = value
 
-    lax.fori_loop(0, stretches, forward, h)
+    lax.fori_loop(0, stretches, forward, h, unroll=4)
     put(yo_ref, store_y)
-    lax.fori_loop(0, stretches, backward, k)
+    lax.fori_loop(0, stretches, backward, k, unroll=4)
     put(zo_ref, store_z)
 
 
@@ -607,7 +617,7 @@
 
     def chip_sums(flip, outs, weighted, hs, ks, sk, *par):
         return call(
-            functools.partial(sums_kernel, part=min(4, modes), unroll=4, flip=flip, tree=tree, **sizes),
+            functools.partial(sums_kernel, part=min(2, modes), unroll=16, flip=flip, tree=tree, **sizes),
             (() if flip and tree else (shape(4, rows // 2, LANES),)) + outs,
             [SMEM] + [VMEM] * (6 + len(par)),
             work * 3,
@@ -642,12 +652,16 @@
             enter, hs_own, gated, gate_grad = tie(enter, hs_own, gated, gate_grad)
         span *= 2
     far = [exchange(message, hop * top, count) for hop, message in zip(HOPS, messages)]
-    hs, ks = call(
+    hs, ks, const = call(
         functools.partial(order_kernel, **sizes),
-        (shape(2, stretches, modes * members, LANES), shape(2, stretches + 1, modes * members, LANES)),
-        [VMEM] * 4,
+        (
+            shape(2, stretches, modes * members, LANES),
+            shape(2, stretches + 1, modes * members, LANES),
+            shape(3, modes, members, LANES),
+        ),
+        [VMEM] * 5,
         work,
-    )(hs_own, ks_own, hs_far, ks_far)
+    )(hs_own, ks_own, hs_far, ks_far, par)
     y, z = call(functools.partial(taps_kernel, **sizes), (series, series), [SMEM] + [VMEM] * 3, work)(
         me, gated, gate_grad, par
     )
@@ -659,12 +673,12 @@
     scratch = (pltpu.VMEM((tokens * members, LANES), F32),) * 2
     finish = functools.partial(finish_kernel, tokens=tokens, modes=modes, members=members)
     (send_conv,) = call(functools.partial(finish, own=False), (half,), [SMEM] + [VMEM] * 6, work * 2, scratch=scratch)(
-        me, y, z, hs, ks, par, states_in
+        me, y, z, hs, ks, const, states_in
     )
     got_conv = exchange(send_conv, 1, count)
     grads = (shape(tokens, channels, dtype=BF16),) * 3
     done = call(functools.partial(finish, own=True), grads, [SMEM] + [VMEM] * 9, work * 2, scratch=scratch)(
-        me, y, z, hs, ks, par, states_in, key_proj, value_proj, output_grad
+        me, y, z, hs, ks, const, states_in, key_proj, value_proj, output_grad
     )
     scale = float(tokens * count) ** (-0.5)
     extra = (*kept, *far, own) if tree else ()

time: 38.8 us -> 38 us (0.979)
  Pallas kernels: 16.3 us -> 15.2 us
    pallas_call x2, Pallas kernels: 3.71 us -> 3.26 us  [chip_sums(): call(functools.partial(sums_kernel, part=min(2, modes), unroll=16, flip=f...]
  transfers between devices with their start and end apart: 9 -> 9, of which waited for: 7 -> 8; matrix products, arithmetic and copies ran while one was open for 0% -> 0% of each run, Pallas kernels for 25% -> 24%
where the time goes in v6:
time: 38 us; the launch traced here: 37.8 us
  Pallas kernels  15.2 us (40%)
  starting transfers between devices  13.7 us (36%)
  waiting for transfers between devices  7.23 us (19%)
  between operations  0.85 us (2%)
  other arithmetic  0.75 us (2%)
    ppermute x9, starting transfers between devices, exchange(): return lax.ppermute(value, 'ctx', [(i, i ^ distance) for i in range(count)])  13.7 us
    ppermute x9, waiting for transfers between devices, exchange(): return lax.ppermute(value, 'ctx', [(i, i ^ distance) for i in range(count)])  7.23 us
    pallas_call x2, Pallas kernels, chip_sums(): call(functools.partial(sums_kernel, part=min(2, modes), unroll=16, flip=f...  3.26 us
    pallas_call x2, Pallas kernels, chip_states(): call(functools.partial(state_kernel, flip=flip, **sizes), states + (half_...  2.54 us
    pallas_call x1, Pallas kernels, local(): call(functools.partial(gate_kernel, members=members, pieces=pieces), (hal...  1.87 us
    pallas_call x1, Pallas kernels, local(): call(functools.partial(finish, own=True), grads, [SMEM] + [VMEM] * 9, wor...  1.72 us
    pallas_call x1, Pallas kernels, local(): call(functools.partial(finish, own=False), (half,), [SMEM] + [VMEM] * 6,...  1.49 us
    pallas_call x1, Pallas kernels, local(): call(functools.partial(last_kernel, tokens=tokens, modes=modes, members=m...  1.42 us
  transfers between devices with their start and end apart: 9, of which 8 were waited for; matrix products, arithmetic and copies ran while one was open for 0% of the time, Pallas kernels for 24%

profile of v6, /device:TPU:0, one launch (start us, length us, event | category | flops | bytes accessed | tf_op | source)
XLA Modules:
  0.0 37.8 jit_solution(3628484765525431074)
XLA Ops:
  0.6 0.7 %pad_maximum_fusion.3.refs_4_ = f32[2,16,128]{2,1,0:T(8,128)S(1)} fusion(f32[1,16,128]{2,1,0:T(8,128)} %bitcast.26, f32[1,16,128]{2,1,0:T(8,128)} %bitcast.27), kind=kLoop, calls=%fused_computation.5 | loop fusion | flops 4096 | bytes 32768 | tf_op jit(solution)/shard_map/stack | solution.py:575
  1.3 4.0 %collective-permute-start = (f32[2,16,128]{2,1,0:T(8,128)S(1)}, f32[2,16,128]{2,1,0:T(8,128)S(1)}, u32[]{:S(2)}, u32[]{:S(2)}) collective-permute-start(f32[2,16,128]{2,1,0:T(8,128)S(1)} %pad_maximum_fusion.3.refs_4_), channel_id=1, source_target_pairs={{0,16},{2,18},{4,20},{6,22},{8,24},{10,26},{12,28},{14,30},{16,0},... | collective-permute-start | bytes 49160 | tf_op jit(solution)/shard_map/ppermute | solution.py:526
  5.4 1.9 %shard_map.101 = (bf16[2,8,128,128]{3,2,1,0:T(8,128)(2,1)S(1)}, bf16[2,8,128,128]{3,2,1,0:T(8,128)(2,1)S(1)}) custom-call(s32[1]{0:T(128)} %bitcast.me_ref, bf16[128,2048]{1,0:T(8,128)(2,1)} %q_hbm.1, bf16[128,2048]{1,0:T(8,128)(2,1)} %k_ref.1, bf16[128,2048]{1,0:T(8,128)(2,1)} %v_ref.1, bf16[128,2048]{1,0:T(8,128)(2,1)} %u_ref.1), custom_call_target="tpu_custom_call" | custom-call | flops 4194304 | bytes 1048576 | tf_op jit(solution)/shard_map/pallas_call | solution.py:567
  7.3 0.0 collective-permute-done
  7.3 0.1 collective-permute-start.2
  7.4 1.7 %collective-permute-start.1 = (f32[2,2,16,128]{3,2,1,0:T(8,128)S(1)}, f32[2,2,16,128]{3,2,1,0:T(8,128)S(1)}, u32[]{:S(2)}, u32[]{:S(2)}) collective-permute-start(f32[2,2,16,128]{3,2,1,0:T(8,128)S(1)} %pad_maximum_fusion.2), channel_id=1, source_target_pairs={{0,8},{2,10},{4,12},{6,14},{8,0},{10,2},{12,4},{14,6},{16,24},{18,... | collective-permute-start | bytes 98312 | tf_op jit(solution)/shard_map/ppermute | solution.py:526
  9.1 0.2 collective-permute-done.2.got_ref
  9.3 1.0 %shard_map.102 = (f32[2,1024,128]{2,1,0:T(8,128)S(1)}, f32[2,1024,128]{2,1,0:T(8,128)S(1)}, f32[2,8,8,128]{3,2,1,0:T(8,128)S(1)}) custom-call(s32[1]{0:T(128)} %bitcast.me_ref, bf16[2,8,128,128]{3,2,1,0:T(8,128)(2,1)S(1)} %get-tuple-element.61.own_ref, bf16[2,8,128,128]{3,2,1,0:T(8,128)(2,1)S(1)} %collective-permute-done.2.got_ref), custom_call_target="tpu_custom_call" | custom-call | flops 4194304 | bytes 1048576 | tf_op jit(solution)/shard_map/pallas_call | solution.py:583
  10.2 1.2 %collective-permute-done.1 = f32[2,2,16,128]{3,2,1,0:T(8,128)S(1)} collective-permute-done((f32[2,2,16,128]{3,2,1,0:T(8,128)S(1)}, f32[2,2,16,128]{3,2,1,0:T(8,128)S(1)}, u32[]{:S(2)}, u32[]{:S(2)}) %collective-permute-start.1) | collective-permute-done | bytes 32800 | tf_op jit(solution)/shard_map/ppermute | solution.py:526
  11.4 1.7 %collective-permute-start.3 = (f32[2,2,2,16,128]{4,3,2,0,1:T(8,128)S(1)}, f32[2,2,2,16,128]{4,3,2,0,1:T(8,128)S(1)}, u32[]{:S(2)}, u32[]{:S(2)}) collective-permute-start(f32[2,2,2,16,128]{4,3,2,0,1:T(8,128)S(1)} %pad_maximum_fusion.1), channel_id=1, source_target_pairs={{0,4},{2,6},{4,0},{6,2},{8,12},{10,14},{12,8},{14,10},{16,20},{18,... | collective-permute-start | bytes 196616 | tf_op jit(solution)/shard_map/ppermute | solution.py:526
  13.1 1.3 %shard_map.103 = (f32[2,2,64,128]{3,2,1,0:T(8,128)S(1)}, f32[16,16,8,128]{3,2,1,0:T(8,128)S(1)}, f32[17,16,8,128]{3,2,1,0:T(8,128)S(1)}, f32[1024,128]{1,0:T(8,128)S(1)}, f32[1024,128]{1,0:T(8,128)S(1)}) custom-call(s32[1]{0:T(128)} %bitcast.me_ref, f32[2,1024,128]{2,1,0:T(8,128)S(1)} %get-tuple-element.88.x_ref, ...), custom_call_target="tpu_custom_call" | custom-call | flops 8388608 | bytes 1048576 | tf_op jit(solution)/shard_map/pallas_call | solution.py:562
  14.4 1.4 %collective-permute-done.3 = f32[2,2,2,16,128]{4,3,2,0,1:T(8,128)S(1)} collective-permute-done((f32[2,2,2,16,128]{4,3,2,0,1:T(8,128)S(1)}, f32[2,2,2,16,128]{4,3,2,0,1:T(8,128)S(1)}, u32[]{:S(2)}, u32[]{:S(2)}) %collective-permute-start.3) | collective-permute-done | bytes 65568 | tf_op jit(solution)/shard_map/ppermute | solution.py:526
  15.8 1.3 %shard_map.104 = (f32[2,2,64,128]{3,2,1,0:T(8,128)S(1)}, f32[16,16,8,128]{3,2,1,0:T(8,128)S(1)}, f32[17,16,8,128]{3,2,1,0:T(8,128)S(1)}, f32[1024,128]{1,0:T(8,128)S(1)}, f32[1024,128]{1,0:T(8,128)S(1)}) custom-call(s32[1]{0:T(128)} %bitcast.me_ref, f32[2,1024,128]{2,1,0:T(8,128)S(1)} %get-tuple-element.88.x_ref, ...), custom_call_target="tpu_custom_call" | custom-call | flops 8388608 | bytes 1048576 | tf_op jit(solution)/shard_map/pallas_call | solution.py:562
  17.0 1.6 %shard_map.105 = (f32[2,128,128]{2,1,0:T(8,128)S(1)}, bf16[512,128]{1,0:T(8,128)(2,1)S(1)}) custom-call(s32[1]{0:T(128)} %bitcast.me_ref, f32[1024,128]{1,0:T(8,128)S(1)} %get-tuple-element.71.x_ref, f32[1024,128]{1,0:T(8,128)S(1)} %get-tuple-element.72.g_ref, f32[2,8,8,128]{3,2,1,0:T(8,128)S(1)} %get-tuple-element.73.lag_ref, ...), custom_call_target="tpu_custom_call" | custom-call | flops 12582912 | bytes 1048576 | tf_op jit(solution)/shard_map/pallas_call | solution.py:619
  18.7 1.7 %collective-permute-start.4 = (bf16[512,128]{1,0:T(8,128)(2,1)S(1)}, bf16[512,128]{1,0:T(8,128)(2,1)S(1)}, u32[]{:S(2)}, u32[]{:S(2)}) collective-permute-start(bf16[512,128]{1,0:T(8,128)(2,1)S(1)} %get-tuple-element.81), channel_id=1, source_target_pairs={{0,4},{2,6},{4,0},{6,2},{8,12},{10,14},{12,8},{14,10},{16,20},{18,... | collective-permute-start | bytes 393224 | tf_op jit(solution)/shard_map/ppermute | solution.py:526
  20.4 1.6 %shard_map.106.refs_0_ = f32[4,64,128]{2,1,0:T(8,128)S(1)} custom-call(s32[1]{0:T(128)} %bitcast.me_ref, f32[1024,128]{1,0:T(8,128)S(1)} %get-tuple-element.82.x_ref, f32[1024,128]{1,0:T(8,128)S(1)} %get-tuple-element.83.g_ref, f32[2,8,8,128]{3,2,1,0:T(8,128)S(1)} %get-tuple-element.73.lag_ref, f32[16,16,8,128]{3,2,1,0:T(8,128)S(1)} %get-tuple-element.91.hs_ref.hs_own, ...), custom_call_target="tpu_custom_call" | custom-call | flops 12582912 | bytes 1048576 | tf_op jit(solution)/shard_map/pallas_call | solution.py:619
  22.0 1.7 %collective-permute-done.4.got_ref = bf16[512,128]{1,0:T(8,128)(2,1)S(1)} collective-permute-done((bf16[512,128]{1,0:T(8,128)(2,1)S(1)}, bf16[512,128]{1,0:T(8,128)(2,1)S(1)}, u32[]{:S(2)}, u32[]{:S(2)}) %collective-permute-start.4) | collective-permute-done | bytes 131104 | tf_op jit(solution)/shard_map/ppermute | solution.py:526
  23.7 0.2 shard_map.107
  23.9 3.8 %collective-permute-start.5 = (bf16[224,128]{1,0:T(8,128)(2,1)S(1)}, bf16[224,128]{1,0:T(8,128)(2,1)S(1)}, u32[]{:S(2)}, u32[]{:S(2)}) collective-permute-start(bf16[224,128]{1,0:T(8,128)(2,1)S(1)} %get-tuple-element.86), channel_id=1, source_target_pairs={{0,24},{2,26},{4,28},{6,30},{8,16},{10,18},{12,20},{14,22},{16,8},... | collective-permute-start | bytes 172040 | tf_op jit(solution)/shard_map/ppermute | solution.py:526
  27.7 0.0 collective-permute-start.6
  27.7 0.7 %collective-permute-start.7 = (bf16[224,128]{1,0:T(8,128)(2,1)S(1)}, bf16[224,128]{1,0:T(8,128)(2,1)S(1)}, u32[]{:S(2)}, u32[]{:S(2)}) collective-permute-start(bf16[224,128]{1,0:T(8,128)(2,1)S(1)} %get-tuple-element.101), channel_id=1, source_target_pairs={{0,16},{2,18},{4,20},{6,22},{8,24},{10,26},{12,28},{14,30},{16,0},... | collective-permute-start | bytes 172040 | tf_op jit(solution)/shard_map/ppermute | solution.py:526
  28.3 0.9 %shard_map.109 = (f32[2,16,128,128]{3,2,1,0:T(8,128)S(1)}, f32[2,17,128,128]{3,2,1,0:T(8,128)S(1)}, f32[3,16,8,128]{3,2,1,0:T(8,128)S(1)}) custom-call(f32[16,16,8,128]{3,2,1,0:T(8,128)S(1)} %get-tuple-element.91.hs_ref.hs_own, f32[17,16,8,128]{3,2,1,0:T(8,128)S(1)} %get-tuple-element.85.ks_ref.ks_own, ...), custom_call_target="tpu_custom_call" | custom-call | flops 4194304 | bytes 1048576 | tf_op jit(solution)/shard_map/pallas_call | solution.py:655
  29.2 0.9 %shard_map.108 = (f32[2048,128]{1,0:T(8,128)S(1)}, f32[2048,128]{1,0:T(8,128)S(1)}) custom-call(s32[1]{0:T(128)} %bitcast.me_ref, f32[2,1024,128]{2,1,0:T(8,128)S(1)} %get-tuple-element.88.x_ref, f32[2,1024,128]{2,1,0:T(8,128)S(1)} %get-tuple-element.89.g_ref, f32[256,128]{1,0:T(8,128)S(1)} %pad_maximum_fusion.par_ref), custom_call_target="tpu_custom_call" | custom-call | flops 4194304 | bytes 1048576 | tf_op jit(solution)/shard_map/pallas_call | solution.py:665
  30.1 0.3 collective-permute-done.5.a_ref.refs_1_
  30.4 1.4 %collective-permute-done.6.b_ref.refs_2_ = bf16[224,128]{1,0:T(8,128)(2,1)S(1)} collective-permute-done((bf16[224,128]{1,0:T(8,128)(2,1)S(1)}, bf16[224,128]{1,0:T(8,128)(2,1)S(1)}, u32[]{:S(2)}, u32[]{:S(2)}) %collective-permute-start.6) | collective-permute-done | bytes 57376 | tf_op jit(solution)/shard_map/ppermute | solution.py:526
  31.8 0.9 %collective-permute-done.7.c_ref.refs_3_ = bf16[224,128]{1,0:T(8,128)(2,1)S(1)} collective-permute-done((bf16[224,128]{1,0:T(8,128)(2,1)S(1)}, bf16[224,128]{1,0:T(8,128)(2,1)S(1)}, u32[]{:S(2)}, u32[]{:S(2)}) %collective-permute-start.7) | collective-permute-done | bytes 57376 | tf_op jit(solution)/shard_map/ppermute | solution.py:526
  32.7 0.1 shard_map.110.in_ref
  32.8 0.0 copy-start
  32.8 0.0 copy-start.1
  32.9 0.0 copy-start.2
  32.9 1.5 %shard_map.111 = bf16[2,8,128,128]{3,2,1,0:T(8,128)(2,1)S(1)} custom-call(s32[1]{0:T(128)} %bitcast.me_ref, f32[2048,128]{1,0:T(8,128)S(1)} %get-tuple-element.93.y_ref, f32[2048,128]{1,0:T(8,128)S(1)} %get-tuple-element.94.z_ref, f32[2,16,128,128]{3,2,1,0:T(8,128)S(1)} %get-tuple-element.95.hs_ref, f32[2,17,128,128]{3,2,1,0:T(8,128)S(1)} %get-tuple-element.96.ks_ref, ...), custom_call_target="tpu_custom_call" | custom-call | flops 8388608 | bytes 1048576 | tf_op jit(solution)/shard_map/pallas_call | solution.py:675
  34.4 0.1 collective-permute-start.8
  34.4 0.0 copy-done
  34.5 0.0 copy-done.1
  34.5 0.0 copy-done.2
  34.5 1.7 %shard_map.112 = (bf16[128,2048]{1,0:T(8,128)(2,1)S(1)}, bf16[128,2048]{1,0:T(8,128)(2,1)S(1)}, bf16[128,2048]{1,0:T(8,128)(2,1)S(1)}) custom-call(s32[1]{0:T(128)} %bitcast.me_ref, f32[2048,128]{1,0:T(8,128)S(1)} %get-tuple-element.93.y_ref, f32[2048,128]{1,0:T(8,128)S(1)} %get-tuple-element.94.z_ref, f32[2,16,128,128]{3,2,1,0:T(8,128)S(1)} %get-tuple-element.95.hs_ref, ...), custom_call_target="tpu_custom_call" | custom-call | flops 8388608 | bytes 1048576 | tf_op jit(solution)/shard_map/pallas_call | solution.py:680
  36.2 0.1 collective-permute-done.8.got_ref
  36.3 1.4 %shard_map.113 = (bf16[128,2048]{1,0:T(8,128)(2,1)S(1)}, bf16[128,2048]{1,0:T(8,128)(2,1)S(1)}, bf16[128,2048]{1,0:T(8,128)(2,1)S(1)}, bf16[128,2048]{1,0:T(8,12...) custom-call(s32[1]{0:T(128)} %bitcast.me_ref, ...), custom_call_target="tpu_custom_call", output_to_operand_aliasing={{0}: (10, {}), {1}: (11, {}), {2}: (12, {})} | custom-call | flops 4194304 | bytes 1048576 | tf_op jit(solution)/shard_map/pallas_call | solution.py:686
  (7 shorter events, 0.0 us)
Async XLA Ops:
  1.3 5.9 %collective-permute-start = (f32[2,16,128]{2,1,0:T(8,128)S(1)}, f32[2,16,128]{2,1,0:T(8,128)S(1)}, u32[]{:S(2)}, u32[]{:S(2)}) collective-permute-start(f32[2,16,128]{2,1,0:T(8,128)S(1)} %pad_maximum_fusion.3.refs_4_), channel_id=1, source_target_pairs={{0,16},{2,18},{4,20},{6,22},{8,24},{10,26},{12,28},{14,30},{16,0},... | collective-permute-start | bytes 49160 | tf_op jit(solution)/shard_map/ppermute | solution.py:526
  7.3 2.0 %collective-permute-start.2 = (bf16[2,8,128,128]{3,2,1,0:T(8,128)(2,1)S(1)}, bf16[2,8,128,128]{3,2,1,0:T(8,128)(2,1)S(1)}, u32[]{:S(2)}, u32[]{:S(2)}) collective-permute-start(bf16[2,8,128,128]{3,2,1,0:T(8,128)(2,1)S(1)} %get-tuple-element.62), channel_id=1, source_target_pairs={{0,2},{2,0},{4,6},{6,4},{8,10},{10,8},{12,14},{14,12},{16,18},{18,... | collective-permute-start | bytes 1572872 | tf_op jit(solution)/shard_map/ppermute | solution.py:526
  7.4 4.0 %collective-permute-start.1 = (f32[2,2,16,128]{3,2,1,0:T(8,128)S(1)}, f32[2,2,16,128]{3,2,1,0:T(8,128)S(1)}, u32[]{:S(2)}, u32[]{:S(2)}) collective-permute-start(f32[2,2,16,128]{3,2,1,0:T(8,128)S(1)} %pad_maximum_fusion.2), channel_id=1, source_target_pairs={{0,8},{2,10},{4,12},{6,14},{8,0},{10,2},{12,4},{14,6},{16,24},{18,... | collective-permute-start | bytes 98312 | tf_op jit(solution)/shard_map/ppermute | solution.py:526
  11.4 4.3 %collective-permute-start.3 = (f32[2,2,2,16,128]{4,3,2,0,1:T(8,128)S(1)}, f32[2,2,2,16,128]{4,3,2,0,1:T(8,128)S(1)}, u32[]{:S(2)}, u32[]{:S(2)}) collective-permute-start(f32[2,2,2,16,128]{4,3,2,0,1:T(8,128)S(1)} %pad_maximum_fusion.1), channel_id=1, source_target_pairs={{0,4},{2,6},{4,0},{6,2},{8,12},{10,14},{12,8},{14,10},{16,20},{18,... | collective-permute-start | bytes 196616 | tf_op jit(solution)/shard_map/ppermute | solution.py:526
  18.7 5.0 %collective-permute-start.4 = (bf16[512,128]{1,0:T(8,128)(2,1)S(1)}, bf16[512,128]{1,0:T(8,128)(2,1)S(1)}, u32[]{:S(2)}, u32[]{:S(2)}) collective-permute-start(bf16[512,128]{1,0:T(8,128)(2,1)S(1)} %get-tuple-element.81), channel_id=1, source_target_pairs={{0,4},{2,6},{4,0},{6,2},{8,12},{10,14},{12,8},{14,10},{16,20},{18,... | collective-permute-start | bytes 393224 | tf_op jit(solution)/shard_map/ppermute | solution.py:526
  23.9 6.5 %collective-permute-start.5 = (bf16[224,128]{1,0:T(8,128)(2,1)S(1)}, bf16[224,128]{1,0:T(8,128)(2,1)S(1)}, u32[]{:S(2)}, u32[]{:S(2)}) collective-permute-start(bf16[224,128]{1,0:T(8,128)(2,1)S(1)} %get-tuple-element.86), channel_id=1, source_target_pairs={{0,24},{2,26},{4,28},{6,30},{8,16},{10,18},{12,20},{14,22},{16,8},... | collective-permute-start | bytes 172040 | tf_op jit(solution)/shard_map/ppermute | solution.py:526
  27.7 4.2 %collective-permute-start.6 = (bf16[224,128]{1,0:T(8,128)(2,1)S(1)}, bf16[224,128]{1,0:T(8,128)(2,1)S(1)}, u32[]{:S(2)}, u32[]{:S(2)}) collective-permute-start(bf16[224,128]{1,0:T(8,128)(2,1)S(1)} %get-tuple-element.100), channel_id=1, source_target_pairs={{0,8},{2,10},{4,12},{6,14},{8,0},{10,2},{12,4},{14,6},{16,24},{18,... | collective-permute-start | bytes 172040 | tf_op jit(solution)/shard_map/ppermute | solution.py:526
  27.7 5.1 %collective-permute-start.7 = (bf16[224,128]{1,0:T(8,128)(2,1)S(1)}, bf16[224,128]{1,0:T(8,128)(2,1)S(1)}, u32[]{:S(2)}, u32[]{:S(2)}) collective-permute-start(bf16[224,128]{1,0:T(8,128)(2,1)S(1)} %get-tuple-element.101), channel_id=1, source_target_pairs={{0,16},{2,18},{4,20},{6,22},{8,24},{10,26},{12,28},{14,30},{16,0},... | collective-permute-start | bytes 172040 | tf_op jit(solution)/shard_map/ppermute | solution.py:526
  32.8 1.6 %copy-start = (bf16[128,2048]{1,0:T(8,128)(2,1)S(1)}, bf16[128,2048]{1,0:T(8,128)(2,1)}, u32[]{:S(2)}) copy-start(bf16[128,2048]{1,0:T(8,128)(2,1)} %k_ref.1) | copy-start | bytes 1572868
  32.8 1.6 %copy-start.1 = (bf16[128,2048]{1,0:T(8,128)(2,1)S(1)}, bf16[128,2048]{1,0:T(8,128)(2,1)}, u32[]{:S(2)}) copy-start(bf16[128,2048]{1,0:T(8,128)(2,1)} %v_ref.1) | copy-start | bytes 1572868
  32.9 1.6 %copy-start.2 = (bf16[128,2048]{1,0:T(8,128)(2,1)S(1)}, bf16[128,2048]{1,0:T(8,128)(2,1)}, u32[]{:S(2)}) copy-start(bf16[128,2048]{1,0:T(8,128)(2,1)} %u_ref.1) | copy-start | bytes 1572868
  34.4 2.0 %collective-permute-start.8 = (bf16[2,8,128,128]{3,2,1,0:T(8,128)(2,1)S(1)}, bf16[2,8,128,128]{3,2,1,0:T(8,128)(2,1)S(1)}, u32[]{:S(2)}, u32[]{:S(2)}) collective-permute-start(bf16[2,8,128,128]{3,2,1,0:T(8,128)(2,1)S(1)} %shard_map.111), channel_id=1, source_target_pairs={{0,2},{2,0},{4,6},{6,4},{8,10},{10,8},{12,14},{14,12},{16,18},{18,... | collective-permute-start | bytes 1572872 | tf_op jit(solution)/shard_map/ppermute | solution.py:526

commit v7 on v6

--- a/solution.py
+++ b/solution.py
@@ -297,6 +297,16 @@
                 tot_ref[0, to, :] = s
                 tot_ref[1, to, :] = k
                 put_states([message_ref], me, SETS, to, to_k, s, k, False)
+
+
+def far_kernel(me_ref, x_ref, g_ref, lag_ref, par_ref, sk_own, par_own, sk_ref, hs_ref, ks_ref, *refs, tokens, modes, members, part, unroll, tree):
+    *outs, xw_ref, gw_ref, work_ref = refs
+    sizes = dict(tokens=tokens, modes=modes, members=members)
+    state_kernel(me_ref, x_ref, g_ref, par_ref, sk_ref, hs_ref, ks_ref, xw_ref, gw_ref, flip=True, **sizes)
+    sums_kernel(
+        me_ref, xw_ref, gw_ref, lag_ref, hs_ref, ks_ref, sk_ref, par_ref, sk_own, par_own, *outs, work_ref,
+        part=part, unroll=unroll, flip=True, tree=tree, **sizes,
+    )
 
 
 def join(rate, left, right, length):
@@ -456,6 +466,15 @@
     put(yo_ref, store_y)
     lax.fori_loop(0, stretches, backward, k, unroll=4)
     put(zo_ref, store_z)
+
+
+def first_finish_kernel(
+    me_ref, y_ref, z_ref, hs_ref, ks_ref, const_ref, enter_ref, a_ref, b_ref, c_ref, par_ref, sk_own, sk_far, send_ref, in_ref, *scratch,
+    tokens, modes, members, span,
+):
+    sizes = dict(tokens=tokens, modes=modes, members=members)
+    enter_kernel(me_ref, enter_ref, a_ref, b_ref, c_ref, par_ref, sk_own, sk_far, in_ref, span=span, **sizes)
+    finish_kernel(me_ref, y_ref, z_ref, hs_ref, ks_ref, const_ref, in_ref, send_ref, *scratch, own=False, **sizes)
 
 
 def last_kernel(me_ref, got_ref, k_ref, v_ref, u_ref, *refs, tokens, modes, members, span, scale, tree):
@@ -557,10 +576,11 @@
     stretches = tokens // STRETCH
     sizes = dict(tokens=tokens, modes=modes, members=members)
 
-    def chip_states(flip, gated, gate_grad, par):
-        states = shape(2, 2, rows // 2, LANES), shape(stretches, modes, members, LANES), shape(stretches + 1, modes, members, LANES)
+    states = shape(2, 2, rows // 2, LANES), shape(stretches, modes, members, LANES), shape(stretches + 1, modes, members, LANES)
+
+    def chip_states(gated, gate_grad, par):
         out = call(
-            functools.partial(state_kernel, flip=flip, **sizes), states + (half_series,) * 2, [SMEM] + [VMEM] * 3, work * 2
+            functools.partial(state_kernel, flip=False, **sizes), states + (half_series,) * 2, [SMEM] + [VMEM] * 3, work * 2
         )(me, gated, gate_grad, par)
         return list(out)
 
@@ -590,7 +610,7 @@
             other, gated, gate_grad, lags = tie(other, gated, gate_grad, lags)
         if tree and distance == SETS:
             par_own, par_far = (a.reshape(rows, LANES) for a in (params, other))
-            states_own = chip_states(False, gated, gate_grad, par_own)
+            states_own = chip_states(gated, gate_grad, par_own)
             par_far, states_own[0] = tie(par_far, states_own[0])
             break
         upper = (index // distance) % 2 == 1
@@ -604,10 +624,9 @@
         par_own, par_far = (
             lax.dynamic_index_in_dim(halves, s, 1, keepdims=False).reshape(rows, LANES) for s in (side, 1 - side)
         )
-        states_own = chip_states(False, gated, gate_grad, par_own)
+        states_own = chip_states(gated, gate_grad, par_own)
     par = jnp.concatenate([par_own, par_far])
 
-    sk_far, hs_far, ks_far, *weighted_far = chip_states(True, gated, gate_grad, par_far)
     sk_own, hs_own, ks_own, *weighted_own = states_own
 
     def message_shapes(span):
@@ -615,21 +634,22 @@
             return (shape(rows + (6 * modes if tree else 0), LANES, dtype=BF16),) * (WAYS - 1)
         return (shape(rows * 2 + (4 * rows // span if tree else 0), LANES, dtype=BF16),)
 
-    def chip_sums(flip, outs, weighted, hs, ks, sk, *par):
-        return call(
-            functools.partial(sums_kernel, part=min(2, modes), unroll=16, flip=flip, tree=tree, **sizes),
-            (() if flip and tree else (shape(4, rows // 2, LANES),)) + outs,
-            [SMEM] + [VMEM] * (6 + len(par)),
-            work * 3,
-            scratch=(pltpu.VMEM((4, 2, rows // 2, LANES), F32),),
-        )(me, *weighted, lags, hs, ks, sk, *par)
-
-    *sums_far, tot, message = chip_sums(
-        True, (pair, *message_shapes(SETS)), weighted_far, hs_far, ks_far, sk_far, par_far, sk_own, par_own
-    )
+    loops = dict(part=min(2, modes), unroll=16, tree=tree, **sizes)
+    half_sums = shape(4, rows // 2, LANES)
+    work_sums = pltpu.VMEM((4, 2, rows // 2, LANES), F32)
+    weighted = pltpu.VMEM(half_series.shape, F32)
+    sk_far, hs_far, ks_far, *sums_far, tot, message = call(
+        functools.partial(far_kernel, **loops),
+        states + (() if tree else (half_sums,)) + (pair, *message_shapes(SETS)),
+        [SMEM] + [VMEM] * 6,
+        work * 5,
+        scratch=(weighted, weighted, work_sums),
+    )(me, gated, gate_grad, lags, par_far, sk_own, par_own)
     messages = [message]
     tot, weighted_own[0] = tie(tot, weighted_own[0])
-    (sums_own,) = chip_sums(False, (), weighted_own, hs_own, ks_own, sk_own, par_own)
+    (sums_own,) = call(
+        functools.partial(sums_kernel, flip=False, **loops), (half_sums,), [SMEM] + [VMEM] * 7, work * 3, scratch=(work_sums,)
+    )(me, *weighted_own, lags, hs_own, ks_own, sk_own, par_own)
 
     enter, span, pair_tot, kept = tot, SETS, tot, [sums_own] if tree else []
     while span < top:
@@ -666,15 +686,15 @@
         me, gated, gate_grad, par
     )
     far[0], y, hs = tie(far[0], y, hs)
-    (states_in,) = call(
-        functools.partial(enter_kernel, span=top, **sizes), (shape(2, 2, rows, LANES),), [SMEM] + [VMEM] * 7, rows
-    )(me, enter, *far, par, sk_own, sk_far)
-
     scratch = (pltpu.VMEM((tokens * members, LANES), F32),) * 2
     finish = functools.partial(finish_kernel, tokens=tokens, modes=modes, members=members)
-    (send_conv,) = call(functools.partial(finish, own=False), (half,), [SMEM] + [VMEM] * 6, work * 2, scratch=scratch)(
-        me, y, z, hs, ks, const, states_in
-    )
+    send_conv, states_in = call(
+        functools.partial(first_finish_kernel, span=top, **sizes),
+        (half, shape(2, 2, rows, LANES)),
+        [SMEM] + [VMEM] * 12,
+        work * 2,
+        scratch=scratch,
+    )(me, y, z, hs, ks, const, enter, *far, par, sk_own, sk_far)
     got_conv = exchange(send_conv, 1, count)
     grads = (shape(tokens, channels, dtype=BF16),) * 3
     done = call(functools.partial(finish, own=True), grads, [SMEM] + [VMEM] * 9, work * 2, scratch=scratch)(

time: 38 us -> 38 us (level)
    pallas_call x6 -> x4, Pallas kernels: 7.38 us -> 7.44 us  [the longest x1 2.93 us: local(): call(functools.partial(far_kernel, **loops), states + (() if tree else (h...]
where the time goes in v7:
time: 38 us; the launch traced here: 37.8 us
  Pallas kernels  15.3 us (40%)
  starting transfers between devices  13.7 us (36%)
  waiting for transfers between devices  7.18 us (19%)
  between operations  0.81 us (2%)
  other arithmetic  0.75 us (2%)
    ppermute x9, starting transfers between devices, exchange(): return lax.ppermute(value, 'ctx', [(i, i ^ distance) for i in range(count)])  13.7 us
    ppermute x9, waiting for transfers between devices, exchange(): return lax.ppermute(value, 'ctx', [(i, i ^ distance) for i in range(count)])  7.18 us
    pallas_call x1, Pallas kernels, local(): call(functools.partial(far_kernel, **loops), states + (() if tree else (h...  2.93 us
    pallas_call x1, Pallas kernels, local(): call(functools.partial(gate_kernel, members=members, pieces=pieces), (hal...  1.87 us
    pallas_call x1, Pallas kernels, local(): call(functools.partial(finish, own=True), grads, [SMEM] + [VMEM] * 9, wor...  1.76 us
    pallas_call x1, Pallas kernels, local(): call(functools.partial(sums_kernel, flip=False, **loops), (half_sums,), [...  1.62 us
    pallas_call x1, Pallas kernels, local(): call(functools.partial(first_finish_kernel, span=top, **sizes), (half, sh...  1.61 us
    pallas_call x1, Pallas kernels, local(): call(functools.partial(last_kernel, tokens=tokens, modes=modes, members=m...  1.42 us
  transfers between devices with their start and end apart: 9, of which 8 were waited for; matrix products, arithmetic and copies ran while one was open for 0% of the time, Pallas kernels for 24%

profile of v7, /device:TPU:0, one launch (start us, length us, event | category | flops | bytes accessed | tf_op | source)
XLA Modules:
  0.0 37.8 jit_solution(942541061637768400)
XLA Ops:
  0.6 0.7 %pad_maximum_fusion.3.refs_4_ = f32[2,16,128]{2,1,0:T(8,128)S(1)} fusion(f32[1,16,128]{2,1,0:T(8,128)} %bitcast.25, f32[1,16,128]{2,1,0:T(8,128)} %bitcast.26), kind=kLoop, calls=%fused_computation.5 | loop fusion | flops 4096 | bytes 32768 | tf_op jit(solution)/shard_map/stack | solution.py:595
  1.3 4.0 %collective-permute-start = (f32[2,16,128]{2,1,0:T(8,128)S(1)}, f32[2,16,128]{2,1,0:T(8,128)S(1)}, u32[]{:S(2)}, u32[]{:S(2)}) collective-permute-start(f32[2,16,128]{2,1,0:T(8,128)S(1)} %pad_maximum_fusion.3.refs_4_), channel_id=1, source_target_pairs={{0,16},{2,18},{4,20},{6,22},{8,24},{10,26},{12,28},{14,30},{16,0},... | collective-permute-start | bytes 49160 | tf_op jit(solution)/shard_map/ppermute | solution.py:545
  5.4 1.9 %shard_map.101 = (bf16[2,8,128,128]{3,2,1,0:T(8,128)(2,1)S(1)}, bf16[2,8,128,128]{3,2,1,0:T(8,128)(2,1)S(1)}) custom-call(s32[1]{0:T(128)} %bitcast.me_ref, bf16[128,2048]{1,0:T(8,128)(2,1)} %q_hbm.1, bf16[128,2048]{1,0:T(8,128)(2,1)} %k_ref.1, bf16[128,2048]{1,0:T(8,128)(2,1)} %v_ref.1, bf16[128,2048]{1,0:T(8,128)(2,1)} %u_ref.1), custom_call_target="tpu_custom_call" | custom-call | flops 4194304 | bytes 1048576 | tf_op jit(solution)/shard_map/pallas_call | solution.py:587
  7.3 0.0 collective-permute-done
  7.3 0.1 collective-permute-start.2
  7.4 1.7 %collective-permute-start.1 = (f32[2,2,16,128]{3,2,1,0:T(8,128)S(1)}, f32[2,2,16,128]{3,2,1,0:T(8,128)S(1)}, u32[]{:S(2)}, u32[]{:S(2)}) collective-permute-start(f32[2,2,16,128]{3,2,1,0:T(8,128)S(1)} %pad_maximum_fusion.2), channel_id=1, source_target_pairs={{0,8},{2,10},{4,12},{6,14},{8,0},{10,2},{12,4},{14,6},{16,24},{18,... | collective-permute-start | bytes 98312 | tf_op jit(solution)/shard_map/ppermute | solution.py:545
  9.1 0.2 collective-permute-done.2.got_ref
  9.3 1.0 %shard_map.102 = (f32[2,1024,128]{2,1,0:T(8,128)S(1)}, f32[2,1024,128]{2,1,0:T(8,128)S(1)}, f32[2,8,8,128]{3,2,1,0:T(8,128)S(1)}) custom-call(s32[1]{0:T(128)} %bitcast.me_ref, bf16[2,8,128,128]{3,2,1,0:T(8,128)(2,1)S(1)} %get-tuple-element.61.own_ref, bf16[2,8,128,128]{3,2,1,0:T(8,128)(2,1)S(1)} %collective-permute-done.2.got_ref), custom_call_target="tpu_custom_call" | custom-call | flops 4194304 | bytes 1048576 | tf_op jit(solution)/shard_map/pallas_call | solution.py:603
  10.2 1.2 %collective-permute-done.1 = f32[2,2,16,128]{3,2,1,0:T(8,128)S(1)} collective-permute-done((f32[2,2,16,128]{3,2,1,0:T(8,128)S(1)}, f32[2,2,16,128]{3,2,1,0:T(8,128)S(1)}, u32[]{:S(2)}, u32[]{:S(2)}) %collective-permute-start.1) | collective-permute-done | bytes 32800 | tf_op jit(solution)/shard_map/ppermute | solution.py:545
  11.4 1.7 %collective-permute-start.3 = (f32[2,2,2,16,128]{4,3,2,0,1:T(8,128)S(1)}, f32[2,2,2,16,128]{4,3,2,0,1:T(8,128)S(1)}, u32[]{:S(2)}, u32[]{:S(2)}) collective-permute-start(f32[2,2,2,16,128]{4,3,2,0,1:T(8,128)S(1)} %pad_maximum_fusion.1), channel_id=1, source_target_pairs={{0,4},{2,6},{4,0},{6,2},{8,12},{10,14},{12,8},{14,10},{16,20},{18,... | collective-permute-start | bytes 196616 | tf_op jit(solution)/shard_map/ppermute | solution.py:545
  13.1 1.3 %shard_map.103 = (f32[2,2,64,128]{3,2,1,0:T(8,128)S(1)}, f32[16,16,8,128]{3,2,1,0:T(8,128)S(1)}, f32[17,16,8,128]{3,2,1,0:T(8,128)S(1)}, f32[1024,128]{1,0:T(8,128)S(1)}, f32[1024,128]{1,0:T(8,128)S(1)}) custom-call(s32[1]{0:T(128)} %bitcast.me_ref, f32[2,1024,128]{2,1,0:T(8,128)S(1)} %get-tuple-element.83.x_ref, ...), custom_call_target="tpu_custom_call" | custom-call | flops 8388608 | bytes 1048576 | tf_op jit(solution)/shard_map/pallas_call | solution.py:582
  14.4 1.4 %collective-permute-done.3 = f32[2,2,2,16,128]{4,3,2,0,1:T(8,128)S(1)} collective-permute-done((f32[2,2,2,16,128]{4,3,2,0,1:T(8,128)S(1)}, f32[2,2,2,16,128]{4,3,2,0,1:T(8,128)S(1)}, u32[]{:S(2)}, u32[]{:S(2)}) %collective-permute-start.3) | collective-permute-done | bytes 65568 | tf_op jit(solution)/shard_map/ppermute | solution.py:545
  15.8 2.9 %shard_map.104 = (f32[2,2,64,128]{3,2,1,0:T(8,128)S(1)}, f32[16,16,8,128]{3,2,1,0:T(8,128)S(1)}, f32[17,16,8,128]{3,2,1,0:T(8,128)S(1)}, f32[2,128,128]{2,1,0:T(8,128)S(1)}, bf16[512,128]{1,0:T(8,128)(2,1)S(1)}) custom-call(s32[1]{0:T(128)} %bitcast.me_ref, f32[2,1024,128]{2,1,0:T(8,128)S(1)} %get-tuple-element.83.x_ref, ...), custom_call_target="tpu_custom_call" | custom-call | flops 20971520 | bytes 1048576 | tf_op jit(solution)/shard_map/pallas_call | solution.py:641
  18.7 1.7 %collective-permute-start.4 = (bf16[512,128]{1,0:T(8,128)(2,1)S(1)}, bf16[512,128]{1,0:T(8,128)(2,1)S(1)}, u32[]{:S(2)}, u32[]{:S(2)}) collective-permute-start(bf16[512,128]{1,0:T(8,128)(2,1)S(1)} %get-tuple-element.76), channel_id=1, source_target_pairs={{0,4},{2,6},{4,0},{6,2},{8,12},{10,14},{12,8},{14,10},{16,20},{18,... | collective-permute-start | bytes 393224 | tf_op jit(solution)/shard_map/ppermute | solution.py:545
  20.4 1.6 %shard_map.105.refs_0_ = f32[4,64,128]{2,1,0:T(8,128)S(1)} custom-call(s32[1]{0:T(128)} %bitcast.me_ref, f32[1024,128]{1,0:T(8,128)S(1)} %get-tuple-element.77.x_ref, f32[1024,128]{1,0:T(8,128)S(1)} %get-tuple-element.78.g_ref, f32[2,8,8,128]{3,2,1,0:T(8,128)S(1)} %get-tuple-element.68.lag_ref, f32[16,16,8,128]{3,2,1,0:T(8,128)S(1)} %get-tuple-element.86.hs_ref.hs_own, ...), custom_call_target="tpu_custom_call" | custom-call | flops 12582912 | bytes 1048576 | tf_op jit(solution)/shard_map/pallas_call | solution.py:650
  22.0 1.7 %collective-permute-done.4.got_ref = bf16[512,128]{1,0:T(8,128)(2,1)S(1)} collective-permute-done((bf16[512,128]{1,0:T(8,128)(2,1)S(1)}, bf16[512,128]{1,0:T(8,128)(2,1)S(1)}, u32[]{:S(2)}, u32[]{:S(2)}) %collective-permute-start.4) | collective-permute-done | bytes 131104 | tf_op jit(solution)/shard_map/ppermute | solution.py:545
  23.7 0.2 shard_map.106
  23.9 3.8 %collective-permute-start.5 = (bf16[224,128]{1,0:T(8,128)(2,1)S(1)}, bf16[224,128]{1,0:T(8,128)(2,1)S(1)}, u32[]{:S(2)}, u32[]{:S(2)}) collective-permute-start(bf16[224,128]{1,0:T(8,128)(2,1)S(1)} %get-tuple-element.81), channel_id=1, source_target_pairs={{0,24},{2,26},{4,28},{6,30},{8,16},{10,18},{12,20},{14,22},{16,8},... | collective-permute-start | bytes 172040 | tf_op jit(solution)/shard_map/ppermute | solution.py:545
  27.7 0.0 collective-permute-start.6
  27.7 0.7 %collective-permute-start.7 = (bf16[224,128]{1,0:T(8,128)(2,1)S(1)}, bf16[224,128]{1,0:T(8,128)(2,1)S(1)}, u32[]{:S(2)}, u32[]{:S(2)}) collective-permute-start(bf16[224,128]{1,0:T(8,128)(2,1)S(1)} %get-tuple-element.98), channel_id=1, source_target_pairs={{0,16},{2,18},{4,20},{6,22},{8,24},{10,26},{12,28},{14,30},{16,0},... | collective-permute-start | bytes 172040 | tf_op jit(solution)/shard_map/ppermute | solution.py:545
  28.3 0.8 %shard_map.107 = (f32[2048,128]{1,0:T(8,128)S(1)}, f32[2048,128]{1,0:T(8,128)S(1)}) custom-call(s32[1]{0:T(128)} %bitcast.me_ref, f32[2,1024,128]{2,1,0:T(8,128)S(1)} %get-tuple-element.83.x_ref, f32[2,1024,128]{2,1,0:T(8,128)S(1)} %get-tuple-element.84.g_ref, f32[256,128]{1,0:T(8,128)S(1)} %pad_maximum_fusion.par_ref), custom_call_target="tpu_custom_call" | custom-call | flops 4194304 | bytes 1048576 | tf_op jit(solution)/shard_map/pallas_call | solution.py:685
  29.2 0.9 %shard_map.108 = (f32[2,16,128,128]{3,2,1,0:T(8,128)S(1)}, f32[2,17,128,128]{3,2,1,0:T(8,128)S(1)}, f32[3,16,8,128]{3,2,1,0:T(8,128)S(1)}) custom-call(f32[16,16,8,128]{3,2,1,0:T(8,128)S(1)} %get-tuple-element.86.hs_ref.hs_own, f32[17,16,8,128]{3,2,1,0:T(8,128)S(1)} %get-tuple-element.80.ks_ref.ks_own, f32[16,16,8,128]{3,2,1,0:T(8,128)S(1)} %get-tuple-element.87.hs_far, ...), custom_call_target="tpu_custom_call" | custom-call | flops 4194304 | bytes 1048576 | tf_op jit(solution)/shard_map/pallas_call | solution.py:675
  30.1 0.3 collective-permute-done.5.a_ref.refs_1_
  30.4 1.4 %collective-permute-done.6.b_ref.refs_2_ = bf16[224,128]{1,0:T(8,128)(2,1)S(1)} collective-permute-done((bf16[224,128]{1,0:T(8,128)(2,1)S(1)}, bf16[224,128]{1,0:T(8,128)(2,1)S(1)}, u32[]{:S(2)}, u32[]{:S(2)}) %collective-permute-start.6) | collective-permute-done | bytes 57376 | tf_op jit(solution)/shard_map/ppermute | solution.py:545
  31.8 0.9 %collective-permute-done.7.c_ref.refs_3_ = bf16[224,128]{1,0:T(8,128)(2,1)S(1)} collective-permute-done((bf16[224,128]{1,0:T(8,128)(2,1)S(1)}, bf16[224,128]{1,0:T(8,128)(2,1)S(1)}, u32[]{:S(2)}, u32[]{:S(2)}) %collective-permute-start.7) | collective-permute-done | bytes 57376 | tf_op jit(solution)/shard_map/ppermute | solution.py:545
  32.7 0.0 copy-start
  32.7 0.0 copy-start.1
  32.7 0.0 copy-start.2
  32.8 1.6 %shard_map.109 = (bf16[2,8,128,128]{3,2,1,0:T(8,128)(2,1)S(1)}, f32[2,2,128,128]{3,2,1,0:T(8,128)S(1)}) custom-call(s32[1]{0:T(128)} %bitcast.me_ref, f32[2048,128]{1,0:T(8,128)S(1)} %get-tuple-element.90.y_ref, f32[2048,128]{1,0:T(8,128)S(1)} %get-tuple-element.91.z_ref, f32[2,16,128,128]{3,2,1,0:T(8,128)S(1)} %get-tuple-element.92.hs_ref, ...), custom_call_target="tpu_custom_call" | custom-call | flops 8388608 | bytes 1048576 | tf_op jit(solution)/shard_map/pallas_call | solution.py:691
  34.4 0.1 collective-permute-start.8
  34.4 0.0 copy-done
  34.5 0.0 copy-done.1
  34.5 0.0 copy-done.2
  34.5 1.8 %shard_map.110 = (bf16[128,2048]{1,0:T(8,128)(2,1)S(1)}, bf16[128,2048]{1,0:T(8,128)(2,1)S(1)}, bf16[128,2048]{1,0:T(8,128)(2,1)S(1)}) custom-call(s32[1]{0:T(128)} %bitcast.me_ref, f32[2048,128]{1,0:T(8,128)S(1)} %get-tuple-element.90.y_ref, f32[2048,128]{1,0:T(8,128)S(1)} %get-tuple-element.91.z_ref, f32[2,16,128,128]{3,2,1,0:T(8,128)S(1)} %get-tuple-element.92.hs_ref, ...), custom_call_target="tpu_custom_call" | custom-call | flops 8388608 | bytes 1048576 | tf_op jit(solution)/shard_map/pallas_call | solution.py:700
  36.2 0.1 collective-permute-done.8.got_ref
  36.3 1.4 %shard_map.111 = (bf16[128,2048]{1,0:T(8,128)(2,1)S(1)}, bf16[128,2048]{1,0:T(8,128)(2,1)S(1)}, bf16[128,2048]{1,0:T(8,128)(2,1)S(1)}, bf16[128,2048]{1,0:T(8,12...) custom-call(s32[1]{0:T(128)} %bitcast.me_ref, ...), custom_call_target="tpu_custom_call", output_to_operand_aliasing={{0}: (10, {}), {1}: (11, {}), {2}: (12, {})} | custom-call | flops 4194304 | bytes 1048576 | tf_op jit(solution)/shard_map/pallas_call | solution.py:706
  (7 shorter events, 0.0 us)
Async XLA Ops:
  1.3 5.9 %collective-permute-start = (f32[2,16,128]{2,1,0:T(8,128)S(1)}, f32[2,16,128]{2,1,0:T(8,128)S(1)}, u32[]{:S(2)}, u32[]{:S(2)}) collective-permute-start(f32[2,16,128]{2,1,0:T(8,128)S(1)} %pad_maximum_fusion.3.refs_4_), channel_id=1, source_target_pairs={{0,16},{2,18},{4,20},{6,22},{8,24},{10,26},{12,28},{14,30},{16,0},... | collective-permute-start | bytes 49160 | tf_op jit(solution)/shard_map/ppermute | solution.py:545
  7.3 2.0 %collective-permute-start.2 = (bf16[2,8,128,128]{3,2,1,0:T(8,128)(2,1)S(1)}, bf16[2,8,128,128]{3,2,1,0:T(8,128)(2,1)S(1)}, u32[]{:S(2)}, u32[]{:S(2)}) collective-permute-start(bf16[2,8,128,128]{3,2,1,0:T(8,128)(2,1)S(1)} %get-tuple-element.62), channel_id=1, source_target_pairs={{0,2},{2,0},{4,6},{6,4},{8,10},{10,8},{12,14},{14,12},{16,18},{18,... | collective-permute-start | bytes 1572872 | tf_op jit(solution)/shard_map/ppermute | solution.py:545
  7.4 4.0 %collective-permute-start.1 = (f32[2,2,16,128]{3,2,1,0:T(8,128)S(1)}, f32[2,2,16,128]{3,2,1,0:T(8,128)S(1)}, u32[]{:S(2)}, u32[]{:S(2)}) collective-permute-start(f32[2,2,16,128]{3,2,1,0:T(8,128)S(1)} %pad_maximum_fusion.2), channel_id=1, source_target_pairs={{0,8},{2,10},{4,12},{6,14},{8,0},{10,2},{12,4},{14,6},{16,24},{18,... | collective-permute-start | bytes 98312 | tf_op jit(solution)/shard_map/ppermute | solution.py:545
  11.4 4.3 %collective-permute-start.3 = (f32[2,2,2,16,128]{4,3,2,0,1:T(8,128)S(1)}, f32[2,2,2,16,128]{4,3,2,0,1:T(8,128)S(1)}, u32[]{:S(2)}, u32[]{:S(2)}) collective-permute-start(f32[2,2,2,16,128]{4,3,2,0,1:T(8,128)S(1)} %pad_maximum_fusion.1), channel_id=1, source_target_pairs={{0,4},{2,6},{4,0},{6,2},{8,12},{10,14},{12,8},{14,10},{16,20},{18,... | collective-permute-start | bytes 196616 | tf_op jit(solution)/shard_map/ppermute | solution.py:545
  18.7 5.0 %collective-permute-start.4 = (bf16[512,128]{1,0:T(8,128)(2,1)S(1)}, bf16[512,128]{1,0:T(8,128)(2,1)S(1)}, u32[]{:S(2)}, u32[]{:S(2)}) collective-permute-start(bf16[512,128]{1,0:T(8,128)(2,1)S(1)} %get-tuple-element.76), channel_id=1, source_target_pairs={{0,4},{2,6},{4,0},{6,2},{8,12},{10,14},{12,8},{14,10},{16,20},{18,... | collective-permute-start | bytes 393224 | tf_op jit(solution)/shard_map/ppermute | solution.py:545
  23.9 6.5 %collective-permute-start.5 = (bf16[224,128]{1,0:T(8,128)(2,1)S(1)}, bf16[224,128]{1,0:T(8,128)(2,1)S(1)}, u32[]{:S(2)}, u32[]{:S(2)}) collective-permute-start(bf16[224,128]{1,0:T(8,128)(2,1)S(1)} %get-tuple-element.81), channel_id=1, source_target_pairs={{0,24},{2,26},{4,28},{6,30},{8,16},{10,18},{12,20},{14,22},{16,8},... | collective-permute-start | bytes 172040 | tf_op jit(solution)/shard_map/ppermute | solution.py:545
  27.7 4.2 %collective-permute-start.6 = (bf16[224,128]{1,0:T(8,128)(2,1)S(1)}, bf16[224,128]{1,0:T(8,128)(2,1)S(1)}, u32[]{:S(2)}, u32[]{:S(2)}) collective-permute-start(bf16[224,128]{1,0:T(8,128)(2,1)S(1)} %get-tuple-element.97), channel_id=1, source_target_pairs={{0,8},{2,10},{4,12},{6,14},{8,0},{10,2},{12,4},{14,6},{16,24},{18,... | collective-permute-start | bytes 172040 | tf_op jit(solution)/shard_map/ppermute | solution.py:545
  27.7 5.1 %collective-permute-start.7 = (bf16[224,128]{1,0:T(8,128)(2,1)S(1)}, bf16[224,128]{1,0:T(8,128)(2,1)S(1)}, u32[]{:S(2)}, u32[]{:S(2)}) collective-permute-start(bf16[224,128]{1,0:T(8,128)(2,1)S(1)} %get-tuple-element.98), channel_id=1, source_target_pairs={{0,16},{2,18},{4,20},{6,22},{8,24},{10,26},{12,28},{14,30},{16,0},... | collective-permute-start | bytes 172040 | tf_op jit(solution)/shard_map/ppermute | solution.py:545
  32.7 1.7 %copy-start = (bf16[128,2048]{1,0:T(8,128)(2,1)S(1)}, bf16[128,2048]{1,0:T(8,128)(2,1)}, u32[]{:S(2)}) copy-start(bf16[128,2048]{1,0:T(8,128)(2,1)} %k_ref.1) | copy-start | bytes 1572868
  32.7 1.7 %copy-start.1 = (bf16[128,2048]{1,0:T(8,128)(2,1)S(1)}, bf16[128,2048]{1,0:T(8,128)(2,1)}, u32[]{:S(2)}) copy-start(bf16[128,2048]{1,0:T(8,128)(2,1)} %v_ref.1) | copy-start | bytes 1572868
  32.7 1.7 %copy-start.2 = (bf16[128,2048]{1,0:T(8,128)(2,1)S(1)}, bf16[128,2048]{1,0:T(8,128)(2,1)}, u32[]{:S(2)}) copy-start(bf16[128,2048]{1,0:T(8,128)(2,1)} %u_ref.1) | copy-start | bytes 1572868
  34.4 2.0 %collective-permute-start.8 = (bf16[2,8,128,128]{3,2,1,0:T(8,128)(2,1)S(1)}, bf16[2,8,128,128]{3,2,1,0:T(8,128)(2,1)S(1)}, u32[]{:S(2)}, u32[]{:S(2)}) collective-permute-start(bf16[2,8,128,128]{3,2,1,0:T(8,128)(2,1)S(1)} %get-tuple-element.100), channel_id=1, source_target_pairs={{0,2},{2,0},{4,6},{6,4},{8,10},{10,8},{12,14},{14,12},{16,18},{18,... | collective-permute-start | bytes 1572872 | tf_op jit(solution)/shard_map/ppermute | solution.py:545

commit v8 on v7

--- a/solution.py
+++ b/solution.py
@@ -462,9 +462,9 @@
         else:
             send_ref[1, member, rows, :] = value
 
-    lax.fori_loop(0, stretches, forward, h, unroll=4)
+    lax.fori_loop(0, stretches, forward, h, unroll=8)
     put(yo_ref, store_y)
-    lax.fori_loop(0, stretches, backward, k, unroll=4)
+    lax.fori_loop(0, stretches, backward, k, unroll=8)
     put(zo_ref, store_z)
 
 
@@ -521,9 +521,11 @@
             dq_ref[rows, cols] = (u_ref[rows, cols].astype(F32) * y).astype(BF16)
             dk_ref[rows, cols] = (z * v_ref[rows, cols].astype(F32)).astype(BF16)
             dv_ref[rows, cols] = (z * k_ref[rows, cols].astype(F32)).astype(BF16)
-        for i, (ref, out) in enumerate(((dq_ref, dq_hbm), (dk_ref, dk_hbm), (dv_ref, dv_hbm))):
-            copies.append(pltpu.make_async_copy(ref.at[rows], out.at[rows], sems.at[i, tile]))
-            copies[-1].start()
+        if tile % 2:
+            rows = pl.ds(tile * 16 - 16, 32)
+            for i, (ref, out) in enumerate(((dq_ref, dq_hbm), (dk_ref, dk_hbm), (dv_ref, dv_hbm))):
+                copies.append(pltpu.make_async_copy(ref.at[rows], out.at[rows], sems.at[i, tile]))
+                copies[-1].start()
     for copy in copies:
         copy.wait()
 

time: 38 us -> 38 us (level)
  no operation moved by 1% of the time
where the time goes in v8:
time: 38 us; the launch traced here: 37.8 us
  Pallas kernels  15.3 us (40%)
  starting transfers between devices  13.7 us (36%)
  waiting for transfers between devices  7.18 us (19%)
  between operations  0.81 us (2%)
  other arithmetic  0.75 us (2%)
    ppermute x9, starting transfers between devices, exchange(): return lax.ppermute(value, 'ctx', [(i, i ^ distance) for i in range(count)])  13.7 us
    ppermute x9, waiting for transfers between devices, exchange(): return lax.ppermute(value, 'ctx', [(i, i ^ distance) for i in range(count)])  7.18 us
    pallas_call x1, Pallas kernels, local(): call(functools.partial(far_kernel, **loops), states + (() if tree else (h...  2.93 us
    pallas_call x1, Pallas kernels, local(): call(functools.partial(gate_kernel, members=members, pieces=pieces), (hal...  1.87 us
    pallas_call x1, Pallas kernels, local(): call(functools.partial(finish, own=True), grads, [SMEM] + [VMEM] * 9, wor...  1.76 us
    pallas_call x1, Pallas kernels, local(): call(functools.partial(first_finish_kernel, span=top, **sizes), (half, sh...  1.62 us
    pallas_call x1, Pallas kernels, local(): call(functools.partial(sums_kernel, flip=False, **loops), (half_sums,), [...  1.62 us
    pallas_call x1, Pallas kernels, local(): call(functools.partial(last_kernel, tokens=tokens, modes=modes, members=m...  1.41 us
  transfers between devices with their start and end apart: 9, of which 8 were waited for; matrix products, arithmetic and copies ran while one was open for 0% of the time, Pallas kernels for 24%

profile of v8, /device:TPU:0, one launch (start us, length us, event | category | flops | bytes accessed | tf_op | source)
XLA Modules:
  0.0 37.8 jit_solution(1455265939246050214)
XLA Ops:
  0.6 0.7 %pad_maximum_fusion.3.refs_4_ = f32[2,16,128]{2,1,0:T(8,128)S(1)} fusion(f32[1,16,128]{2,1,0:T(8,128)} %bitcast.25, f32[1,16,128]{2,1,0:T(8,128)} %bitcast.26), kind=kLoop, calls=%fused_computation.5 | loop fusion | flops 4096 | bytes 32768 | tf_op jit(solution)/shard_map/stack | solution.py:597
  1.3 4.0 %collective-permute-start = (f32[2,16,128]{2,1,0:T(8,128)S(1)}, f32[2,16,128]{2,1,0:T(8,128)S(1)}, u32[]{:S(2)}, u32[]{:S(2)}) collective-permute-start(f32[2,16,128]{2,1,0:T(8,128)S(1)} %pad_maximum_fusion.3.refs_4_), channel_id=1, source_target_pairs={{0,16},{2,18},{4,20},{6,22},{8,24},{10,26},{12,28},{14,30},{16,0},... | collective-permute-start | bytes 49160 | tf_op jit(solution)/shard_map/ppermute | solution.py:547
  5.4 1.9 %shard_map.101 = (bf16[2,8,128,128]{3,2,1,0:T(8,128)(2,1)S(1)}, bf16[2,8,128,128]{3,2,1,0:T(8,128)(2,1)S(1)}) custom-call(s32[1]{0:T(128)} %bitcast.me_ref, bf16[128,2048]{1,0:T(8,128)(2,1)} %q_hbm.1, bf16[128,2048]{1,0:T(8,128)(2,1)} %k_ref.1, bf16[128,2048]{1,0:T(8,128)(2,1)} %v_ref.1, bf16[128,2048]{1,0:T(8,128)(2,1)} %u_ref.1), custom_call_target="tpu_custom_call" | custom-call | flops 4194304 | bytes 1048576 | tf_op jit(solution)/shard_map/pallas_call | solution.py:589
  7.3 0.0 collective-permute-done
  7.3 0.1 collective-permute-start.2
  7.4 1.7 %collective-permute-start.1 = (f32[2,2,16,128]{3,2,1,0:T(8,128)S(1)}, f32[2,2,16,128]{3,2,1,0:T(8,128)S(1)}, u32[]{:S(2)}, u32[]{:S(2)}) collective-permute-start(f32[2,2,16,128]{3,2,1,0:T(8,128)S(1)} %pad_maximum_fusion.2), channel_id=1, source_target_pairs={{0,8},{2,10},{4,12},{6,14},{8,0},{10,2},{12,4},{14,6},{16,24},{18,... | collective-permute-start | bytes 98312 | tf_op jit(solution)/shard_map/ppermute | solution.py:547
  9.1 0.2 collective-permute-done.2.got_ref
  9.3 1.0 %shard_map.102 = (f32[2,1024,128]{2,1,0:T(8,128)S(1)}, f32[2,1024,128]{2,1,0:T(8,128)S(1)}, f32[2,8,8,128]{3,2,1,0:T(8,128)S(1)}) custom-call(s32[1]{0:T(128)} %bitcast.me_ref, bf16[2,8,128,128]{3,2,1,0:T(8,128)(2,1)S(1)} %get-tuple-element.61.own_ref, bf16[2,8,128,128]{3,2,1,0:T(8,128)(2,1)S(1)} %collective-permute-done.2.got_ref), custom_call_target="tpu_custom_call" | custom-call | flops 4194304 | bytes 1048576 | tf_op jit(solution)/shard_map/pallas_call | solution.py:605
  10.2 1.2 %collective-permute-done.1 = f32[2,2,16,128]{3,2,1,0:T(8,128)S(1)} collective-permute-done((f32[2,2,16,128]{3,2,1,0:T(8,128)S(1)}, f32[2,2,16,128]{3,2,1,0:T(8,128)S(1)}, u32[]{:S(2)}, u32[]{:S(2)}) %collective-permute-start.1) | collective-permute-done | bytes 32800 | tf_op jit(solution)/shard_map/ppermute | solution.py:547
  11.4 1.7 %collective-permute-start.3 = (f32[2,2,2,16,128]{4,3,2,0,1:T(8,128)S(1)}, f32[2,2,2,16,128]{4,3,2,0,1:T(8,128)S(1)}, u32[]{:S(2)}, u32[]{:S(2)}) collective-permute-start(f32[2,2,2,16,128]{4,3,2,0,1:T(8,128)S(1)} %pad_maximum_fusion.1), channel_id=1, source_target_pairs={{0,4},{2,6},{4,0},{6,2},{8,12},{10,14},{12,8},{14,10},{16,20},{18,... | collective-permute-start | bytes 196616 | tf_op jit(solution)/shard_map/ppermute | solution.py:547
  13.1 1.3 %shard_map.103 = (f32[2,2,64,128]{3,2,1,0:T(8,128)S(1)}, f32[16,16,8,128]{3,2,1,0:T(8,128)S(1)}, f32[17,16,8,128]{3,2,1,0:T(8,128)S(1)}, f32[1024,128]{1,0:T(8,128)S(1)}, f32[1024,128]{1,0:T(8,128)S(1)}) custom-call(s32[1]{0:T(128)} %bitcast.me_ref, f32[2,1024,128]{2,1,0:T(8,128)S(1)} %get-tuple-element.83.x_ref, ...), custom_call_target="tpu_custom_call" | custom-call | flops 8388608 | bytes 1048576 | tf_op jit(solution)/shard_map/pallas_call | solution.py:584
  14.4 1.4 %collective-permute-done.3 = f32[2,2,2,16,128]{4,3,2,0,1:T(8,128)S(1)} collective-permute-done((f32[2,2,2,16,128]{4,3,2,0,1:T(8,128)S(1)}, f32[2,2,2,16,128]{4,3,2,0,1:T(8,128)S(1)}, u32[]{:S(2)}, u32[]{:S(2)}) %collective-permute-start.3) | collective-permute-done | bytes 65568 | tf_op jit(solution)/shard_map/ppermute | solution.py:547
  15.8 2.9 %shard_map.104 = (f32[2,2,64,128]{3,2,1,0:T(8,128)S(1)}, f32[16,16,8,128]{3,2,1,0:T(8,128)S(1)}, f32[17,16,8,128]{3,2,1,0:T(8,128)S(1)}, f32[2,128,128]{2,1,0:T(8,128)S(1)}, bf16[512,128]{1,0:T(8,128)(2,1)S(1)}) custom-call(s32[1]{0:T(128)} %bitcast.me_ref, f32[2,1024,128]{2,1,0:T(8,128)S(1)} %get-tuple-element.83.x_ref, ...), custom_call_target="tpu_custom_call" | custom-call | flops 20971520 | bytes 1048576 | tf_op jit(solution)/shard_map/pallas_call | solution.py:643
  18.7 1.7 %collective-permute-start.4 = (bf16[512,128]{1,0:T(8,128)(2,1)S(1)}, bf16[512,128]{1,0:T(8,128)(2,1)S(1)}, u32[]{:S(2)}, u32[]{:S(2)}) collective-permute-start(bf16[512,128]{1,0:T(8,128)(2,1)S(1)} %get-tuple-element.76), channel_id=1, source_target_pairs={{0,4},{2,6},{4,0},{6,2},{8,12},{10,14},{12,8},{14,10},{16,20},{18,... | collective-permute-start | bytes 393224 | tf_op jit(solution)/shard_map/ppermute | solution.py:547
  20.4 1.6 %shard_map.105.refs_0_ = f32[4,64,128]{2,1,0:T(8,128)S(1)} custom-call(s32[1]{0:T(128)} %bitcast.me_ref, f32[1024,128]{1,0:T(8,128)S(1)} %get-tuple-element.77.x_ref, f32[1024,128]{1,0:T(8,128)S(1)} %get-tuple-element.78.g_ref, f32[2,8,8,128]{3,2,1,0:T(8,128)S(1)} %get-tuple-element.68.lag_ref, f32[16,16,8,128]{3,2,1,0:T(8,128)S(1)} %get-tuple-element.86.hs_ref.hs_own, ...), custom_call_target="tpu_custom_call" | custom-call | flops 12582912 | bytes 1048576 | tf_op jit(solution)/shard_map/pallas_call | solution.py:652
  22.0 1.7 %collective-permute-done.4.got_ref = bf16[512,128]{1,0:T(8,128)(2,1)S(1)} collective-permute-done((bf16[512,128]{1,0:T(8,128)(2,1)S(1)}, bf16[512,128]{1,0:T(8,128)(2,1)S(1)}, u32[]{:S(2)}, u32[]{:S(2)}) %collective-permute-start.4) | collective-permute-done | bytes 131104 | tf_op jit(solution)/shard_map/ppermute | solution.py:547
  23.7 0.2 shard_map.106
  23.9 3.8 %collective-permute-start.5 = (bf16[224,128]{1,0:T(8,128)(2,1)S(1)}, bf16[224,128]{1,0:T(8,128)(2,1)S(1)}, u32[]{:S(2)}, u32[]{:S(2)}) collective-permute-start(bf16[224,128]{1,0:T(8,128)(2,1)S(1)} %get-tuple-element.81), channel_id=1, source_target_pairs={{0,24},{2,26},{4,28},{6,30},{8,16},{10,18},{12,20},{14,22},{16,8},... | collective-permute-start | bytes 172040 | tf_op jit(solution)/shard_map/ppermute | solution.py:547
  27.7 0.0 collective-permute-start.6
  27.7 0.7 %collective-permute-start.7 = (bf16[224,128]{1,0:T(8,128)(2,1)S(1)}, bf16[224,128]{1,0:T(8,128)(2,1)S(1)}, u32[]{:S(2)}, u32[]{:S(2)}) collective-permute-start(bf16[224,128]{1,0:T(8,128)(2,1)S(1)} %get-tuple-element.98), channel_id=1, source_target_pairs={{0,16},{2,18},{4,20},{6,22},{8,24},{10,26},{12,28},{14,30},{16,0},... | collective-permute-start | bytes 172040 | tf_op jit(solution)/shard_map/ppermute | solution.py:547
  28.3 0.8 %shard_map.107 = (f32[2048,128]{1,0:T(8,128)S(1)}, f32[2048,128]{1,0:T(8,128)S(1)}) custom-call(s32[1]{0:T(128)} %bitcast.me_ref, f32[2,1024,128]{2,1,0:T(8,128)S(1)} %get-tuple-element.83.x_ref, f32[2,1024,128]{2,1,0:T(8,128)S(1)} %get-tuple-element.84.g_ref, f32[256,128]{1,0:T(8,128)S(1)} %pad_maximum_fusion.par_ref), custom_call_target="tpu_custom_call" | custom-call | flops 4194304 | bytes 1048576 | tf_op jit(solution)/shard_map/pallas_call | solution.py:687
  29.2 0.9 %shard_map.108 = (f32[2,16,128,128]{3,2,1,0:T(8,128)S(1)}, f32[2,17,128,128]{3,2,1,0:T(8,128)S(1)}, f32[3,16,8,128]{3,2,1,0:T(8,128)S(1)}) custom-call(f32[16,16,8,128]{3,2,1,0:T(8,128)S(1)} %get-tuple-element.86.hs_ref.hs_own, f32[17,16,8,128]{3,2,1,0:T(8,128)S(1)} %get-tuple-element.80.ks_ref.ks_own, f32[16,16,8,128]{3,2,1,0:T(8,128)S(1)} %get-tuple-element.87.hs_far, ...), custom_call_target="tpu_custom_call" | custom-call | flops 4194304 | bytes 1048576 | tf_op jit(solution)/shard_map/pallas_call | solution.py:677
  30.1 0.3 collective-permute-done.5.a_ref.refs_1_
  30.4 1.4 %collective-permute-done.6.b_ref.refs_2_ = bf16[224,128]{1,0:T(8,128)(2,1)S(1)} collective-permute-done((bf16[224,128]{1,0:T(8,128)(2,1)S(1)}, bf16[224,128]{1,0:T(8,128)(2,1)S(1)}, u32[]{:S(2)}, u32[]{:S(2)}) %collective-permute-start.6) | collective-permute-done | bytes 57376 | tf_op jit(solution)/shard_map/ppermute | solution.py:547
  31.8 0.9 %collective-permute-done.7.c_ref.refs_3_ = bf16[224,128]{1,0:T(8,128)(2,1)S(1)} collective-permute-done((bf16[224,128]{1,0:T(8,128)(2,1)S(1)}, bf16[224,128]{1,0:T(8,128)(2,1)S(1)}, u32[]{:S(2)}, u32[]{:S(2)}) %collective-permute-start.7) | collective-permute-done | bytes 57376 | tf_op jit(solution)/shard_map/ppermute | solution.py:547
  32.7 0.0 copy-start
  32.7 0.0 copy-start.1
  32.7 0.0 copy-start.2
  32.8 1.6 %shard_map.109 = (bf16[2,8,128,128]{3,2,1,0:T(8,128)(2,1)S(1)}, f32[2,2,128,128]{3,2,1,0:T(8,128)S(1)}) custom-call(s32[1]{0:T(128)} %bitcast.me_ref, f32[2048,128]{1,0:T(8,128)S(1)} %get-tuple-element.90.y_ref, f32[2048,128]{1,0:T(8,128)S(1)} %get-tuple-element.91.z_ref, f32[2,16,128,128]{3,2,1,0:T(8,128)S(1)} %get-tuple-element.92.hs_ref, ...), custom_call_target="tpu_custom_call" | custom-call | flops 8388608 | bytes 1048576 | tf_op jit(solution)/shard_map/pallas_call | solution.py:693
  34.4 0.1 collective-permute-start.8
  34.5 0.0 copy-done
  34.5 0.0 copy-done.1
  34.5 0.0 copy-done.2
  34.5 1.8 %shard_map.110 = (bf16[128,2048]{1,0:T(8,128)(2,1)S(1)}, bf16[128,2048]{1,0:T(8,128)(2,1)S(1)}, bf16[128,2048]{1,0:T(8,128)(2,1)S(1)}) custom-call(s32[1]{0:T(128)} %bitcast.me_ref, f32[2048,128]{1,0:T(8,128)S(1)} %get-tuple-element.90.y_ref, f32[2048,128]{1,0:T(8,128)S(1)} %get-tuple-element.91.z_ref, f32[2,16,128,128]{3,2,1,0:T(8,128)S(1)} %get-tuple-element.92.hs_ref, ...), custom_call_target="tpu_custom_call" | custom-call | flops 8388608 | bytes 1048576 | tf_op jit(solution)/shard_map/pallas_call | solution.py:702
  36.2 0.1 collective-permute-done.8.got_ref
  36.3 1.4 %shard_map.111 = (bf16[128,2048]{1,0:T(8,128)(2,1)S(1)}, bf16[128,2048]{1,0:T(8,128)(2,1)S(1)}, bf16[128,2048]{1,0:T(8,128)(2,1)S(1)}, bf16[128,2048]{1,0:T(8,12...) custom-call(s32[1]{0:T(128)} %bitcast.me_ref, ...), custom_call_target="tpu_custom_call", output_to_operand_aliasing={{0}: (10, {}), {1}: (11, {}), {2}: (12, {})} | custom-call | flops 4194304 | bytes 1048576 | tf_op jit(solution)/shard_map/pallas_call | solution.py:708
  (7 shorter events, 0.0 us)
Async XLA Ops:
  1.3 5.9 %collective-permute-start = (f32[2,16,128]{2,1,0:T(8,128)S(1)}, f32[2,16,128]{2,1,0:T(8,128)S(1)}, u32[]{:S(2)}, u32[]{:S(2)}) collective-permute-start(f32[2,16,128]{2,1,0:T(8,128)S(1)} %pad_maximum_fusion.3.refs_4_), channel_id=1, source_target_pairs={{0,16},{2,18},{4,20},{6,22},{8,24},{10,26},{12,28},{14,30},{16,0},... | collective-permute-start | bytes 49160 | tf_op jit(solution)/shard_map/ppermute | solution.py:547
  7.3 2.0 %collective-permute-start.2 = (bf16[2,8,128,128]{3,2,1,0:T(8,128)(2,1)S(1)}, bf16[2,8,128,128]{3,2,1,0:T(8,128)(2,1)S(1)}, u32[]{:S(2)}, u32[]{:S(2)}) collective-permute-start(bf16[2,8,128,128]{3,2,1,0:T(8,128)(2,1)S(1)} %get-tuple-element.62), channel_id=1, source_target_pairs={{0,2},{2,0},{4,6},{6,4},{8,10},{10,8},{12,14},{14,12},{16,18},{18,... | collective-permute-start | bytes 1572872 | tf_op jit(solution)/shard_map/ppermute | solution.py:547
  7.4 4.0 %collective-permute-start.1 = (f32[2,2,16,128]{3,2,1,0:T(8,128)S(1)}, f32[2,2,16,128]{3,2,1,0:T(8,128)S(1)}, u32[]{:S(2)}, u32[]{:S(2)}) collective-permute-start(f32[2,2,16,128]{3,2,1,0:T(8,128)S(1)} %pad_maximum_fusion.2), channel_id=1, source_target_pairs={{0,8},{2,10},{4,12},{6,14},{8,0},{10,2},{12,4},{14,6},{16,24},{18,... | collective-permute-start | bytes 98312 | tf_op jit(solution)/shard_map/ppermute | solution.py:547
  11.4 4.3 %collective-permute-start.3 = (f32[2,2,2,16,128]{4,3,2,0,1:T(8,128)S(1)}, f32[2,2,2,16,128]{4,3,2,0,1:T(8,128)S(1)}, u32[]{:S(2)}, u32[]{:S(2)}) collective-permute-start(f32[2,2,2,16,128]{4,3,2,0,1:T(8,128)S(1)} %pad_maximum_fusion.1), channel_id=1, source_target_pairs={{0,4},{2,6},{4,0},{6,2},{8,12},{10,14},{12,8},{14,10},{16,20},{18,... | collective-permute-start | bytes 196616 | tf_op jit(solution)/shard_map/ppermute | solution.py:547
  18.7 5.0 %collective-permute-start.4 = (bf16[512,128]{1,0:T(8,128)(2,1)S(1)}, bf16[512,128]{1,0:T(8,128)(2,1)S(1)}, u32[]{:S(2)}, u32[]{:S(2)}) collective-permute-start(bf16[512,128]{1,0:T(8,128)(2,1)S(1)} %get-tuple-element.76), channel_id=1, source_target_pairs={{0,4},{2,6},{4,0},{6,2},{8,12},{10,14},{12,8},{14,10},{16,20},{18,... | collective-permute-start | bytes 393224 | tf_op jit(solution)/shard_map/ppermute | solution.py:547
  23.9 6.5 %collective-permute-start.5 = (bf16[224,128]{1,0:T(8,128)(2,1)S(1)}, bf16[224,128]{1,0:T(8,128)(2,1)S(1)}, u32[]{:S(2)}, u32[]{:S(2)}) collective-permute-start(bf16[224,128]{1,0:T(8,128)(2,1)S(1)} %get-tuple-element.81), channel_id=1, source_target_pairs={{0,24},{2,26},{4,28},{6,30},{8,16},{10,18},{12,20},{14,22},{16,8},... | collective-permute-start | bytes 172040 | tf_op jit(solution)/shard_map/ppermute | solution.py:547
  27.7 4.2 %collective-permute-start.6 = (bf16[224,128]{1,0:T(8,128)(2,1)S(1)}, bf16[224,128]{1,0:T(8,128)(2,1)S(1)}, u32[]{:S(2)}, u32[]{:S(2)}) collective-permute-start(bf16[224,128]{1,0:T(8,128)(2,1)S(1)} %get-tuple-element.97), channel_id=1, source_target_pairs={{0,8},{2,10},{4,12},{6,14},{8,0},{10,2},{12,4},{14,6},{16,24},{18,... | collective-permute-start | bytes 172040 | tf_op jit(solution)/shard_map/ppermute | solution.py:547
  27.7 5.1 %collective-permute-start.7 = (bf16[224,128]{1,0:T(8,128)(2,1)S(1)}, bf16[224,128]{1,0:T(8,128)(2,1)S(1)}, u32[]{:S(2)}, u32[]{:S(2)}) collective-permute-start(bf16[224,128]{1,0:T(8,128)(2,1)S(1)} %get-tuple-element.98), channel_id=1, source_target_pairs={{0,16},{2,18},{4,20},{6,22},{8,24},{10,26},{12,28},{14,30},{16,0},... | collective-permute-start | bytes 172040 | tf_op jit(solution)/shard_map/ppermute | solution.py:547
  32.7 1.7 %copy-start = (bf16[128,2048]{1,0:T(8,128)(2,1)S(1)}, bf16[128,2048]{1,0:T(8,128)(2,1)}, u32[]{:S(2)}) copy-start(bf16[128,2048]{1,0:T(8,128)(2,1)} %k_ref.1) | copy-start | bytes 1572868
  32.7 1.7 %copy-start.1 = (bf16[128,2048]{1,0:T(8,128)(2,1)S(1)}, bf16[128,2048]{1,0:T(8,128)(2,1)}, u32[]{:S(2)}) copy-start(bf16[128,2048]{1,0:T(8,128)(2,1)} %v_ref.1) | copy-start | bytes 1572868
  32.7 1.7 %copy-start.2 = (bf16[128,2048]{1,0:T(8,128)(2,1)S(1)}, bf16[128,2048]{1,0:T(8,128)(2,1)}, u32[]{:S(2)}) copy-start(bf16[128,2048]{1,0:T(8,128)(2,1)} %u_ref.1) | copy-start | bytes 1572868
  34.4 2.0 %collective-permute-start.8 = (bf16[2,8,128,128]{3,2,1,0:T(8,128)(2,1)S(1)}, bf16[2,8,128,128]{3,2,1,0:T(8,128)(2,1)S(1)}, u32[]{:S(2)}, u32[]{:S(2)}) collective-permute-start(bf16[2,8,128,128]{3,2,1,0:T(8,128)(2,1)S(1)} %get-tuple-element.100), channel_id=1, source_target_pairs={{0,2},{2,0},{4,6},{6,4},{8,10},{10,8},{12,14},{14,12},{16,18},{18,... | collective-permute-start | bytes 1572872 | tf_op jit(solution)/shard_map/ppermute | solution.py:547
